TPU v7x, 32 devices: a whole 2x2x4 slice. The times are simulated.
32 devices in a mesh: expert: 16 (over z, y, x), half: 2 (over core).
Axes of the slice: x: 2, y: 2, z: 4, core: 2. Of those that a mesh axis runs over, the one named last changes fastest.
Arguments:
- hidden_in: bfloat16 [2048, 2048], P('expert'), may hold values from -6 to 6
- modality: int32 [2048], replicated, may hold values from 0 to 1, as said below
- expert_ids: int32 [2048, 8], P('expert'), may hold values from 0 to 15, all different within a row; in each aligned block of 128 rows (0 to 127, 128 to 255, ...) at most 96 rows name the same one
- route_weights: float32 [2048, 8], P('expert'), may hold values from 0.03 to 0.3
- w_gate_up: bfloat16 [32, 2048, 2, 768], P('expert', None, None, 'half'), may hold values from -0.125 to 0.125
- w_down: bfloat16 [32, 768, 2048], P('expert', 'half'), may hold values from -0.21875 to 0.21875
- norm_gain: float32 [2048], replicated, may hold values from 0.1 to 1.9
- w_query: bfloat16 [2048, 4096], P(None, 'half'), may hold values from -1 to 1
- key_value_weight: bfloat16 [2048, 2, 512], P(None, None, 'half'), may hold values from -1 to 1
- q_gain: float32 [128], replicated, may hold values from 1 to 8
- k_gain: float32 [128], replicated, may hold values from 1 to 8
Outputs:
- hidden_out: float32 [2048, 2048], P('expert')
- attended: bfloat16 [2048, 4096], P('expert', 'half')
Inputs may be any that keep to these rules, and one draw needn't show every extreme that they name: `modality`: constant over each aligned block of 128 tokens; both values occur. `expert_ids`: the 8 ids of a token differ; among the tokens of one aligned block of 128 no id is named more than 96 times, a bound that some block reaches.
All inputs are finite; a program needn't handle non-finite values.
Results may differ from a plain program's by a relative error of at most 0.03.
The roundings to bfloat16 on the way count: a program that leaves them out, or rounds other values in their place, can miss the bound.
Values may be sent and summed in bfloat16 or wider, within the bound.
No kernel may reach another device: no remote copies, remote signals or barrier semaphores. Data moves between devices by JAX's collectives and lax.ppermute only.
A program may use at most 128 MiB of HBM per device.

v0:
```python
import math

import jax
import jax.numpy as jnp
from jax import lax
from jax.sharding import PartitionSpec as P

EPSILON = 1e-06


def rms_scale(values, gain_row):
    mean_sq = jnp.mean(values * values, axis=-1, keepdims=True)
    return values * lax.rsqrt(mean_sq + EPSILON) * gain_row


def expert_pass(received, source_kind, w_gate_up, w_down):
    groups, slots, model_width = received.shape
    ordering = jnp.argsort(source_kind, stable=True)
    restore = jnp.argsort(ordering, stable=True)
    text_count = jnp.sum((source_kind == 0).astype(jnp.int32))
    group_sizes = jnp.stack([text_count * slots, (groups - text_count) * slots])
    rows_sorted = received[ordering].reshape(groups * slots, model_width)
    local_experts = w_gate_up.shape[0]
    half_units = w_gate_up.shape[3]
    gate_up = lax.ragged_dot(
        rows_sorted,
        w_gate_up.reshape(local_experts, model_width, 2 * half_units),
        group_sizes,
        preferred_element_type=jnp.float32,
    )
    activated = (jax.nn.silu(gate_up[:, :half_units]) * gate_up[:, half_units:]).astype(
        jnp.bfloat16
    )
    partial_out = lax.ragged_dot(activated, w_down, group_sizes, preferred_element_type=jnp.float32)
    return partial_out.reshape(groups, slots, model_width)[restore]


def body(
    hidden_in,
    modality,
    expert_ids,
    route_weights,
    w_gate_up,
    w_down,
    norm_gain,
    w_query,
    key_value_weight,
    q_gain,
    k_gain,
):
    tok_rows, model_width = hidden_in.shape
    top_count = expert_ids.shape[1]
    groups = lax.axis_size("expert")
    capacity = max(2, 3 * tok_rows * top_count // (2 * groups))
    source_kind = modality.reshape(groups, tok_rows)[:, 0]
    flat_ids = expert_ids.reshape(-1)
    row_total = tok_rows * top_count
    one_hot = (flat_ids[:, None] == jnp.arange(groups, dtype=jnp.int32)[None, :]).astype(jnp.int32)
    slot_rank = jnp.sum((jnp.cumsum(one_hot, axis=0) - one_hot) * one_hot, axis=1)
    slot_index = flat_ids * capacity + slot_rank
    row_token = jnp.arange(row_total, dtype=jnp.int32) // top_count
    slot_token = jnp.full((groups * capacity,), tok_rows, jnp.int32).at[slot_index].set(row_token)
    padded_in = jnp.concatenate([hidden_in, jnp.zeros((1, model_width), hidden_in.dtype)], axis=0)
    outgoing = padded_in[slot_token].reshape(groups, capacity, model_width)
    half_slots = capacity // lax.axis_size("half")
    my_slots = lax.dynamic_slice_in_dim(
        outgoing, lax.axis_index("half") * half_slots, half_slots, 1
    )
    full_gate_up, full_down = (
        lax.all_gather(w_gate_up, "half", axis=3, tiled=True),
        lax.all_gather(w_down, "half", axis=1, tiled=True),
    )
    whole_out = expert_pass(
        lax.all_to_all(my_slots, "expert", split_axis=0, concat_axis=0, tiled=True),
        source_kind,
        full_gate_up,
        full_down,
    )
    mine_back = lax.all_to_all(
        whole_out.astype(jnp.bfloat16), "expert", split_axis=0, concat_axis=0, tiled=True
    )
    returned = lax.all_gather(mine_back, "half", axis=1, tiled=True)
    part_width = returned.shape[2]
    gathered = (
        returned.reshape(groups * capacity, part_width)[slot_index]
        .astype(jnp.float32)
        .reshape(tok_rows, top_count, part_width)
    )
    mixture = jnp.sum(gathered * route_weights[:, :, None], axis=1)
    hidden_out = hidden_in.astype(jnp.float32) + mixture
    normalized_input = rms_scale(hidden_out, norm_gain).astype(jnp.bfloat16)
    head_dim = q_gain.shape[0]
    queries = jnp.dot(normalized_input, w_query, preferred_element_type=jnp.float32)
    local_heads = queries.shape[1] // head_dim
    queries = rms_scale(queries.reshape(tok_rows, local_heads, head_dim), q_gain).astype(
        jnp.bfloat16
    )
    kv_width = key_value_weight.shape[2]
    kv_heads = kv_width // head_dim
    key_value_rows = jnp.dot(
        normalized_input,
        key_value_weight.reshape(model_width, 2 * kv_width),
        preferred_element_type=jnp.float32,
    ).reshape(tok_rows, 2, kv_heads, head_dim)
    keys_local = rms_scale(key_value_rows[:, 0], k_gain).astype(jnp.bfloat16)
    values_local = key_value_rows[:, 1].astype(jnp.bfloat16)
    stacked = jnp.stack([keys_local, values_local], axis=1).reshape(tok_rows, 2, kv_width)
    queries_per_group = local_heads // kv_heads
    query_rows = queries_per_group * tok_rows
    grouped_queries = (
        queries.reshape(tok_rows, kv_heads, queries_per_group, head_dim)
        .transpose(1, 2, 0, 3)
        .reshape(kv_heads, query_rows, head_dim)
    )
    score_scale = head_dim ** (-0.5)
    initial = (
        jnp.full((kv_heads, query_rows), -1e30, jnp.float32),
        jnp.zeros((kv_heads, query_rows), jnp.float32),
        jnp.zeros((kv_heads, query_rows, head_dim), jnp.float32),
    )
    kv_piece = lax.all_gather(stacked, "expert", axis=0, tiled=True)
    key_rows = kv_piece.shape[0]
    key_block = math.gcd(key_rows, 1024)
    blocks = kv_piece.reshape(key_rows // key_block, key_block, 2, kv_heads, head_dim)

    def step_block(inner_state, kv_block):
        peak_in, totals_in, accum_in = inner_state
        scores = (
            jnp.einsum(
                "hrd,khd->hrk", grouped_queries, kv_block[:, 0], preferred_element_type=jnp.float32
            )
            * score_scale
        )
        new_peak = jnp.maximum(peak_in, jnp.max(scores, axis=-1))
        weights = jnp.exp(scores - new_peak[..., None])
        rescale = jnp.exp(peak_in - new_peak)
        totals_out = totals_in * rescale + jnp.sum(weights, axis=-1)
        accum_out = accum_in * rescale[..., None] + jnp.einsum(
            "hrk,khd->hrd",
            weights.astype(jnp.bfloat16),
            kv_block[:, 1],
            preferred_element_type=jnp.float32,
        )
        return ((new_peak, totals_out, accum_out), None)

    final_state = lax.scan(step_block, initial, blocks)[0]
    accumulated = final_state[2] / final_state[1][..., None]
    attended = (
        accumulated.reshape(kv_heads, queries_per_group, tok_rows, head_dim)
        .transpose(2, 0, 1, 3)
        .reshape(tok_rows, local_heads * head_dim)
        .astype(jnp.bfloat16)
    )
    return (hidden_out, attended)


def solution(mesh):
    in_specs = (
        P("expert", None),
        P(),
        P("expert", None),
        P("expert", None),
        P("expert", None, None, "half"),
        P("expert", "half", None),
        P(),
        P(None, "half"),
        P(None, None, "half"),
        P(),
        P(),
    )
    out_specs = (P("expert", None), P("expert", "half"))
    return jax.shard_map(body, mesh=mesh, in_specs=in_specs, out_specs=out_specs, check_vma=False)
```

profile of v0, /device:TPU:0, one launch (start us, length us, event | category | flops | bytes accessed | tf_op | source)
XLA Modules:
  0.0 385.2 jit_solution(16069365210748990501)
XLA Ops:
  7.2 0.7 all-gather.5.cloned.1.call-update
  7.9 0.1 copy.65
  8.0 0.1 eq.32
  8.1 0.1 eq.28
  8.2 4.5 %reduce-window.6 = s32[16,8,128]{2,1,0:T(8,128)S(1)} reduce-window(s32[16,8,128]{2,1,0:T(8,128)S(1)} %fusion.22, s32[]{:T(128)} %constant.34.clone.1), window={size=1x1x128 pad=0_0x0_0x127_0}, to_apply=%region_0.0 | reduce-window | flops 2080768 | bytes 131076 | tf_op jit(solution)/shard_map/reduce-window
  12.8 0.1 copy.67
  13.1 0.1 copy.64
  13.2 0.1 mul.127
  13.5 4.3 %scatter_custom_fusion = s32[1536]{0:T(1024)S(1)} fusion(s32[1024]{0:T(1024)S(1)} %bitcast.123, s32[1024]{0:T(1024)S(1)} %add_select_fusion, s32[]{:T(128)} %constant.32.clone.1), kind=kCustom, calls=%fused_computation.65 | custom fusion | bytes 6148 | tf_op jit(solution)/shard_map/scatter | solution.py:62
  17.9 7.1 %gather_fusion = bf16[1536,2048]{1,0:T(8,128)(2,1)} fusion(bf16[129,2048]{1,0:T(8,128)(2,1)S(1)} %concatenate.4, s32[2048]{0:T(1024)S(1)} %pad_clamp_fusion), kind=kCustom, calls=%fused_computation | custom fusion | bytes 12589056 | tf_op jit(solution)/shard_map/gather | solution.py:64
  25.0 4.4 %constant_dynamic-slice_fusion.1 = bf16[16,48,2048]{2,1,0:T(8,128)(2,1)} fusion(bf16[16,96,2048]{2,1,0:T(8,128)(2,1)} %bitcast.107, s32[]{:T(128)S(6)} %select_n.31), kind=kLoop, calls=%fused_computation.77 | loop fusion | bytes 6291460 | tf_op jit(solution)/shard_map/dynamic_slice | solution.py:66
  29.4 8.6 %all-to-all-start = ((bf16[16,48,2048]{2,1,0:T(8,128)(2,1)}), bf16[16,48,2048]{2,1,0:T(8,128)(2,1)S(1)}, u32[]{:S(2)}, u32[]{:S(2)}) async-start(bf16[16,48,2048]{2,1,0:T(8,128)(2,1)} %constant_dynamic-slice_fusion.1), calls=%async_computation | async-start | bytes 6291456 | tf_op jit(solution)/shard_map/all_to_all | solution.py:74
  38.1 0.7 all-gather.7.cloned.1.call-update
  38.9 0.1 slice_reduce_fusion
  39.0 1.3 sort.31
  40.2 0.6 fusion.28
  42.2 0.7 pad_add_fusion
  42.8 1.3 ragged-dot-metadata
  44.1 1.3 sort.32
  45.5 53.5 %all-to-all-done = bf16[16,48,2048]{2,1,0:T(8,128)(2,1)S(1)} async-done(((bf16[16,48,2048]{2,1,0:T(8,128)(2,1)}), bf16[16,48,2048]{2,1,0:T(8,128)(2,1)S(1)}, u32[]{:S(2)}, u32[]{:S(2)}) %all-to-all-start) | async-done | bytes 3145760 | tf_op jit(solution)/shard_map/all_to_all | solution.py:74
  99.0 2.4 gather_fusion.1
  101.4 27.3 %reshape.140 = bf16[2,2048,1536]{2,1,0:T(8,128)(2,1)} reshape(bf16[2,2048,2,768]{3,2,1,0:T(2,128)(2,1)} %all-gather.5.cloned.1.call-done) | data formatting | bytes 25165824 | tf_op jit(solution)/shard_map/reshape | solution.py:27
  128.7 13.4 %ragged-dot-none.1 = f32[768,1536]{1,0:T(8,128)} custom-call(s32[1]{0:T(128)} %get-tuple-element.41, s32[3]{0:T(128)} %get-tuple-element.42, s32[4]{0:T(128)} %get-tuple-element.43, s32[4]{0:T(128)} %get-tuple-element.44, s32[1]{0:T(128)} %get-tuple-element.41, bf16[768,2048]{1,0:T(8,128)(2,1)} %bitcast.108, bf16[2,2048,1536]{2,1,0:T(8,128)(2,1)} %reshape.140), custom_call_target="tpu_custom_call" | custom-call | flops 4831838208 | bytes 20447240 | tf_op jit(solution)/shard_map/ragged_dot_general/ragged-dot-none
  142.1 4.1 %fusion.15 = bf16[768,768]{1,0:T(8,128)(2,1)} fusion(f32[768,1536]{1,0:T(8,128)} %ragged-dot-none.1), kind=kLoop, calls=%fused_computation.29 | loop fusion | flops 3538944 | bytes 5898240 | tf_op jit(solution)/shard_map/convert_element_type | solution.py:31
  146.1 9.5 %ragged-dot-none = f32[768,2048]{1,0:T(8,128)} custom-call(s32[1]{0:T(128)} %get-tuple-element.41, s32[3]{0:T(128)} %get-tuple-element.42, s32[4]{0:T(128)} %get-tuple-element.43, s32[4]{0:T(128)} %get-tuple-element.44, s32[1]{0:T(128)} %get-tuple-element.41, bf16[768,768]{1,0:T(8,128)(2,1)} %fusion.15, bf16[2,768,2048]{2,1,0:T(8,128)(2,1)} %all-gather.7.cloned.1.call-done), custom_call_target="tpu_custom_call" | custom-call | flops 2415919104 | bytes 13762568 | tf_op jit(solution)/shard_map/ragged_dot_general/ragged-dot-none
  155.7 3.6 gather_fusion.2
  159.3 85.6 %all_to_all.10 = bf16[16,48,2048]{2,1,0:T(8,128)(2,1)} all-to-all(bf16[16,48,2048]{2,1,0:T(8,128)(2,1)S(1)} %gather_fusion.2), channel_id=1, replica_groups=mesh['expert'=16,'half'=2] {'expert'}, dimensions={0} | all-to-all | bytes 6291456 | tf_op jit(solution)/shard_map/all_to_all | solution.py:79
  245.0 0.2 all-gather.11.cloned.1.call-start
  245.2 0.1 copy.69
  245.3 2.0 copy.82
  247.4 2.4 copy.70
  249.8 10.4 %all-gather.9.cloned.1.call-done = bf16[16,96,2048]{2,1,0:T(8,128)(2,1)} async-done(((bf16[16,48,2048]{2,1,0:T(8,128)(2,1)}), bf16[16,96,2048]{2,1,0:T(8,128)(2,1)}) %all-gather.9.cloned.1.call-update) | async-done | bytes 6291472 | tf_op jit(solution)/shard_map/all_gather | solution.py:82
  260.2 12.4 %gather_fusion.3 = bf16[1024,2048]{1,0:T(8,128)(2,1)} fusion(bf16[1536,2048]{1,0:T(8,128)(2,1)} %bitcast.102, s32[1024]{0:T(1024)S(1)} %broadcast_clamp_fusion), kind=kCustom, calls=%fused_computation.3 | custom fusion | bytes 8392704 | tf_op jit(solution)/shard_map/gather | solution.py:85
  272.7 6.7 %fusion.14 = f32[128,2048]{1,0:T(8,128)S(1)} fusion(bf16[1024,2048]{1,0:T(8,128)(2,1)} %gather_fusion.3, f32[128,8]{1,0:T(8,128)S(1)} %copy.69), kind=kLoop, calls=%fused_computation.27 | loop fusion | flops 6029312 | bytes 5246976 | tf_op jit(solution)/shard_map/reduce_sum | solution.py:89
  279.4 0.2 multiply_reduce_fusion
  279.6 0.8 fusion.17
  280.6 0.1 copy.71
  280.7 0.1 copy.72
  280.8 0.7 pad_maximum_fusion
  281.5 4.7 %fusion.29 = f32[128,2048]{1,0:T(8,128)S(1)} fusion(bf16[2048,2048]{1,0:T(8,128)(2,1)} %param.20, f32[128,2048]{1,0:T(8,128)S(1)} %get-tuple-element.109, f32[2048]{0:T(1024)S(1)} %copy-done.5, f32[128]{0:T(128)S(1)} %add_rsqrt_fusion.1), kind=kOutput, calls=%fused_computation.78 | convolution fusion | flops 1074528256 | bytes 10494464 | tf_op jit(solution)/shard_map/dot_general | solution.py:93
  286.3 0.2 copy.84
  286.5 0.3 reduce_sum.71
  286.9 0.2 copy.74
  287.1 0.2 copy.83
  287.3 0.4 fusion.16
  287.7 0.1 copy.75
  287.8 55.7 %all-gather.11.cloned.1.call-done = bf16[2048,2,256]{2,0,1:T(8,128)(2,1)} async-done(((bf16[128,2,256]{2,0,1:T(8,128)(2,1)}), bf16[2048,2,256]{2,0,1:T(8,128)(2,1)}) %all-gather.11.cloned.1.call-update) | async-done | bytes 2097168 | tf_op jit(solution)/shard_map/all_gather | solution.py:121
  343.5 4.0 %reshape.144 = bf16[2,1024,2,2,128]{4,3,1,0,2:T(2,128)(2,1)} reshape(bf16[2048,2,256]{2,0,1:T(8,128)(2,1)} %all-gather.11.cloned.1.call-done) | data formatting | bytes 4194304 | tf_op jit(solution)/shard_map/reshape | solution.py:124
  347.5 29.5 %while.15 = (s32[]{:T(128)}, f32[2,1024]{1,0:T(2,128)S(1)}, f32[2,1024]{1,0:T(2,128)S(1)}, f32[2,1024,128]{2,1,0:T(8,128)S(1)}, bf16[2,1024,2,2,128]{4,3,1,0,2:T...) while((s32[]{:T(128)}, f32[2,1024]{1,0:T(2,128)S(1)}, ...), condition=%wide.region_14.15_spmd.clone, body=%wide.region_11.14_spmd.clone.sunk | while | flops 1091315712 | bytes 66715776 | solution.py:146
  347.5 1.9 constant_dynamic-slice_fusion.3
  349.4 0.1 copy.92
  349.6 4.5 %bitcast_reduce_fusion.2 = (f32[2,1024]{1,0:T(2,128)S(1)}, f32[2,1024,1024]{2,1,0:T(8,128)}) fusion(bf16[2,1024,128]{2,1,0:T(8,128)(2,1)S(1)} %get-tuple-element.178, bf16[1024,2,2,128]{3,0,2,1:T(8,128)(2,1)S(1)} %bitcast.103), kind=kOutput, calls=%fused_computation.6.clone.1 | convolution fusion | flops 541063168 | bytes 9445376 | tf_op jit(solution)/shard_map/while/body/eval_jaxpr/hrd,khd->hrk/dot_general | solution.py:129
  354.1 4.9 %fusion.42 = f32[2,1024]{1,0:T(2,128)S(1)} fusion(f32[2,1024,1024]{2,1,0:T(8,128)} %get-tuple-element.154, f32[2,1024]{1,0:T(2,128)S(1)} %fusion.41), kind=kLoop, calls=%fused_computation.9.clone.1 | loop fusion | flops 6289408 | bytes 8404992 | tf_op jit(solution)/shard_map/while/body/eval_jaxpr/reduce_sum | solution.py:137
  359.0 0.8 copy-done
  359.8 2.4 fusion.44
  362.3 2.0 constant_dynamic-slice_fusion.3
  364.2 0.1 copy.92
  364.4 4.5 %bitcast_reduce_fusion.2 = (f32[2,1024]{1,0:T(2,128)S(1)}, f32[2,1024,1024]{2,1,0:T(8,128)}) fusion(bf16[2,1024,128]{2,1,0:T(8,128)(2,1)S(1)} %get-tuple-element.178, bf16[1024,2,2,128]{3,0,2,1:T(8,128)(2,1)S(1)} %bitcast.103), kind=kOutput, calls=%fused_computation.6.clone.1 | convolution fusion | flops 541063168 | bytes 9445376 | tf_op jit(solution)/shard_map/while/body/eval_jaxpr/hrd,khd->hrk/dot_general | solution.py:129
  368.9 4.9 %fusion.42 = f32[2,1024]{1,0:T(2,128)S(1)} fusion(f32[2,1024,1024]{2,1,0:T(8,128)} %get-tuple-element.154, f32[2,1024]{1,0:T(2,128)S(1)} %fusion.41), kind=kLoop, calls=%fused_computation.9.clone.1 | loop fusion | flops 6289408 | bytes 8404992 | tf_op jit(solution)/shard_map/while/body/eval_jaxpr/reduce_sum | solution.py:137
  373.8 0.8 copy-done
  374.6 2.4 fusion.44
  377.0 0.3 divide_convert_fusion
  377.4 0.3 copy.77
  377.7 0.9 copy.90
  (66 shorter events, 1.0 us)
Async XLA Ops:
  7.2 0.8 copy-start.6
  7.2 6.1 %copy-start.3 = (bf16[128,2048]{1,0:T(8,128)(2,1)S(1)}, bf16[128,2048]{1,0:T(8,128)(2,1)}, u32[]{:S(2)}) copy-start(bf16[128,2048]{1,0:T(8,128)(2,1)} %param.13) | copy-start | bytes 1572868
  7.2 94.2 %all-gather.5.cloned.1.call-start = ((), (), s32[]{:S(2)}) async-start(), calls=%async_computation.2 | async-start | bytes 18874368 | tf_op jit(solution)/shard_map/all_gather | solution.py:70
  29.4 9.4 %copy-start.7 = (s32[2048]{0:T(1024)S(1)}, s32[2048]{0:T(1024)}, u32[]{:S(2)}) copy-start(s32[2048]{0:T(1024)} %param.14) | copy-start | bytes 24580
  29.4 69.5 %all-to-all-start = ((bf16[16,48,2048]{2,1,0:T(8,128)(2,1)}), bf16[16,48,2048]{2,1,0:T(8,128)(2,1)S(1)}, u32[]{:S(2)}, u32[]{:S(2)}) async-start(bf16[16,48,2048]{2,1,0:T(8,128)(2,1)} %constant_dynamic-slice_fusion.1), calls=%async_computation | async-start | bytes 6291456 | tf_op jit(solution)/shard_map/all_to_all | solution.py:74
  38.0 108.1 %all-gather.7.cloned.1.call-start = ((), (), s32[]{:S(2)}) async-start(), calls=%async_computation.3 | async-start | bytes 9437184 | tf_op jit(solution)/shard_map/all_gather | solution.py:71
  38.8 221.4 %all-gather.9.cloned.1.call-start = ((), (), s32[]{:S(2)}) async-start(), calls=%async_computation.4 | async-start | bytes 9437184 | tf_op jit(solution)/shard_map/all_gather | solution.py:82
  159.3 85.9 %copy-start.8 = (f32[128,8]{0,1:T(8,128)S(1)}, f32[128,8]{0,1:T(8,128)}, u32[]{:S(2)}) copy-start(f32[128,8]{0,1:T(8,128)} %param.16) | copy-start | bytes 12292
  245.0 98.5 %all-gather.11.cloned.1.call-start = ((), (), s32[]{:S(2)}) async-start(), calls=%async_computation.5 | async-start | bytes 2228224 | tf_op jit(solution)/shard_map/all_gather | solution.py:121
  272.6 6.7 %copy-start.4 = (bf16[128,2048]{1,0:T(8,128)(2,1)S(1)}, bf16[128,2048]{1,0:T(8,128)(2,1)}, u32[]{:S(2)}) copy-start(bf16[128,2048]{1,0:T(8,128)(2,1)} %param.13) | copy-start | bytes 1572868
  272.7 7.0 %copy-start.2 = (bf16[512,2048]{1,0:T(8,128)(2,1)S(1)}, bf16[512,2048]{1,0:T(8,128)(2,1)}, u32[]{:S(2)}) copy-start(bf16[512,2048]{1,0:T(8,128)(2,1)} %copy.70) | copy-start | bytes 6291460
  272.7 7.0 %copy-start.5 = (f32[2048]{0:T(1024)S(1)}, f32[2048]{0:T(1024)}, u32[]{:S(2)}) copy-start(f32[2048]{0:T(1024)} %param.19) | copy-start | bytes 24580
  279.3 1.1 copy-start.10
  279.6 6.6 %copy-start.1 = (f32[128,2048]{1,0:T(8,128)}, f32[128,2048]{1,0:T(8,128)S(1)}, u32[]{:S(2)}) copy-start(f32[128,2048]{1,0:T(8,128)S(1)} %get-tuple-element.109) | copy-start | bytes 3145732
  286.2 1.1 copy-start.9
  354.1 5.8 %copy-start = (f32[2,1024,1024]{2,1,0:T(8,128)S(1)}, f32[2,1024,1024]{2,1,0:T(8,128)}, u32[]{:S(2)}) copy-start(f32[2,1024,1024]{2,1,0:T(8,128)} %get-tuple-element.154) | copy-start | bytes 25165828 | tf_op jit(solution)/shard_map/while
  368.9 5.8 %copy-start = (f32[2,1024,1024]{2,1,0:T(8,128)S(1)}, f32[2,1024,1024]{2,1,0:T(8,128)}, u32[]{:S(2)}) copy-start(f32[2,1024,1024]{2,1,0:T(8,128)} %get-tuple-element.154) | copy-start | bytes 25165828 | tf_op jit(solution)/shard_map/while
Sparse Core Ops, SparseCore 0:
  9.6 28.7 all-gather.4
  40.4 18.0 all-gather.6
  245.1 15.0 all-gather.8
  281.6 61.8 all-gather.10
where the time goes:
time: 387 us; the launch traced here: 385 us
  waiting for transfers between devices  121 us (31%)
  blocking collectives  85.6 us (22%)
  local copies, waits for them, and re-layouts  79.3 us (20%)
  other arithmetic  31.4 us (8%)
  Pallas kernels  24.2 us (6%)
  matrix products  19.2 us (5%)
  between operations  15.5 us (4%)
  starting transfers between devices  8.94 us (2%)
    all_to_all x1, blocking collectives, body(): lax.all_to_all(whole_out.astype(jnp.bfloat16), 'expert', split_axis=0, co...  85.6 us
    all_gather x1, waiting for transfers between devices, body(): kv_piece = lax.all_gather(stacked, 'expert', axis=0, tiled=True)  55.7 us
    all_to_all x1, waiting for transfers between devices, body(): lax.all_to_all(my_slots, 'expert', split_axis=0, concat_axis=0, tiled=True)  53.5 us
    reshape x1, local copies, waits for them, and re-layouts, expert_pass(): w_gate_up.reshape(local_experts, model_width, 2 * half_units)  27.3 us
    another operation x2, Pallas kernels  22.9 us
    gather x1, local copies, waits for them, and re-layouts, body(): returned.reshape(groups * capacity, part_width)[slot_index]  12.4 us
    all_gather x1, waiting for transfers between devices, body(): returned = lax.all_gather(mine_back, 'half', axis=1, tiled=True)  10.4 us
    reduce_sum x2, other arithmetic, step_block(): totals_out = totals_in * rescale + jnp.sum(weights, axis=-1)  9.82 us
  transfers between devices with their start and end apart: 5, of which 3 were waited for; matrix products, arithmetic and copies ran while one was open for 18% of the time, Pallas kernels for 4%

commit v1 on v0

v1 whole, which is shorter than its diff:
```python
import functools

import jax
import jax.numpy as jnp
from jax import lax
from jax.experimental import pallas as pl
from jax.experimental.pallas import tpu as pltpu
from jax.sharding import PartitionSpec as P

EPSILON = 1e-06
LANES = 128
KEYS_AT_ONCE = 2048
MIB = 1024 * 1024


def rms_scale(values, gain_row):
    mean_sq = jnp.mean(values * values, axis=-1, keepdims=True)
    return values * lax.rsqrt(mean_sq + EPSILON) * gain_row


def swap(value, mask_first, mask_second):
    pairs = []
    for expert in range(lax.axis_size("expert")):
        for half, mask in enumerate((mask_first, mask_second)):
            pairs.append((2 * expert + half, 2 * (expert ^ mask) + half))
    return lax.ppermute(value, ("expert", "half"), pairs)


def swap_half(value):
    return lax.ppermute(value, "half", [(0, 1), (1, 0)])


def expert_kernel(
    block_rows,
    kinds_ref,
    x_ref,
    pick_ref,
    own_gu,
    other_gu,
    own_down,
    other_down,
    keep_ref,
    send_ref,
    gu_ref,
    down_ref,
    act_ref,
    sems,
):
    width = own_down.shape[2]
    units = own_down.shape[1]
    tiles = x_ref.shape[0] // (4 * block_rows)
    copies = []
    for m in range(2):
        for k, (gu, down) in enumerate(((own_gu, own_down), (other_gu, other_down))):
            group = [
                pltpu.make_async_copy(
                    gu.at[m, c], gu_ref.at[m, k, :, pl.ds(c * units, units)], sems.at[m, k, c]
                )
                for c in range(2)
            ]
            group.append(
                pltpu.make_async_copy(
                    down.at[m], down_ref.at[m, pl.ds(k * units, units)], sems.at[m, k, 2]
                )
            )
            copies.append(group)
            for copy in group:
                copy.start()
    tile_rows = 4 * block_rows
    for m in range(2):
        for k in range(2):
            for copy in copies[2 * m + k]:
                copy.wait()
        for tile in range(tiles):
            rows = pl.ds(tile * tile_rows, tile_rows)
            kinds = [kinds_ref[4 * tile + p] for p in range(4)]
            row_block = lax.broadcasted_iota(jnp.int32, (tile_rows, 1), 0) // block_rows
            row_kind = jnp.where(
                row_block == 0,
                kinds[0],
                jnp.where(row_block == 1, kinds[1], jnp.where(row_block == 2, kinds[2], kinds[3])),
            )
            used = sum((kind == m).astype(jnp.int32) for kind in kinds) > 0
            half_tiles = tiles // 2 if tiles > 1 else 0

            def store(value, ref, at, count, row_at):
                mine = row_kind[row_at : row_at + count] == m
                if m == 0:
                    ref[at : at + count] = jnp.where(mine, value, 0.0).astype(ref.dtype)
                else:
                    before = ref[at : at + count].astype(jnp.float32)
                    ref[at : at + count] = jnp.where(mine, value, before).astype(ref.dtype)

            def place(value):
                if tiles == 1:
                    cut = tile_rows // 2
                    store(value[:cut], keep_ref, 0, cut, 0)
                    store(value[cut:], send_ref, 0, cut, cut)
                elif tile < half_tiles:
                    store(value, keep_ref, tile * tile_rows, tile_rows, 0)
                else:
                    store(value, send_ref, (tile - half_tiles) * tile_rows, tile_rows, 0)

            @pl.when(used)
            def _():
                x = x_ref[rows, :width]
                extra = x_ref[rows, width:].astype(jnp.float32)
                weight = jnp.sum(extra * pick_ref[...], axis=-1, keepdims=True)
                for k in range(2):
                    pre = jnp.dot(x, gu_ref[m, k], preferred_element_type=jnp.float32)
                    gate, up = pre[:, :units], pre[:, units:]
                    act = gate / (1.0 + jnp.exp(-gate)) * up
                    act_ref[:, k * units : (k + 1) * units] = act.astype(jnp.bfloat16)
                out = jnp.dot(act_ref[...], down_ref[m], preferred_element_type=jnp.float32)
                place(out.astype(jnp.bfloat16).astype(jnp.float32) * weight)

            if m == 0:

                @pl.when(jnp.logical_not(used))
                def _():
                    place(jnp.zeros((tile_rows, width), jnp.float32))


def expert_call(kinds, rows, pick, own_gu, other_gu, own_down, other_down, block_rows):
    total = rows.shape[0]
    _, units, width = own_down.shape
    half = total // 2
    vmem, anywhere = pl.BlockSpec(memory_space=pltpu.VMEM), pl.BlockSpec(memory_space=pl.ANY)
    return pl.pallas_call(
        functools.partial(expert_kernel, block_rows),
        out_shape=(
            jax.ShapeDtypeStruct((half, width), jnp.float32),
            jax.ShapeDtypeStruct((half, width), jnp.bfloat16),
        ),
        in_specs=[pl.BlockSpec(memory_space=pltpu.SMEM), vmem, vmem] + [anywhere] * 4,
        out_specs=(vmem, vmem),
        scratch_shapes=[
            pltpu.VMEM((2, 2, width, 2 * units), jnp.bfloat16),
            pltpu.VMEM((2, 2 * units, width), jnp.bfloat16),
            pltpu.VMEM((4 * block_rows, 2 * units), jnp.bfloat16),
            pltpu.SemaphoreType.DMA((2, 2, 3)),
        ],
        compiler_params=pltpu.CompilerParams(vmem_limit_bytes=48 * MIB),
        cost_estimate=pl.CostEstimate(
            flops=2 * total * width * 6 * units * 2,
            bytes_accessed=2 * 2 * 6 * units * width,
            transcendentals=total * units * 4,
        ),
        name="experts",
    )(kinds, rows, pick, own_gu, other_gu, own_down, other_down)


def attention_kernel(head_dim, group, q_ref, *refs):
    kv_refs, out_ref = refs[:-1], refs[-1]
    kv_heads = kv_refs[0].shape[1] // (2 * head_dim)
    scale = head_dim**-0.5
    rows = q_ref.shape[0]
    step = max(1, KEYS_AT_ONCE // kv_refs[0].shape[0])
    def columns(ref, head, count=1):
        return ref[:, pl.ds(pl.multiple_of(head * head_dim, head_dim), count * head_dim)]

    def two_heads(pair, carry):
        g = pair // (group // 2)
        both = columns(q_ref, 2 * pair, 2)
        q = jnp.concatenate([both[:, :head_dim], both[:, head_dim:]], axis=0)
        keys = [columns(ref, g) for ref in kv_refs]
        vals = [columns(ref, kv_heads + g) for ref in kv_refs]
        peak, total, mixed = None, 0.0, 0.0
        for at in range(0, len(keys), step):
            scores = [
                lax.dot_general(q, k, (((1,), (1,)), ((), ())), preferred_element_type=jnp.float32)
                for k in keys[at : at + step]
            ]
            peaks = [jnp.max(s, axis=-1, keepdims=True) for s in scores]
            if peak is not None:
                before = peak
                peak = functools.reduce(jnp.maximum, peaks + [before])
                shrink = jnp.exp((before - peak) * scale)
                total, mixed = total * shrink, mixed * shrink
            else:
                peak = functools.reduce(jnp.maximum, peaks)
            for s, v in zip(scores, vals[at : at + step]):
                p = jnp.exp((s - peak) * scale)
                total = total + jnp.sum(p, axis=-1, keepdims=True)
                mixed = mixed + jnp.dot(
                    p.astype(jnp.bfloat16), v, preferred_element_type=jnp.float32
                )
        mixed = (mixed / total).astype(jnp.bfloat16)
        at = pl.multiple_of(2 * pair * head_dim, 2 * head_dim)
        out_ref[:, pl.ds(at, 2 * head_dim)] = jnp.concatenate([mixed[:rows], mixed[rows:]], axis=1)
        return carry

    lax.fori_loop(0, kv_heads * group // 2, two_heads, 0)


def attention_call(queries, kv_parts, head_dim, group):
    vmem = pl.BlockSpec(memory_space=pltpu.VMEM)
    rows, width = queries.shape
    keys = sum(part.shape[0] for part in kv_parts)
    return pl.pallas_call(
        functools.partial(attention_kernel, head_dim, group),
        out_shape=jax.ShapeDtypeStruct((rows, width), jnp.bfloat16),
        in_specs=[vmem] * (1 + len(kv_parts)),
        out_specs=vmem,
        compiler_params=pltpu.CompilerParams(vmem_limit_bytes=48 * MIB),
        cost_estimate=pl.CostEstimate(
            flops=4 * rows * keys * width,
            bytes_accessed=4 * rows * width,
            transcendentals=rows * keys * width // head_dim,
        ),
        name="attention",
    )(queries, *kv_parts)


def body(
    hidden_in,
    modality,
    expert_ids,
    route_weights,
    w_gate_up,
    w_down,
    norm_gain,
    w_query,
    key_value_weight,
    q_gain,
    k_gain,
):
    tok_rows, model_width = hidden_in.shape
    groups = lax.axis_size("expert")
    me, core = lax.axis_index("expert"), lax.axis_index("half")
    block_rows = tok_rows // 2
    slots = groups // 4
    per_group = max(1, slots // 4)
    slot_groups = [list(range(s, s + per_group)) for s in range(0, slots, per_group)]

    own_gu = w_gate_up.transpose(0, 2, 1, 3)
    other_down = swap_half(w_down)
    other_gu = swap_half(own_gu)

    chosen = expert_ids[:, :, None] == jnp.arange(groups, dtype=jnp.int32)
    table = jnp.sum(jnp.where(chosen, route_weights[:, :, None], 0.0), axis=1)
    table_high = table.astype(jnp.bfloat16)
    table_low = (table - table_high.astype(jnp.float32)).astype(jnp.bfloat16)
    extra = [table_high, table_low]
    if 2 * groups < LANES:
        extra.append(jnp.zeros((tok_rows, LANES - 2 * groups), jnp.bfloat16))
    payload = jnp.concatenate([hidden_in] + extra, axis=1)
    payload = lax.dynamic_slice_in_dim(payload, core * block_rows, block_rows, 0)
    lane = jnp.arange(LANES, dtype=jnp.int32)
    pick = ((lane == me) | (lane == me + groups)).astype(jnp.float32)[None, :]

    kind_of = modality.reshape(groups, tok_rows)[:, 0]
    near = jnp.where(core == 0, jnp.array([0, 1, 2, 3], jnp.int32), jnp.array([0, 2, 1, 3], jnp.int32))

    arrived = {0: payload}
    for s in range(1, slots):
        arrived[s] = swap(payload, 4 * s, 4 * s)
    returned = {}
    for members in slot_groups:
        first = jnp.concatenate([arrived[s] for s in members], axis=0)
        two = jnp.concatenate([first, swap(first, 1, 2)], axis=0)
        four = jnp.concatenate([two, swap(two, 2, 1)], axis=0)
        sources = me ^ (4 * jnp.array(members, jnp.int32)[None, :]) ^ near[:, None]
        kinds = kind_of[sources.reshape(-1)]
        keep, send = expert_call(
            kinds, four, pick, own_gu, other_gu, w_down, other_down, block_rows
        )
        keep = keep + swap(send, 2, 1).astype(jnp.float32)
        cut = first.shape[0]
        back = swap(keep[cut:].astype(jnp.bfloat16), 1, 2)
        keep = keep[:cut] + back.astype(jnp.float32)
        for i, s in enumerate(members):
            returned[s] = keep[i * block_rows : (i + 1) * block_rows]
    mixture = returned[0]
    for s in range(1, slots):
        mixture = mixture + swap(returned[s].astype(jnp.bfloat16), 4 * s, 4 * s).astype(jnp.float32)
    mine = payload[:, :model_width].astype(jnp.float32) + mixture
    theirs = swap_half(mine)
    hidden_out = jnp.where(
        core == 0,
        jnp.concatenate([mine, theirs], axis=0),
        jnp.concatenate([theirs, mine], axis=0),
    )

    normed = rms_scale(hidden_out, norm_gain).astype(jnp.bfloat16)
    head_dim = q_gain.shape[0]
    kv_width = key_value_weight.shape[2]
    kv_heads = kv_width // head_dim
    key_value = jnp.dot(
        normed,
        key_value_weight.reshape(model_width, 2 * kv_width),
        preferred_element_type=jnp.float32,
    )
    keys = rms_scale(key_value[:, :kv_width].reshape(tok_rows, kv_heads, head_dim), k_gain)
    own_kv = jnp.concatenate(
        [keys.reshape(tok_rows, kv_width), key_value[:, kv_width:]], axis=1
    ).astype(jnp.bfloat16)
    queries = jnp.dot(normed, w_query, preferred_element_type=jnp.float32)
    heads = queries.shape[1] // head_dim
    queries = rms_scale(queries.reshape(tok_rows, heads, head_dim), q_gain)
    queries = queries.reshape(tok_rows, heads * head_dim).astype(jnp.bfloat16)

    arrived = {0: own_kv}
    for s in range(1, slots):
        arrived[s] = swap(own_kv, 4 * s, 4 * s)
    kv_parts = []
    for members in slot_groups:
        first = jnp.concatenate([arrived[s] for s in members], axis=0)
        two = jnp.concatenate([first, swap(first, 1, 2)], axis=0)
        kv_parts += [two, swap(two, 2, 1)]
    attended = attention_call(queries, kv_parts, head_dim, heads // kv_heads)
    return hidden_out, attended


def solution(mesh):
    in_specs = (
        P("expert", None),
        P(),
        P("expert", None),
        P("expert", None),
        P("expert", None, None, "half"),
        P("expert", "half", None),
        P(),
        P(None, "half"),
        P(None, None, "half"),
        P(),
        P(),
    )
    out_specs = (P("expert", None), P("expert", "half"))
    return jax.shard_map(body, mesh=mesh, in_specs=in_specs, out_specs=out_specs, check_vma=False)
```

time: 387 us -> 190 us (0.49)
  blocking collectives: 85.6 us -> 0 us
  local copies, waits for them, and re-layouts: 79.3 us -> 14 us
  waiting for transfers between devices: 121 us -> 64.7 us
  starting transfers between devices: 8.94 us -> 48.4 us
  Pallas kernels: 24.2 us -> 47 us
  other arithmetic: 31.4 us -> 9.41 us
  between operations: 15.5 us -> 1.18 us
  matrix products: 19.2 us -> 5.2 us
    all_to_all x1 -> x0, blocking collectives: 85.6 us -> none  [body(): lax.all_to_all(whole_out.astype(jnp.bfloat16), 'expert', split_axis=0, co...]
    all_gather x4 -> x0, waiting for transfers between devices: 66.1 us -> none  [the longest x1 55.7 us: body(): kv_piece = lax.all_gather(stacked, 'expert', axis=0, tiled=True)]
    ppermute x0 -> x36, waiting for transfers between devices: none -> 64.7 us  [the longest x33 63.5 us: swap(): return lax.ppermute(value, ('expert', 'half'), pairs)]
    all_to_all x1 -> x0, waiting for transfers between devices: 53.5 us -> none  [body(): lax.all_to_all(my_slots, 'expert', split_axis=0, concat_axis=0, tiled=True)]
    ppermute x0 -> x36, starting transfers between devices: none -> 48.4 us  [the longest x33 47.8 us: swap(): return lax.ppermute(value, ('expert', 'half'), pairs)]
    pallas_call x0 -> x5, Pallas kernels: none -> 47 us  [the longest x4 37.9 us: expert_call(): pl.pallas_call(functools.partial(expert_kernel, block_rows), out_shape=(j...]
    reshape x2 -> x0, local copies, waits for them, and re-layouts: 31.3 us -> none  [the longest x1 27.3 us: expert_pass(): w_gate_up.reshape(local_experts, model_width, 2 * half_units)]
    gather x4, local copies, waits for them, and re-layouts: 25.6 us -> 2.56 us  [body(): kinds = kind_of[sources.reshape(-1)]]
  transfers between devices with their start and end apart: 5 -> 36, of which waited for: 3 -> 18; matrix products, arithmetic and copies ran while one was open for 18% -> 10% of each run, Pallas kernels for 4% -> 15%
where the time goes in v1:
time: 190 us
  waiting for transfers between devices  64.7 us (34%)
  starting transfers between devices  48.4 us (25%)
  Pallas kernels  47 us (25%)
  local copies, waits for them, and re-layouts  14 us (7%)
  other arithmetic  9.41 us (5%)
  matrix products  5.2 us (3%)
    ppermute x33, waiting for transfers between devices, swap(): return lax.ppermute(value, ('expert', 'half'), pairs)  63.5 us
    ppermute x33, starting transfers between devices, swap(): return lax.ppermute(value, ('expert', 'half'), pairs)  47.8 us
    pallas_call x4, Pallas kernels, expert_call(): pl.pallas_call(functools.partial(expert_kernel, block_rows), out_shape=(j...  37.9 us
    pallas_call x1, Pallas kernels, attention_call(): pl.pallas_call(functools.partial(attention_kernel, head_dim, group), out_...  9.1 us
    unnamed x26, local copies, waits for them, and re-layouts  7.28 us
    dot_general x1, matrix products, body(): queries = jnp.dot(normed, w_query, preferred_element_type=jnp.float32)  4.72 us
  transfers between devices with their start and end apart: 36, of which 18 were waited for; matrix products, arithmetic and copies ran while one was open for 10% of the time, Pallas kernels for 15%

profile of v1, /device:TPU:0, one launch (start us, length us, event | category | flops | bytes accessed | tf_op | source)
XLA Modules:
  0.0 189.8 jit_solution(17712799496923511609)
XLA Ops:
  0.7 6.4 %copy.53 = bf16[2,2048,2,384]{3,1,2,0:T(8,128)(2,1)} copy(bf16[2,2048,2,384]{3,2,1,0:T(2,128)(2,1)} %param.21) | data formatting | bytes 12582912 | tf_op args[4]
  7.9 1.9 concatenate.53
  9.8 1.0 constant_dynamic-slice_fusion
  10.7 2.7 %collective-permute-start.6 = (bf16[64,2176]{1,0:T(8,128)(2,1)S(1)}, bf16[64,2176]{1,0:T(8,128)(2,1)}, u32[]{:S(2)}, u32[]{:S(2)}) collective-permute-start(bf16[64,2176]{1,0:T(8,128)(2,1)S(1)} %constant_dynamic-slice_fusion), channel_id=1, source_target_pairs={{0,8},{1,9},{2,10},{3,11},{4,12},{5,13},{6,14},{7,15},{8,0},{9,1},... | collective-permute-start | bytes 835592 | tf_op jit(solution)/shard_map/ppermute | solution.py:26
  13.4 2.6 %collective-permute-start.12 = (bf16[64,2176]{1,0:T(8,128)(2,1)S(1)}, bf16[64,2176]{1,0:T(8,128)(2,1)}, u32[]{:S(2)}, u32[]{:S(2)}) collective-permute-start(bf16[64,2176]{1,0:T(8,128)(2,1)S(1)} %constant_dynamic-slice_fusion), channel_id=1, source_target_pairs={{0,16},{1,17},{2,18},{3,19},{4,20},{5,21},{6,22},{7,23},{8,24},{9,... | collective-permute-start | bytes 835592 | tf_op jit(solution)/shard_map/ppermute | solution.py:26
  16.0 1.5 collective-permute-start
  17.7 0.6 gather_fusion.1
  18.3 0.6 gather_fusion.2
  18.9 0.6 gather_fusion.3
  19.6 0.6 gather_fusion
  20.2 6.4 %collective-permute-done.6 = bf16[64,2176]{1,0:T(8,128)(2,1)} collective-permute-done((bf16[64,2176]{1,0:T(8,128)(2,1)S(1)}, bf16[64,2176]{1,0:T(8,128)(2,1)}, u32[]{:S(2)}, u32[]{:S(2)}) %collective-permute-start.6) | collective-permute-done | bytes 278560 | tf_op jit(solution)/shard_map/ppermute | solution.py:26
  26.7 2.6 %collective-permute-start.18 = (bf16[64,2176]{1,0:T(8,128)(2,1)S(1)}, bf16[64,2176]{1,0:T(8,128)(2,1)S(1)}, u32[]{:S(2)}, u32[]{:S(2)}) collective-permute-start(bf16[64,2176]{1,0:T(8,128)(2,1)S(1)} %constant_dynamic-slice_fusion), channel_id=1, source_target_pairs={{0,24},{1,25},{2,26},{3,27},{4,28},{5,29},{6,30},{7,31},{8,16},{9,... | collective-permute-start | bytes 835592 | tf_op jit(solution)/shard_map/ppermute | solution.py:26
  29.3 1.5 collective-permute-start.7
  30.8 1.0 pad_maximum_fusion.4
  31.8 1.6 collective-permute-start.1
  33.4 3.7 %collective-permute-done.18 = bf16[64,2176]{1,0:T(8,128)(2,1)S(1)} collective-permute-done((bf16[64,2176]{1,0:T(8,128)(2,1)S(1)}, bf16[64,2176]{1,0:T(8,128)(2,1)S(1)}, u32[]{:S(2)}, u32[]{:S(2)}) %collective-permute-start.18) | collective-permute-done | bytes 278560 | tf_op jit(solution)/shard_map/ppermute | solution.py:26
  37.0 1.4 collective-permute-start.13
  38.6 1.5 collective-permute-start.19
  40.0 1.0 pad_maximum_fusion.5
  41.0 4.0 %collective-permute-done.13 = bf16[64,2176]{1,0:T(8,128)(2,1)S(1)} collective-permute-done((bf16[64,2176]{1,0:T(8,128)(2,1)}, bf16[64,2176]{1,0:T(8,128)(2,1)S(1)}, u32[]{:S(2)}, u32[]{:S(2)}) %collective-permute-start.13) | collective-permute-done | bytes 278560 | tf_op jit(solution)/shard_map/ppermute | solution.py:26
  45.0 1.1 collective-permute-start.8
  46.1 1.0 pad_maximum_fusion.6
  47.1 1.7 collective-permute-done.19
  48.8 0.6 collective-permute-start.14
  49.5 1.5 collective-permute-start.20
  51.0 1.0 pad_maximum_fusion.x_ref
  52.0 2.5 %collective-permute-done.8 = bf16[128,2176]{1,0:T(8,128)(2,1)S(1)} collective-permute-done((bf16[128,2176]{1,0:T(8,128)(2,1)S(1)}, bf16[128,2176]{1,0:T(8,128)(2,1)S(1)}, u32[]{:S(2)}, u32[]{:S(2)}) %collective-permute-start.8) | collective-permute-done | bytes 557088 | tf_op jit(solution)/shard_map/ppermute | solution.py:26
  54.6 1.0 pad_maximum_fusion.1.x_ref
  55.6 4.9 %collective-permute-done.14 = bf16[128,2176]{1,0:T(8,128)(2,1)S(1)} collective-permute-done((bf16[128,2176]{1,0:T(8,128)(2,1)S(1)}, bf16[128,2176]{1,0:T(8,128)(2,1)S(1)}, u32[]{:S(2)}, u32[]{:S(2)}) %collective-permute-start.14) | collective-permute-done | bytes 557088 | tf_op jit(solution)/shard_map/ppermute | solution.py:26
  60.5 1.0 pad_maximum_fusion.2.x_ref
  61.6 4.9 %collective-permute-done.20 = bf16[128,2176]{1,0:T(8,128)(2,1)S(1)} collective-permute-done((bf16[128,2176]{1,0:T(8,128)(2,1)S(1)}, bf16[128,2176]{1,0:T(8,128)(2,1)S(1)}, u32[]{:S(2)}, u32[]{:S(2)}) %collective-permute-start.20) | collective-permute-done | bytes 557088 | tf_op jit(solution)/shard_map/ppermute | solution.py:26
  66.6 9.4 %experts.5 = (f32[128,2048]{1,0:T(8,128)S(1)}, bf16[128,2048]{1,0:T(8,128)(2,1)S(1)}) custom-call(s32[4]{0:T(128)S(1)} %gather_fusion.1, bf16[256,2176]{1,0:T(8,128)(2,1)S(1)} %pad_maximum_fusion.1.x_ref, f32[1,128]{1,0:T(1,128)S(1)} %or_convert_fusion.pick_ref, bf16[2,2,2048,384]{3,2,1,0:T(8,128)(2,1)} %bitcast.28.own_gu, ...), custom_call_target="tpu_custom_call" | custom-call | flops 4831838208 | bytes 18874368 | tf_op jit(solution)/shard_map/experts/pallas_call | solution.py:129
  76.0 1.1 collective-permute-start.9
  77.2 9.4 %experts.6 = (f32[128,2048]{1,0:T(8,128)S(1)}, bf16[128,2048]{1,0:T(8,128)(2,1)S(1)}) custom-call(s32[4]{0:T(128)S(1)} %gather_fusion.2, bf16[256,2176]{1,0:T(8,128)(2,1)S(1)} %pad_maximum_fusion.2.x_ref, f32[1,128]{1,0:T(1,128)S(1)} %or_convert_fusion.pick_ref, bf16[2,2,2048,384]{3,2,1,0:T(8,128)(2,1)} %bitcast.28.own_gu, ...), custom_call_target="tpu_custom_call" | custom-call | flops 4831838208 | bytes 18874368 | tf_op jit(solution)/shard_map/experts/pallas_call | solution.py:129
  86.6 1.0 collective-permute-start.15
  87.6 9.4 %experts.7 = (f32[128,2048]{1,0:T(8,128)S(1)}, bf16[128,2048]{1,0:T(8,128)(2,1)S(1)}) custom-call(s32[4]{0:T(128)S(1)} %gather_fusion.3, bf16[256,2176]{1,0:T(8,128)(2,1)S(1)} %pad_maximum_fusion.3.x_ref, f32[1,128]{1,0:T(1,128)S(1)} %or_convert_fusion.pick_ref, bf16[2,2,2048,384]{3,2,1,0:T(8,128)(2,1)} %bitcast.28.own_gu, ...), custom_call_target="tpu_custom_call" | custom-call | flops 4831838208 | bytes 18874368 | tf_op jit(solution)/shard_map/experts/pallas_call | solution.py:129
  97.0 1.1 collective-permute-start.21
  98.2 9.6 %experts.4 = (f32[128,2048]{1,0:T(8,128)S(1)}, bf16[128,2048]{1,0:T(8,128)(2,1)S(1)}) custom-call(s32[4]{0:T(128)S(1)} %gather_fusion, bf16[256,2176]{1,0:T(8,128)(2,1)S(1)} %pad_maximum_fusion.x_ref, f32[1,128]{1,0:T(1,128)S(1)} %or_convert_fusion.pick_ref, bf16[2,2,2048,384]{3,2,1,0:T(8,128)(2,1)} %bitcast.28.own_gu, ...), custom_call_target="tpu_custom_call" | custom-call | flops 4831838208 | bytes 18874368 | tf_op jit(solution)/shard_map/experts/pallas_call | solution.py:129
  107.8 1.0 collective-permute-start.4
  109.0 1.6 collective-permute-start.10
  111.4 1.6 collective-permute-start.22
  113.0 9.7 %collective-permute-done.4 = bf16[128,2048]{1,0:T(8,128)(2,1)S(1)} collective-permute-done((bf16[128,2048]{1,0:T(8,128)(2,1)S(1)}, bf16[128,2048]{1,0:T(8,128)(2,1)S(1)}, u32[]{:S(2)}, u32[]{:S(2)}) %collective-permute-start.4) | collective-permute-done | bytes 524320 | tf_op jit(solution)/shard_map/ppermute | solution.py:26
  122.9 1.6 collective-permute-start.5
  124.5 3.9 %collective-permute-start.11 = (bf16[64,2048]{1,0:T(8,128)(2,1)S(1)}, bf16[64,2048]{1,0:T(8,128)(2,1)S(1)}, u32[]{:S(2)}, u32[]{:S(2)}) collective-permute-start(bf16[64,2048]{1,0:T(8,128)(2,1)S(1)} %fusion.4), channel_id=1, source_target_pairs={{0,8},{1,9},{2,10},{3,11},{4,12},{5,13},{6,14},{7,15},{8,0},{9,1},... | collective-permute-start | bytes 786440 | tf_op jit(solution)/shard_map/ppermute | solution.py:26
  128.4 1.1 collective-permute-start.17
  129.6 1.5 collective-permute-start.23
  131.1 5.8 %collective-permute-done.11 = bf16[64,2048]{1,0:T(8,128)(2,1)S(1)} collective-permute-done((bf16[64,2048]{1,0:T(8,128)(2,1)S(1)}, bf16[64,2048]{1,0:T(8,128)(2,1)S(1)}, u32[]{:S(2)}, u32[]{:S(2)}) %collective-permute-start.11) | collective-permute-done | bytes 262176 | tf_op jit(solution)/shard_map/ppermute | solution.py:26
  136.9 8.9 %collective-permute-done.17 = bf16[64,2048]{1,0:T(8,128)(2,1)S(1)} collective-permute-done((bf16[64,2048]{1,0:T(8,128)(2,1)S(1)}, bf16[64,2048]{1,0:T(8,128)(2,1)S(1)}, u32[]{:S(2)}, u32[]{:S(2)}) %collective-permute-start.17) | collective-permute-done | bytes 262176 | tf_op jit(solution)/shard_map/ppermute | solution.py:26
  145.8 1.1 fusion.8
  147.7 1.2 collective-permute-done.24
  150.3 2.0 %collective-permute-start.33 = (bf16[128,512]{1,0:T(8,128)(2,1)S(1)}, bf16[128,512]{1,0:T(8,128)(2,1)S(1)}, u32[]{:S(2)}, u32[]{:S(2)}) collective-permute-start(bf16[128,512]{1,0:T(8,128)(2,1)S(1)} %pad_maximum_fusion.9), channel_id=1, source_target_pairs={{0,24},{1,25},{2,26},{3,27},{4,28},{5,29},{6,30},{7,31},{8,16},{9,... | collective-permute-start | bytes 393224 | tf_op jit(solution)/shard_map/ppermute | solution.py:26
  152.2 2.9 %collective-permute-start.30 = (bf16[128,512]{1,0:T(8,128)(2,1)S(1)}, bf16[128,512]{1,0:T(8,128)(2,1)S(1)}, u32[]{:S(2)}, u32[]{:S(2)}) collective-permute-start(bf16[128,512]{1,0:T(8,128)(2,1)S(1)} %pad_maximum_fusion.9), channel_id=1, source_target_pairs={{0,16},{1,17},{2,18},{3,19},{4,20},{5,21},{6,22},{7,23},{8,24},{9,... | collective-permute-start | bytes 393224 | tf_op jit(solution)/shard_map/ppermute | solution.py:26
  155.5 4.7 %fusion.12 = f32[128,2048]{1,0:T(8,128)S(1)} fusion(bf16[2048,2048]{1,0:T(8,128)(2,1)} %param.24, f32[128,2048]{1,0:T(8,128)S(1)} %get-tuple-element.19, f32[2048]{0:T(1024)S(1)} %copy-done.4, f32[128]{0:T(128)S(1)} %add_rsqrt_fusion.2), kind=kOutput, calls=%fused_computation.73 | convolution fusion | flops 1074528256 | bytes 10494464 | tf_op jit(solution)/shard_map/dot_general | solution.py:298
  161.1 2.5 %collective-permute-start.26 = (bf16[256,512]{1,0:T(8,128)(2,1)S(1)}, bf16[256,512]{1,0:T(8,128)(2,1)S(1)}, u32[]{:S(2)}, u32[]{:S(2)}) collective-permute-start(bf16[256,512]{1,0:T(8,128)(2,1)S(1)} %pad_maximum_fusion.8.refs_0_), channel_id=1, source_target_pairs={{0,4},{1,3},{2,6},{3,1},{4,0},{5,7},{6,2},{7,5},{8,12},{9,11},{10,... | collective-permute-start | bytes 786440 | tf_op jit(solution)/shard_map/ppermute | solution.py:26
  163.6 0.6 collective-permute-start.34
  164.2 1.8 collective-permute-done.30
  166.2 2.1 %collective-permute-start.28 = (bf16[128,512]{1,0:T(8,128)(2,1)S(1)}, bf16[128,512]{1,0:T(8,128)(2,1)S(1)}, u32[]{:S(2)}, u32[]{:S(2)}) collective-permute-start(bf16[128,512]{1,0:T(8,128)(2,1)S(1)} %collective-permute-done.27), channel_id=1, source_target_pairs={{0,2},{1,5},{2,0},{3,7},{4,6},{5,1},{6,4},{7,3},{8,10},{9,13},{10,... | collective-permute-start | bytes 393224 | tf_op jit(solution)/shard_map/ppermute | solution.py:26
  169.2 2.2 %collective-permute-done.31 = bf16[128,512]{1,0:T(8,128)(2,1)S(1)} collective-permute-done((bf16[128,512]{1,0:T(8,128)(2,1)S(1)}, bf16[128,512]{1,0:T(8,128)(2,1)S(1)}, u32[]{:S(2)}, u32[]{:S(2)}) %collective-permute-start.31) | collective-permute-done | bytes 131104 | tf_op jit(solution)/shard_map/ppermute | solution.py:26
  171.4 1.1 collective-permute-start.32
  172.5 1.7 collective-permute-done.28
  174.2 1.1 collective-permute-start.29
  176.1 1.8 collective-permute-done.32.refs_5_
  177.9 2.8 %collective-permute-done.29.refs_3_ = bf16[256,512]{1,0:T(8,128)(2,1)S(1)} collective-permute-done((bf16[256,512]{1,0:T(8,128)(2,1)S(1)}, bf16[256,512]{1,0:T(8,128)(2,1)S(1)}, u32[]{:S(2)}, u32[]{:S(2)}) %collective-permute-start.29) | collective-permute-done | bytes 262176 | tf_op jit(solution)/shard_map/ppermute | solution.py:26
  180.7 9.1 %attention.1 = bf16[128,2048]{1,0:T(8,128)(2,1)} custom-call(bf16[128,2048]{1,0:T(8,128)(2,1)S(1)} %fusion.1.q_ref, bf16[256,512]{1,0:T(8,128)(2,1)S(1)} %pad_maximum_fusion.8.refs_0_, bf16[256,512]{1,0:T(8,128)(2,1)S(1)} %collective-permute-done.26.refs_1_, bf16[256,512]{1,0:T(8,128)(2,1)S(1)} %constant_dynamic-update-slice_fusion.refs_2_, ...), custom_call_target="tpu_custom_call" | custom-call | flops 2147483648 | bytes 1048576 | tf_op jit(solution)/shard_map/attention/pallas_call | solution.py:200
  (104 shorter events, 7.4 us)
Async XLA Ops:
  0.6 147.1 %copy-start = (f32[128]{0:T(128)S(1)}, f32[128]{0:T(128)}, u32[]{:S(2)}) copy-start(f32[128]{0:T(128)} %param.26) | copy-start | bytes 1540
  0.6 6.9 %copy-start.7 = (s32[128,8]{0,1:T(8,128)S(1)}, s32[128,8]{0,1:T(8,128)}, u32[]{:S(2)}) copy-start(s32[128,8]{0,1:T(8,128)} %param.19) | copy-start | bytes 12292
  0.7 6.9 %copy-start.6 = (f32[128,8]{0,1:T(8,128)S(1)}, f32[128,8]{0,1:T(8,128)}, u32[]{:S(2)}) copy-start(f32[128,8]{0,1:T(8,128)} %param.20) | copy-start | bytes 12292
  0.7 16.8 %copy-start.1 = (bf16[2,384,2048]{2,1,0:T(8,128)(2,1)S(1)}, bf16[2,384,2048]{2,1,0:T(8,128)(2,1)}, u32[]{:S(2)}) copy-start(bf16[2,384,2048]{2,1,0:T(8,128)(2,1)} %own_down.7) | copy-start | bytes 9437188
  7.1 10.4 %copy-start.8 = (s32[4]{0:T(128)S(1)}, s32[4]{0:T(128)}, u32[]{:S(2)}) copy-start(s32[4]{0:T(128)} %constant.52.clone) | copy-start | bytes 52
  7.1 10.5 %copy-start.5 = (s32[2048]{0:T(1024)S(1)}, s32[2048]{0:T(1024)}, u32[]{:S(2)}) copy-start(s32[2048]{0:T(1024)} %param.18) | copy-start | bytes 24580
  7.1 59.5 %collective-permute-start.2 = (bf16[2,2,2048,384]{3,2,1,0:T(8,128)(2,1)}, bf16[2,2,2048,384]{3,2,1,0:T(8,128)(2,1)}, u32[]{:S(2)}, u32[]{:S(2)}) collective-permute-start(bf16[2,2,2048,384]{3,2,1,0:T(8,128)(2,1)} %bitcast.28.own_gu), channel_id=1, source_target_pairs={{0,1},{1,0},{2,3},{3,2},{4,5},{5,4},{6,7},{7,6},{8,9},{9,8},{10,11... | collective-permute-start | bytes 18874376 | tf_op jit(solution)/shard_map/ppermute | solution.py:30
  10.7 15.9 %collective-permute-start.6 = (bf16[64,2176]{1,0:T(8,128)(2,1)S(1)}, bf16[64,2176]{1,0:T(8,128)(2,1)}, u32[]{:S(2)}, u32[]{:S(2)}) collective-permute-start(bf16[64,2176]{1,0:T(8,128)(2,1)S(1)} %constant_dynamic-slice_fusion), channel_id=1, source_target_pairs={{0,8},{1,9},{2,10},{3,11},{4,12},{5,13},{6,14},{7,15},{8,0},{9,1},... | collective-permute-start | bytes 835592 | tf_op jit(solution)/shard_map/ppermute | solution.py:26
  13.4 18.4 %collective-permute-start.12 = (bf16[64,2176]{1,0:T(8,128)(2,1)S(1)}, bf16[64,2176]{1,0:T(8,128)(2,1)}, u32[]{:S(2)}, u32[]{:S(2)}) collective-permute-start(bf16[64,2176]{1,0:T(8,128)(2,1)S(1)} %constant_dynamic-slice_fusion), channel_id=1, source_target_pairs={{0,16},{1,17},{2,18},{3,19},{4,20},{5,21},{6,22},{7,23},{8,24},{9,... | collective-permute-start | bytes 835592 | tf_op jit(solution)/shard_map/ppermute | solution.py:26
  16.0 13.3 %collective-permute-start = (bf16[64,2176]{1,0:T(8,128)(2,1)S(1)}, bf16[64,2176]{1,0:T(8,128)(2,1)}, u32[]{:S(2)}, u32[]{:S(2)}) collective-permute-start(bf16[64,2176]{1,0:T(8,128)(2,1)S(1)} %constant_dynamic-slice_fusion), channel_id=1, source_target_pairs={{0,2},{1,5},{2,0},{3,7},{4,6},{5,1},{6,4},{7,3},{8,10},{9,13},{10,... | collective-permute-start | bytes 835592 | tf_op jit(solution)/shard_map/ppermute | solution.py:26
  17.5 49.1 %collective-permute-start.3 = (bf16[2,384,2048]{2,1,0:T(8,128)(2,1)S(1)}, bf16[2,384,2048]{2,1,0:T(8,128)(2,1)}, u32[]{:S(2)}, u32[]{:S(2)}) collective-permute-start(bf16[2,384,2048]{2,1,0:T(8,128)(2,1)S(1)} %copy-done.1), channel_id=1, source_target_pairs={{0,1},{1,0},{2,3},{3,2},{4,5},{5,4},{6,7},{7,6},{8,9},{9,8},{10,11... | collective-permute-start | bytes 9437192 | tf_op jit(solution)/shard_map/ppermute | solution.py:30
  26.7 10.4 %collective-permute-start.18 = (bf16[64,2176]{1,0:T(8,128)(2,1)S(1)}, bf16[64,2176]{1,0:T(8,128)(2,1)S(1)}, u32[]{:S(2)}, u32[]{:S(2)}) collective-permute-start(bf16[64,2176]{1,0:T(8,128)(2,1)S(1)} %constant_dynamic-slice_fusion), channel_id=1, source_target_pairs={{0,24},{1,25},{2,26},{3,27},{4,28},{5,29},{6,30},{7,31},{8,16},{9,... | collective-permute-start | bytes 835592 | tf_op jit(solution)/shard_map/ppermute | solution.py:26
  29.3 9.2 %collective-permute-start.7 = (bf16[64,2176]{1,0:T(8,128)(2,1)}, bf16[64,2176]{1,0:T(8,128)(2,1)S(1)}, u32[]{:S(2)}, u32[]{:S(2)}) collective-permute-start(bf16[64,2176]{1,0:T(8,128)(2,1)} %collective-permute-done.6), channel_id=1, source_target_pairs={{0,2},{1,5},{2,0},{3,7},{4,6},{5,1},{6,4},{7,3},{8,10},{9,13},{10,... | collective-permute-start | bytes 835592 | tf_op jit(solution)/shard_map/ppermute | solution.py:26
  31.8 17.7 %collective-permute-start.1 = (bf16[128,2176]{1,0:T(8,128)(2,1)S(1)}, bf16[128,2176]{1,0:T(8,128)(2,1)S(1)}, u32[]{:S(2)}, u32[]{:S(2)}) collective-permute-start(bf16[128,2176]{1,0:T(8,128)(2,1)S(1)} %pad_maximum_fusion.4), channel_id=1, source_target_pairs={{0,4},{1,3},{2,6},{3,1},{4,0},{5,7},{6,2},{7,5},{8,12},{9,11},{10,... | collective-permute-start | bytes 1671176 | tf_op jit(solution)/shard_map/ppermute | solution.py:26
  37.0 8.0 %collective-permute-start.13 = (bf16[64,2176]{1,0:T(8,128)(2,1)}, bf16[64,2176]{1,0:T(8,128)(2,1)S(1)}, u32[]{:S(2)}, u32[]{:S(2)}) collective-permute-start(bf16[64,2176]{1,0:T(8,128)(2,1)} %collective-permute-done.12), channel_id=1, source_target_pairs={{0,2},{1,5},{2,0},{3,7},{4,6},{5,1},{6,4},{7,3},{8,10},{9,13},{10,... | collective-permute-start | bytes 835592 | tf_op jit(solution)/shard_map/ppermute | solution.py:26
  38.6 10.3 %collective-permute-start.19 = (bf16[64,2176]{1,0:T(8,128)(2,1)S(1)}, bf16[64,2176]{1,0:T(8,128)(2,1)S(1)}, u32[]{:S(2)}, u32[]{:S(2)}) collective-permute-start(bf16[64,2176]{1,0:T(8,128)(2,1)S(1)} %collective-permute-done.18), channel_id=1, source_target_pairs={{0,2},{1,5},{2,0},{3,7},{4,6},{5,1},{6,4},{7,3},{8,10},{9,13},{10,... | collective-permute-start | bytes 835592 | tf_op jit(solution)/shard_map/ppermute | solution.py:26
  45.0 9.5 %collective-permute-start.8 = (bf16[128,2176]{1,0:T(8,128)(2,1)S(1)}, bf16[128,2176]{1,0:T(8,128)(2,1)S(1)}, u32[]{:S(2)}, u32[]{:S(2)}) collective-permute-start(bf16[128,2176]{1,0:T(8,128)(2,1)S(1)} %pad_maximum_fusion.5), channel_id=1, source_target_pairs={{0,4},{1,3},{2,6},{3,1},{4,0},{5,7},{6,2},{7,5},{8,12},{9,11},{10,... | collective-permute-start | bytes 1671176 | tf_op jit(solution)/shard_map/ppermute | solution.py:26
  48.8 11.7 %collective-permute-start.14 = (bf16[128,2176]{1,0:T(8,128)(2,1)S(1)}, bf16[128,2176]{1,0:T(8,128)(2,1)S(1)}, u32[]{:S(2)}, u32[]{:S(2)}) collective-permute-start(bf16[128,2176]{1,0:T(8,128)(2,1)S(1)} %pad_maximum_fusion.6), channel_id=1, source_target_pairs={{0,4},{1,3},{2,6},{3,1},{4,0},{5,7},{6,2},{7,5},{8,12},{9,11},{10,... | collective-permute-start | bytes 1671176 | tf_op jit(solution)/shard_map/ppermute | solution.py:26
  49.5 17.0 %collective-permute-start.20 = (bf16[128,2176]{1,0:T(8,128)(2,1)S(1)}, bf16[128,2176]{1,0:T(8,128)(2,1)S(1)}, u32[]{:S(2)}, u32[]{:S(2)}) collective-permute-start(bf16[128,2176]{1,0:T(8,128)(2,1)S(1)} %pad_maximum_fusion.7), channel_id=1, source_target_pairs={{0,4},{1,3},{2,6},{3,1},{4,0},{5,7},{6,2},{7,5},{8,12},{9,11},{10,... | collective-permute-start | bytes 1671176 | tf_op jit(solution)/shard_map/ppermute | solution.py:26
  76.0 32.8 %collective-permute-start.9 = (bf16[128,2048]{1,0:T(8,128)(2,1)S(1)}, bf16[128,2048]{1,0:T(8,128)(2,1)S(1)}, u32[]{:S(2)}, u32[]{:S(2)}) collective-permute-start(bf16[128,2048]{1,0:T(8,128)(2,1)S(1)} %get-tuple-element.13), channel_id=1, source_target_pairs={{0,4},{1,3},{2,6},{3,1},{4,0},{5,7},{6,2},{7,5},{8,12},{9,11},{10,... | collective-permute-start | bytes 1572872 | tf_op jit(solution)/shard_map/ppermute | solution.py:26
  86.6 23.9 %collective-permute-start.15 = (bf16[128,2048]{1,0:T(8,128)(2,1)S(1)}, bf16[128,2048]{1,0:T(8,128)(2,1)S(1)}, u32[]{:S(2)}, u32[]{:S(2)}) collective-permute-start(bf16[128,2048]{1,0:T(8,128)(2,1)S(1)} %get-tuple-element.15), channel_id=1, source_target_pairs={{0,4},{1,3},{2,6},{3,1},{4,0},{5,7},{6,2},{7,5},{8,12},{9,11},{10,... | collective-permute-start | bytes 1572872 | tf_op jit(solution)/shard_map/ppermute | solution.py:26
  97.0 14.3 %collective-permute-start.21 = (bf16[128,2048]{1,0:T(8,128)(2,1)S(1)}, bf16[128,2048]{1,0:T(8,128)(2,1)S(1)}, u32[]{:S(2)}, u32[]{:S(2)}) collective-permute-start(bf16[128,2048]{1,0:T(8,128)(2,1)S(1)} %get-tuple-element.17), channel_id=1, source_target_pairs={{0,4},{1,3},{2,6},{3,1},{4,0},{5,7},{6,2},{7,5},{8,12},{9,11},{10,... | collective-permute-start | bytes 1572872 | tf_op jit(solution)/shard_map/ppermute | solution.py:26
  107.8 14.9 %collective-permute-start.4 = (bf16[128,2048]{1,0:T(8,128)(2,1)S(1)}, bf16[128,2048]{1,0:T(8,128)(2,1)S(1)}, u32[]{:S(2)}, u32[]{:S(2)}) collective-permute-start(bf16[128,2048]{1,0:T(8,128)(2,1)S(1)} %get-tuple-element.11), channel_id=1, source_target_pairs={{0,4},{1,3},{2,6},{3,1},{4,0},{5,7},{6,2},{7,5},{8,12},{9,11},{10,... | collective-permute-start | bytes 1572872 | tf_op jit(solution)/shard_map/ppermute | solution.py:26
  109.0 15.4 %collective-permute-start.10 = (bf16[64,2048]{1,0:T(8,128)(2,1)S(1)}, bf16[64,2048]{1,0:T(8,128)(2,1)S(1)}, u32[]{:S(2)}, u32[]{:S(2)}) collective-permute-start(bf16[64,2048]{1,0:T(8,128)(2,1)S(1)} %slice.100), channel_id=1, source_target_pairs={{0,2},{1,5},{2,0},{3,7},{4,6},{5,1},{6,4},{7,3},{8,10},{9,13},{10,... | collective-permute-start | bytes 786440 | tf_op jit(solution)/shard_map/ppermute | solution.py:26
  110.7 17.7 %collective-permute-start.16 = (bf16[64,2048]{1,0:T(8,128)(2,1)S(1)}, bf16[64,2048]{1,0:T(8,128)(2,1)S(1)}, u32[]{:S(2)}, u32[]{:S(2)}) collective-permute-start(bf16[64,2048]{1,0:T(8,128)(2,1)S(1)} %slice.99), channel_id=1, source_target_pairs={{0,2},{1,5},{2,0},{3,7},{4,6},{5,1},{6,4},{7,3},{8,10},{9,13},{10,... | collective-permute-start | bytes 786440 | tf_op jit(solution)/shard_map/ppermute | solution.py:26
  111.4 18.1 %collective-permute-start.22 = (bf16[64,2048]{1,0:T(8,128)(2,1)S(1)}, bf16[64,2048]{1,0:T(8,128)(2,1)S(1)}, u32[]{:S(2)}, u32[]{:S(2)}) collective-permute-start(bf16[64,2048]{1,0:T(8,128)(2,1)S(1)} %slice.98), channel_id=1, source_target_pairs={{0,2},{1,5},{2,0},{3,7},{4,6},{5,1},{6,4},{7,3},{8,10},{9,13},{10,... | collective-permute-start | bytes 786440 | tf_op jit(solution)/shard_map/ppermute | solution.py:26
  122.9 8.2 %collective-permute-start.5 = (bf16[64,2048]{1,0:T(8,128)(2,1)S(1)}, bf16[64,2048]{1,0:T(8,128)(2,1)S(1)}, u32[]{:S(2)}, u32[]{:S(2)}) collective-permute-start(bf16[64,2048]{1,0:T(8,128)(2,1)S(1)} %slice.101), channel_id=1, source_target_pairs={{0,2},{1,5},{2,0},{3,7},{4,6},{5,1},{6,4},{7,3},{8,10},{9,13},{10,... | collective-permute-start | bytes 786440 | tf_op jit(solution)/shard_map/ppermute | solution.py:26
  124.5 22.6 %copy-start.3 = (bf16[2048,2,256]{2,1,0:T(2,128)(2,1)S(1)}, bf16[2048,2,256]{2,1,0:T(2,128)(2,1)}, u32[]{:S(2)}) copy-start(bf16[2048,2,256]{2,1,0:T(2,128)(2,1)} %param.25) | copy-start | bytes 6291460
  124.5 12.4 %collective-permute-start.11 = (bf16[64,2048]{1,0:T(8,128)(2,1)S(1)}, bf16[64,2048]{1,0:T(8,128)(2,1)S(1)}, u32[]{:S(2)}, u32[]{:S(2)}) collective-permute-start(bf16[64,2048]{1,0:T(8,128)(2,1)S(1)} %fusion.4), channel_id=1, source_target_pairs={{0,8},{1,9},{2,10},{3,11},{4,12},{5,13},{6,14},{7,15},{8,0},{9,1},... | collective-permute-start | bytes 786440 | tf_op jit(solution)/shard_map/ppermute | solution.py:26
  128.4 17.4 %collective-permute-start.17 = (bf16[64,2048]{1,0:T(8,128)(2,1)S(1)}, bf16[64,2048]{1,0:T(8,128)(2,1)S(1)}, u32[]{:S(2)}, u32[]{:S(2)}) collective-permute-start(bf16[64,2048]{1,0:T(8,128)(2,1)S(1)} %fusion.3), channel_id=1, source_target_pairs={{0,16},{1,17},{2,18},{3,19},{4,20},{5,21},{6,22},{7,23},{8,24},{9,... | collective-permute-start | bytes 786440 | tf_op jit(solution)/shard_map/ppermute | solution.py:26
  129.6 16.3 %collective-permute-start.23 = (bf16[64,2048]{1,0:T(8,128)(2,1)S(1)}, bf16[64,2048]{1,0:T(8,128)(2,1)S(1)}, u32[]{:S(2)}, u32[]{:S(2)}) collective-permute-start(bf16[64,2048]{1,0:T(8,128)(2,1)S(1)} %fusion.2), channel_id=1, source_target_pairs={{0,24},{1,25},{2,26},{3,27},{4,28},{5,29},{6,30},{7,31},{8,16},{9,... | collective-permute-start | bytes 786440 | tf_op jit(solution)/shard_map/ppermute | solution.py:26
  147.0 2.0 %collective-permute-start.24 = (f32[64,2048]{1,0:T(8,128)S(1)}, f32[64,2048]{1,0:T(8,128)S(1)}, u32[]{:S(2)}, u32[]{:S(2)}) collective-permute-start(f32[64,2048]{1,0:T(8,128)S(1)} %fusion.8), channel_id=1, source_target_pairs={{0,1},{1,0},{2,3},{3,2},{4,5},{5,4},{6,7},{7,6},{8,9},{9,8},{10,11... | collective-permute-start | bytes 1572872 | tf_op jit(solution)/shard_map/ppermute | solution.py:30
  147.1 0.7 copy-start.9
  147.7 1.4 copy-start.4
  149.1 6.4 %copy-start.2 = (f32[128,2048]{1,0:T(8,128)}, f32[128,2048]{1,0:T(8,128)S(1)}, u32[]{:S(2)}) copy-start(f32[128,2048]{1,0:T(8,128)S(1)} %get-tuple-element.19) | copy-start | bytes 3145732
  150.3 13.4 %collective-permute-start.33 = (bf16[128,512]{1,0:T(8,128)(2,1)S(1)}, bf16[128,512]{1,0:T(8,128)(2,1)S(1)}, u32[]{:S(2)}, u32[]{:S(2)}) collective-permute-start(bf16[128,512]{1,0:T(8,128)(2,1)S(1)} %pad_maximum_fusion.9), channel_id=1, source_target_pairs={{0,24},{1,25},{2,26},{3,27},{4,28},{5,29},{6,30},{7,31},{8,16},{9,... | collective-permute-start | bytes 393224 | tf_op jit(solution)/shard_map/ppermute | solution.py:26
  152.2 13.8 %collective-permute-start.30 = (bf16[128,512]{1,0:T(8,128)(2,1)S(1)}, bf16[128,512]{1,0:T(8,128)(2,1)S(1)}, u32[]{:S(2)}, u32[]{:S(2)}) collective-permute-start(bf16[128,512]{1,0:T(8,128)(2,1)S(1)} %pad_maximum_fusion.9), channel_id=1, source_target_pairs={{0,16},{1,17},{2,18},{3,19},{4,20},{5,21},{6,22},{7,23},{8,24},{9,... | collective-permute-start | bytes 393224 | tf_op jit(solution)/shard_map/ppermute | solution.py:26
  155.2 11.0 %collective-permute-start.27 = (bf16[128,512]{1,0:T(8,128)(2,1)S(1)}, bf16[128,512]{1,0:T(8,128)(2,1)S(1)}, u32[]{:S(2)}, u32[]{:S(2)}) collective-permute-start(bf16[128,512]{1,0:T(8,128)(2,1)S(1)} %pad_maximum_fusion.9), channel_id=1, source_target_pairs={{0,8},{1,9},{2,10},{3,11},{4,12},{5,13},{6,14},{7,15},{8,0},{9,1},... | collective-permute-start | bytes 393224 | tf_op jit(solution)/shard_map/ppermute | solution.py:26
  155.3 5.7 %collective-permute-start.25 = (bf16[128,512]{1,0:T(8,128)(2,1)S(1)}, bf16[128,512]{1,0:T(8,128)(2,1)S(1)}, u32[]{:S(2)}, u32[]{:S(2)}) collective-permute-start(bf16[128,512]{1,0:T(8,128)(2,1)S(1)} %pad_maximum_fusion.9), channel_id=1, source_target_pairs={{0,2},{1,5},{2,0},{3,7},{4,6},{5,1},{6,4},{7,3},{8,10},{9,13},{10,... | collective-permute-start | bytes 393224 | tf_op jit(solution)/shard_map/ppermute | solution.py:26
  161.1 15.0 %collective-permute-start.26 = (bf16[256,512]{1,0:T(8,128)(2,1)S(1)}, bf16[256,512]{1,0:T(8,128)(2,1)S(1)}, u32[]{:S(2)}, u32[]{:S(2)}) collective-permute-start(bf16[256,512]{1,0:T(8,128)(2,1)S(1)} %pad_maximum_fusion.8.refs_0_), channel_id=1, source_target_pairs={{0,4},{1,3},{2,6},{3,1},{4,0},{5,7},{6,2},{7,5},{8,12},{9,11},{10,... | collective-permute-start | bytes 786440 | tf_op jit(solution)/shard_map/ppermute | solution.py:26
  163.6 5.0 %collective-permute-start.34 = (bf16[128,512]{1,0:T(8,128)(2,1)S(1)}, bf16[128,512]{1,0:T(8,128)(2,1)S(1)}, u32[]{:S(2)}, u32[]{:S(2)}) collective-permute-start(bf16[128,512]{1,0:T(8,128)(2,1)S(1)} %collective-permute-done.33), channel_id=1, source_target_pairs={{0,2},{1,5},{2,0},{3,7},{4,6},{5,1},{6,4},{7,3},{8,10},{9,13},{10,... | collective-permute-start | bytes 393224 | tf_op jit(solution)/shard_map/ppermute | solution.py:26
  166.1 5.2 %collective-permute-start.31 = (bf16[128,512]{1,0:T(8,128)(2,1)S(1)}, bf16[128,512]{1,0:T(8,128)(2,1)S(1)}, u32[]{:S(2)}, u32[]{:S(2)}) collective-permute-start(bf16[128,512]{1,0:T(8,128)(2,1)S(1)} %collective-permute-done.30), channel_id=1, source_target_pairs={{0,2},{1,5},{2,0},{3,7},{4,6},{5,1},{6,4},{7,3},{8,10},{9,13},{10,... | collective-permute-start | bytes 393224 | tf_op jit(solution)/shard_map/ppermute | solution.py:26
  166.2 7.9 %collective-permute-start.28 = (bf16[128,512]{1,0:T(8,128)(2,1)S(1)}, bf16[128,512]{1,0:T(8,128)(2,1)S(1)}, u32[]{:S(2)}, u32[]{:S(2)}) collective-permute-start(bf16[128,512]{1,0:T(8,128)(2,1)S(1)} %collective-permute-done.27), channel_id=1, source_target_pairs={{0,2},{1,5},{2,0},{3,7},{4,6},{5,1},{6,4},{7,3},{8,10},{9,13},{10,... | collective-permute-start | bytes 393224 | tf_op jit(solution)/shard_map/ppermute | solution.py:26
  168.7 7.4 %collective-permute-start.35 = (bf16[256,512]{1,0:T(8,128)(2,1)S(1)}, bf16[256,512]{1,0:T(8,128)(2,1)S(1)}, u32[]{:S(2)}, u32[]{:S(2)}) collective-permute-start(bf16[256,512]{1,0:T(8,128)(2,1)S(1)} %constant_dynamic-update-slice_fusion.4.refs_6_), channel_id=1, source_target_pairs={{0,4},{1,3},{2,6},{3,1},{4,0},{5,7},{6,2},{7,5},{8,12},{9,11},{10,... | collective-permute-start | bytes 786440 | tf_op jit(solution)/shard_map/ppermute | solution.py:26
  171.4 6.6 %collective-permute-start.32 = (bf16[256,512]{1,0:T(8,128)(2,1)S(1)}, bf16[256,512]{1,0:T(8,128)(2,1)S(1)}, u32[]{:S(2)}, u32[]{:S(2)}) collective-permute-start(bf16[256,512]{1,0:T(8,128)(2,1)S(1)} %constant_dynamic-update-slice_fusion.2.refs_4_), channel_id=1, source_target_pairs={{0,4},{1,3},{2,6},{3,1},{4,0},{5,7},{6,2},{7,5},{8,12},{9,11},{10,... | collective-permute-start | bytes 786440 | tf_op jit(solution)/shard_map/ppermute | solution.py:26
  174.2 6.6 %collective-permute-start.29 = (bf16[256,512]{1,0:T(8,128)(2,1)S(1)}, bf16[256,512]{1,0:T(8,128)(2,1)S(1)}, u32[]{:S(2)}, u32[]{:S(2)}) collective-permute-start(bf16[256,512]{1,0:T(8,128)(2,1)S(1)} %constant_dynamic-update-slice_fusion.refs_2_), channel_id=1, source_target_pairs={{0,4},{1,3},{2,6},{3,1},{4,0},{5,7},{6,2},{7,5},{8,12},{9,11},{10,... | collective-permute-start | bytes 786440 | tf_op jit(solution)/shard_map/ppermute | solution.py:26

commit v2 on v1

v2 whole, which is shorter than its diff:
```python
import functools

import jax
import jax.numpy as jnp
from jax import lax
from jax.experimental import pallas as pl
from jax.experimental.pallas import tpu as pltpu
from jax.sharding import PartitionSpec as P

EPSILON = 1e-06
LANES = 128
KEYS_AT_ONCE = 2048
MIB = 1024 * 1024


def rms_scale(values, gain_row):
    mean_sq = jnp.mean(values * values, axis=-1, keepdims=True)
    return values * lax.rsqrt(mean_sq + EPSILON) * gain_row


def swap(value, mask_first, mask_second):
    pairs = []
    for expert in range(lax.axis_size("expert")):
        for half, mask in enumerate((mask_first, mask_second)):
            pairs.append((2 * expert + half, 2 * (expert ^ mask) + half))
    return lax.ppermute(value, ("expert", "half"), pairs)


def after(value, earlier):
    return lax.optimization_barrier((value, earlier))[0]


def swap_half(value):
    return lax.ppermute(value, "half", [(0, 1), (1, 0)])


def payload_kernel(groups, core_ref, hidden_ref, ids_ref, weights_ref, out_ref, table_ref):
    rows, width = hidden_ref.shape
    tokens = ids_ref.shape[1]
    row = lax.broadcasted_iota(jnp.int32, (LANES, tokens), 0)
    expert = jnp.where(row < groups, row, row - groups)
    table = jnp.zeros((LANES, tokens), jnp.float32)
    for j in range(ids_ref.shape[0]):
        table += jnp.where(ids_ref[j : j + 1] == expert, weights_ref[j : j + 1], 0.0)
    high = table.astype(jnp.bfloat16).astype(jnp.float32)
    extra = jnp.where(row < groups, high, jnp.where(row < 2 * groups, table - high, 0.0))
    table_ref[...] = extra.T
    mine = pl.ds(pl.multiple_of(core_ref[0] * rows, rows), rows)
    out_ref[:, :width] = hidden_ref[...]
    out_ref[:, width:] = table_ref[mine].astype(jnp.bfloat16)


def payload_call(core, hidden_in, expert_ids, route_weights, groups):
    tok_rows, width = hidden_in.shape
    rows = tok_rows // 2
    top = expert_ids.shape[1]
    return pl.pallas_call(
        functools.partial(payload_kernel, groups),
        out_shape=jax.ShapeDtypeStruct((rows, width + LANES), jnp.bfloat16),
        grid_spec=pltpu.PrefetchScalarGridSpec(
            num_scalar_prefetch=1,
            grid=(1,),
            in_specs=[
                pl.BlockSpec((rows, width), lambda i, core: (core[0], 0)),
                pl.BlockSpec((top, tok_rows), lambda i, core: (0, 0)),
                pl.BlockSpec((top, tok_rows), lambda i, core: (0, 0)),
            ],
            out_specs=pl.BlockSpec((rows, width + LANES), lambda i, core: (0, 0)),
            scratch_shapes=[pltpu.VMEM((tok_rows, LANES), jnp.float32)],
        ),
        name="payload",
    )(core, hidden_in, expert_ids.T, route_weights.T)


def expert_kernel(slots, units, place_ref, kind_ref, pick_ref, *refs):
    count = len(slots)
    x_refs, refs = refs[: 2 * count], refs[2 * count :]
    own_gu, other_gu, own_down, other_down = refs[:4]
    out_refs, refs = refs[4 : 4 + 2 * len(units)], refs[4 + 2 * len(units) :]
    gu_ref, down_ref, sorted_ref, act_ref, done_ref, sems = refs
    hidden_units, width = own_down.shape[1:]
    rows = x_refs[0].shape[0] // 2
    me, core = place_ref[0], place_ref[1]

    near = (0, 1 + core, 2 - core, 3)
    blocks = [(i, p) for i in range(count) for p in range(4)]
    kinds = [kind_ref[me ^ (4 * slots[i]) ^ near[p]] for i, p in blocks]
    images = functools.reduce(lambda a, b: a + b, kinds)
    first = (2 * images > len(blocks)).astype(jnp.int32)
    first_count = jnp.where(first == 1, images, len(blocks) - images)
    second_count = len(blocks) - first_count

    def copies(buffer, kind):
        found = []
        for k, gu in enumerate((own_gu, other_gu)):
            for c in range(2):
                at = pl.ds(c * hidden_units, hidden_units)
                found.append((gu.at[kind, c], gu_ref.at[buffer, k, :, at], sems.at[buffer, k, c]))
        for k, down in enumerate((own_down, other_down)):
            at = pl.ds(k * hidden_units, hidden_units)
            found.append((down.at[kind], down_ref.at[buffer, at], sems.at[buffer, k, 2]))
        return [pltpu.make_async_copy(*parts) for parts in found]

    for copy in copies(0, first):
        copy.start()

    @pl.when(second_count > 0)
    def _():
        for copy in copies(1, 1 - first):
            copy.start()

    offsets = []
    seen_first, seen_second = 0, first_count
    for kind in kinds:
        is_first = (kind == first).astype(jnp.int32)
        offsets.append(pl.multiple_of(jnp.where(is_first == 1, seen_first, seen_second) * rows, rows))
        seen_first, seen_second = seen_first + is_first, seen_second + 1 - is_first
    for (i, p), offset in zip(blocks, offsets):
        source = x_refs[2 * i + p // 2]
        sorted_ref[pl.ds(offset, rows)] = source[(p % 2) * rows : (p % 2 + 1) * rows]

    def rows_of(block, number):
        return pl.ds(pl.multiple_of(block * rows, rows), number * rows)

    def activate(buffer, k, block, number):
        at = rows_of(block, number)
        pre = jnp.dot(sorted_ref[at, :width], gu_ref[buffer, k], preferred_element_type=jnp.float32)
        gate, up = pre[:, :hidden_units], pre[:, hidden_units:]
        act = gate / (1.0 + jnp.exp(-gate)) * up
        act_ref[at, k * hidden_units : (k + 1) * hidden_units] = act.astype(jnp.bfloat16)

    def finish(buffer, block, number):
        at = rows_of(block, number)
        extra = sorted_ref[at, width:].astype(jnp.float32)
        weight = jnp.sum(extra * pick_ref[...], axis=-1, keepdims=True)
        out = jnp.dot(act_ref[at], down_ref[buffer], preferred_element_type=jnp.float32)
        done_ref[at] = out.astype(jnp.bfloat16).astype(jnp.float32) * weight

    def over_blocks(step, start, number):
        rest = lax.rem(number, 4)
        wholes = number // 4 + (rest == 3).astype(jnp.int32)

        def whole(at, carry):
            step(start + 4 * at, 4)
            return carry

        lax.fori_loop(0, wholes, whole, 0)

        @pl.when((rest == 1) | (rest == 2))
        def _():
            step(start + 4 * wholes, 2)

    def expert(buffer, kind, start, number):
        found = copies(buffer, kind)
        for k in range(2):
            for copy in found[2 * k : 2 * k + 2]:
                copy.wait()
            over_blocks(functools.partial(activate, buffer, k), start, number)
        for copy in found[4:]:
            copy.wait()
        over_blocks(functools.partial(finish, buffer), start, number)

    expert(0, first, 0, first_count)

    @pl.when(second_count > 0)
    def _():
        expert(1, 1 - first, first_count, second_count)

    for (i, p), offset in zip(blocks, offsets):
        for u, unit in enumerate(units):
            if slots[i] in unit:
                row = ((p % 2) * len(unit) + unit.index(slots[i])) * rows
                target = out_refs[2 * u + p // 2]
                target[row : row + rows] = done_ref[pl.ds(offset, rows)].astype(target.dtype)


def expert_call(slots, units, place, kinds, pick, parts, weights):
    rows = parts[0].shape[0] // 2
    _, hidden_units, width = weights[2].shape
    vmem, anywhere = pl.BlockSpec(memory_space=pltpu.VMEM), pl.BlockSpec(memory_space=pl.ANY)
    smem = pl.BlockSpec(memory_space=pltpu.SMEM)
    room = (4 * len(slots) + 4) * rows
    shapes = []
    for unit in units:
        for dtype in (jnp.float32, jnp.bfloat16):
            shapes.append(jax.ShapeDtypeStruct((2 * len(unit) * rows, width), dtype))
    return pl.pallas_call(
        functools.partial(expert_kernel, slots, units),
        out_shape=tuple(shapes),
        in_specs=[smem, smem, vmem] + [vmem] * len(parts) + [anywhere] * 4,
        out_specs=(vmem,) * len(shapes),
        scratch_shapes=[
            pltpu.VMEM((2, 2, width, 2 * hidden_units), jnp.bfloat16),
            pltpu.VMEM((2, 2 * hidden_units, width), jnp.bfloat16),
            pltpu.VMEM((room, width + LANES), jnp.bfloat16),
            pltpu.VMEM((room, 2 * hidden_units), jnp.bfloat16),
            pltpu.VMEM((room, width), jnp.float32),
            pltpu.SemaphoreType.DMA((2, 2, 3)),
        ],
        compiler_params=pltpu.CompilerParams(vmem_limit_bytes=36 * MIB),
        name="experts",
    )(place, kinds, pick, *parts, *weights)


def attention_kernel(head_dim, group, q_ref, *refs):
    kv_refs, out_ref = refs[:-1], refs[-1]
    kv_heads = kv_refs[0].shape[1] // (2 * head_dim)
    scale = head_dim**-0.5
    rows = q_ref.shape[0]
    step = max(1, KEYS_AT_ONCE // kv_refs[0].shape[0])
    def columns(ref, head, count=1):
        return ref[:, pl.ds(pl.multiple_of(head * head_dim, head_dim), count * head_dim)]

    def two_heads(pair, carry):
        g = pair // (group // 2)
        both = columns(q_ref, 2 * pair, 2)
        q = jnp.concatenate([both[:, :head_dim], both[:, head_dim:]], axis=0)
        keys = [columns(ref, g) for ref in kv_refs]
        vals = [columns(ref, kv_heads + g) for ref in kv_refs]
        peak, total, mixed = None, 0.0, 0.0
        for at in range(0, len(keys), step):
            scores = [
                lax.dot_general(q, k, (((1,), (1,)), ((), ())), preferred_element_type=jnp.float32)
                for k in keys[at : at + step]
            ]
            peaks = [jnp.max(s, axis=-1, keepdims=True) for s in scores]
            if peak is not None:
                before = peak
                peak = functools.reduce(jnp.maximum, peaks + [before])
                shrink = jnp.exp((before - peak) * scale)
                total, mixed = total * shrink, mixed * shrink
            else:
                peak = functools.reduce(jnp.maximum, peaks)
            for s, v in zip(scores, vals[at : at + step]):
                p = jnp.exp((s - peak) * scale)
                total = total + jnp.sum(p, axis=-1, keepdims=True)
                mixed = mixed + jnp.dot(
                    p.astype(jnp.bfloat16), v, preferred_element_type=jnp.float32
                )
        mixed = (mixed / total).astype(jnp.bfloat16)
        at = pl.multiple_of(2 * pair * head_dim, 2 * head_dim)
        out_ref[:, pl.ds(at, 2 * head_dim)] = jnp.concatenate([mixed[:rows], mixed[rows:]], axis=1)
        return carry

    lax.fori_loop(0, kv_heads * group // 2, two_heads, 0, unroll=2 if len(kv_refs) <= 8 and step >= len(kv_refs) else 1)


def attention_call(queries, kv_parts, head_dim, group):
    vmem = pl.BlockSpec(memory_space=pltpu.VMEM)
    rows, width = queries.shape
    keys = sum(part.shape[0] for part in kv_parts)
    return pl.pallas_call(
        functools.partial(attention_kernel, head_dim, group),
        out_shape=jax.ShapeDtypeStruct((rows, width), jnp.bfloat16),
        in_specs=[vmem] * (1 + len(kv_parts)),
        out_specs=vmem,
        compiler_params=pltpu.CompilerParams(vmem_limit_bytes=48 * MIB),
        name="attention",
    )(queries, *kv_parts)


def body(
    hidden_in,
    modality,
    expert_ids,
    route_weights,
    w_gate_up,
    w_down,
    norm_gain,
    w_query,
    key_value_weight,
    q_gain,
    k_gain,
):
    tok_rows, model_width = hidden_in.shape
    groups = lax.axis_size("expert")
    me, core = lax.axis_index("expert"), lax.axis_index("half")
    slots = groups // 4
    slot_order = [0] + list(range(2, slots, 2)) + list(range(1, slots, 2))
    slot_groups = [[s, s + 2] for s in range(0, slots, 4)] + [[s, s + 2] for s in range(1, slots, 4)]

    payload = payload_call(core[None], hidden_in, expert_ids, route_weights, groups)
    lane = jnp.arange(LANES, dtype=jnp.int32)
    pick = ((lane == me) | (lane == me + groups)).astype(jnp.float32)[None, :]
    kinds = modality.reshape(groups, tok_rows)[:, 0]
    place = jnp.stack([me, core]).astype(jnp.int32)

    arrived = {0: payload}
    for s in range(1, slots):
        arrived[s] = swap(payload, 4 * s, 4 * s)
    own_gu = w_gate_up.transpose(0, 2, 1, 3)
    weights = (own_gu, swap_half(own_gu), w_down, swap_half(w_down))

    jobs = []

    def cross(value, *masks):
        if len(jobs) > 1:
            value = after(value, jobs[-2])
        jobs.append(swap(value, *masks))
        return jobs[-1]

    two, four, outs, returned = {}, {}, {}, {}

    def collect(members, last):
        for s in members:
            two[s] = jnp.concatenate([arrived[s], cross(arrived[s], 1, 2)], axis=0)
            if last is not None and s == members[-1]:
                two[s] = after(two[s], last)
            four[s] = cross(two[s], 2, 1)

    def work(members):
        units = [[s] for s in reversed(members)]
        parts = [part for s in members for part in (two[s], four[s])]
        found = expert_call(members, units, place, kinds, pick, parts, weights)
        for u, unit in enumerate(units):
            outs[unit[0]] = found[2 * u : 2 * u + 2]
        return found[0]

    def give_back(members):
        for s in reversed(members):
            keep, send = outs[s]
            keep = keep + swap(send, 2, 1).astype(jnp.float32)
            cut = keep.shape[0] // 2
            back = swap(keep[cut:].astype(jnp.bfloat16), 1, 2)
            returned[s] = keep[:cut] + back.astype(jnp.float32)

    collect(slot_groups[0], None)
    for before, members in zip(slot_groups, slot_groups[1:]):
        collect(members, work(before))
        give_back(before)
    work(slot_groups[-1])
    give_back(slot_groups[-1])
    mixture = returned[0]
    for s in range(1, slots):
        mixture = mixture + swap(returned[s].astype(jnp.bfloat16), 4 * s, 4 * s).astype(jnp.float32)
    mine = payload[:, :model_width].astype(jnp.float32) + mixture
    theirs = swap_half(mine)
    hidden_out = jnp.where(
        core == 0,
        jnp.concatenate([mine, theirs], axis=0),
        jnp.concatenate([theirs, mine], axis=0),
    )

    normed = rms_scale(hidden_out, norm_gain).astype(jnp.bfloat16)
    head_dim = q_gain.shape[0]
    kv_width = key_value_weight.shape[2]
    kv_heads = kv_width // head_dim
    key_value = jnp.dot(
        normed,
        key_value_weight.reshape(model_width, 2 * kv_width),
        preferred_element_type=jnp.float32,
    )
    keys = rms_scale(key_value[:, :kv_width].reshape(tok_rows, kv_heads, head_dim), k_gain)
    own_kv = jnp.concatenate(
        [keys.reshape(tok_rows, kv_width), key_value[:, kv_width:]], axis=1
    ).astype(jnp.bfloat16)
    queries = jnp.dot(normed, w_query, preferred_element_type=jnp.float32)
    heads = queries.shape[1] // head_dim
    queries = rms_scale(queries.reshape(tok_rows, heads, head_dim), q_gain)
    queries = queries.reshape(tok_rows, heads * head_dim).astype(jnp.bfloat16)

    arrived = {0: own_kv}
    for s in range(1, slots):
        arrived[s] = swap(own_kv, 4 * s, 4 * s)
    kv_parts = []
    for s in slot_order:
        pair = jnp.concatenate([arrived[s], swap(arrived[s], 1, 2)], axis=0)
        kv_parts += [pair, swap(pair, 2, 1)]
    attended = attention_call(queries, kv_parts, head_dim, heads // kv_heads)
    return hidden_out, attended


def solution(mesh):
    in_specs = (
        P("expert", None),
        P(),
        P("expert", None),
        P("expert", None),
        P("expert", None, None, "half"),
        P("expert", "half", None),
        P(),
        P(None, "half"),
        P(None, None, "half"),
        P(),
        P(),
    )
    out_specs = (P("expert", None), P("expert", "half"))
    return jax.shard_map(body, mesh=mesh, in_specs=in_specs, out_specs=out_specs, check_vma=False)
```

time: 190 us -> 164 us (0.86)
  Pallas kernels: 47 us -> 28.6 us
  other arithmetic: 9.41 us -> 3.47 us
  local copies, waits for them, and re-layouts: 14 us -> 9.39 us
    pallas_call x4 -> x3, Pallas kernels: 37.9 us -> 19.9 us  [the longest x2 18.2 us: expert_call(): pl.pallas_call(functools.partial(expert_kernel, slots, units), out_shape=...]
    concatenate x9 -> x3, other arithmetic: 6.23 us -> 1.14 us  [the longest x2 1.12 us: collect(): two[s] = jnp.concatenate([arrived[s], cross(arrived[s], 1, 2)], axis=0)]
    gather x4 -> x0, local copies, waits for them, and re-layouts: 2.56 us -> none  [body(): kinds = kind_of[sources.reshape(-1)]]
    unnamed x26 -> x24, local copies, waits for them, and re-layouts: 7.28 us -> 8.3 us
  transfers between devices with their start and end apart: 36 -> 36, of which waited for: 18 -> 17; matrix products, arithmetic and copies ran while one was open for 10% -> 6% of each run, Pallas kernels for 15% -> 12%
where the time goes in v2:
time: 164 us; the launch traced here: 162 us
  waiting for transfers between devices  65.7 us (40%)
  starting transfers between devices  48.6 us (30%)
  Pallas kernels  28.6 us (17%)
  local copies, waits for them, and re-layouts  9.39 us (6%)
  matrix products  5.2 us (3%)
  other arithmetic  3.47 us (2%)
    ppermute x33, waiting for transfers between devices, swap(): return lax.ppermute(value, ('expert', 'half'), pairs)  64.5 us
    ppermute x33, starting transfers between devices, swap(): return lax.ppermute(value, ('expert', 'half'), pairs)  48 us
    pallas_call x2, Pallas kernels, expert_call(): pl.pallas_call(functools.partial(expert_kernel, slots, units), out_shape=...  18.2 us
    pallas_call x1, Pallas kernels, attention_call(): pl.pallas_call(functools.partial(attention_kernel, head_dim, group), out_...  8.61 us
    unnamed x24, local copies, waits for them, and re-layouts  8.3 us
    dot_general x1, matrix products, body(): queries = jnp.dot(normed, w_query, preferred_element_type=jnp.float32)  4.72 us
  transfers between devices with their start and end apart: 36, of which 17 were waited for; matrix products, arithmetic and copies ran while one was open for 6% of the time, Pallas kernels for 12%

profile of v2, /device:TPU:0, one launch (start us, length us, event | category | flops | bytes accessed | tf_op | source)
XLA Modules:
  0.0 162.0 jit_solution(5363667127055193303)
XLA Ops:
  0.7 6.4 %copy.32 = bf16[2,2048,2,384]{3,1,2,0:T(8,128)(2,1)} copy(bf16[2,2048,2,384]{3,2,1,0:T(2,128)(2,1)} %param.15) | data formatting | bytes 12582912 | tf_op args[4]
  7.0 0.5 collective-permute-start.5
  7.6 1.8 %payload.1 = bf16[64,2176]{1,0:T(8,128)(2,1)} custom-call(s32[1]{0:T(128)} %bitcast.core_ref, bf16[128,2048]{1,0:T(8,128)(2,1)} %hidden_ref.1, s32[8,128]{1,0:T(8,128)} %bitcast.39, f32[8,128]{1,0:T(8,128)} %bitcast.40), custom_call_target="tpu_custom_call" | custom-call | tf_op jit(solution)/shard_map/payload/pallas_call | solution.py:57
  9.3 2.9 %collective-permute-start = (bf16[64,2176]{1,0:T(8,128)(2,1)}, bf16[64,2176]{1,0:T(8,128)(2,1)}, u32[]{:S(2)}, u32[]{:S(2)}) collective-permute-start(bf16[64,2176]{1,0:T(8,128)(2,1)} %payload.1), channel_id=1, source_target_pairs={{0,2},{1,5},{2,0},{3,7},{4,6},{5,1},{6,4},{7,3},{8,10},{9,13},{10,... | collective-permute-start | bytes 835592 | tf_op jit(solution)/shard_map/ppermute | solution.py:26
  12.3 2.6 %collective-permute-start.2 = (bf16[64,2176]{1,0:T(8,128)(2,1)}, bf16[64,2176]{1,0:T(8,128)(2,1)}, u32[]{:S(2)}, u32[]{:S(2)}) collective-permute-start(bf16[64,2176]{1,0:T(8,128)(2,1)} %payload.1), channel_id=1, source_target_pairs={{0,16},{1,17},{2,18},{3,19},{4,20},{5,21},{6,22},{7,23},{8,24},{9,... | collective-permute-start | bytes 835592 | tf_op jit(solution)/shard_map/ppermute | solution.py:26
  14.9 1.6 collective-permute-start.9
  16.6 0.5 collective-permute-done
  17.1 1.1 pad_maximum_fusion.refs_0_
  18.2 2.1 %collective-permute-start.1 = (bf16[128,2176]{1,0:T(8,128)(2,1)S(1)}, bf16[128,2176]{1,0:T(8,128)(2,1)S(1)}, u32[]{:S(2)}, u32[]{:S(2)}) collective-permute-start(bf16[128,2176]{1,0:T(8,128)(2,1)S(1)} %pad_maximum_fusion.refs_0_), channel_id=1, source_target_pairs={{0,4},{1,3},{2,6},{3,1},{4,0},{5,7},{6,2},{7,5},{8,12},{9,11},{10,... | collective-permute-start | bytes 1671176 | tf_op jit(solution)/shard_map/ppermute | solution.py:26
  20.3 7.6 %collective-permute-done.2 = bf16[64,2176]{1,0:T(8,128)(2,1)} collective-permute-done((bf16[64,2176]{1,0:T(8,128)(2,1)}, bf16[64,2176]{1,0:T(8,128)(2,1)}, u32[]{:S(2)}, u32[]{:S(2)}) %collective-permute-start.2) | collective-permute-done | bytes 278560 | tf_op jit(solution)/shard_map/ppermute | solution.py:26
  27.9 1.4 collective-permute-start.3
  29.3 1.0 constant_dynamic-update-slice_fusion.1
  30.3 3.6 %collective-permute-start.12 = (bf16[64,2176]{1,0:T(8,128)(2,1)}, bf16[64,2176]{1,0:T(8,128)(2,1)S(1)}, u32[]{:S(2)}, u32[]{:S(2)}) collective-permute-start(bf16[64,2176]{1,0:T(8,128)(2,1)} %payload.1), channel_id=1, source_target_pairs={{0,24},{1,25},{2,26},{3,27},{4,28},{5,29},{6,30},{7,31},{8,16},{9,... | collective-permute-start | bytes 835592 | tf_op jit(solution)/shard_map/ppermute | solution.py:26
  33.9 0.8 collective-permute-done.3
  34.7 1.4 collective-permute-start.10
  36.1 0.7 collective-permute-start.4
  36.8 2.9 %collective-permute-done.12 = bf16[64,2176]{1,0:T(8,128)(2,1)S(1)} collective-permute-done((bf16[64,2176]{1,0:T(8,128)(2,1)}, bf16[64,2176]{1,0:T(8,128)(2,1)S(1)}, u32[]{:S(2)}, u32[]{:S(2)}) %collective-permute-start.12) | collective-permute-done | bytes 278560 | tf_op jit(solution)/shard_map/ppermute | solution.py:26
  39.7 4.5 %collective-permute-done.10 = bf16[64,2176]{1,0:T(8,128)(2,1)S(1)} collective-permute-done((bf16[64,2176]{1,0:T(8,128)(2,1)S(1)}, bf16[64,2176]{1,0:T(8,128)(2,1)S(1)}, u32[]{:S(2)}, u32[]{:S(2)}) %collective-permute-start.10) | collective-permute-done | bytes 278560 | tf_op jit(solution)/shard_map/ppermute | solution.py:26
  44.3 1.4 collective-permute-start.13
  45.7 3.0 %collective-permute-done.4.refs_3_ = bf16[128,2176]{1,0:T(8,128)(2,1)S(1)} collective-permute-done((bf16[128,2176]{1,0:T(8,128)(2,1)S(1)}, bf16[128,2176]{1,0:T(8,128)(2,1)S(1)}, u32[]{:S(2)}, u32[]{:S(2)}) %collective-permute-start.4) | collective-permute-done | bytes 557088 | tf_op jit(solution)/shard_map/ppermute | solution.py:26
  48.7 0.6 collective-permute-start.11
  49.3 8.9 %experts.2 = (f32[128,2048]{1,0:T(8,128)S(1)}, bf16[128,2048]{1,0:T(8,128)(2,1)S(1)}, f32[128,2048]{1,0:T(8,128)S(1)}, bf16[128,2048]{1,0:T(8,128)(2,1)S(1)}) custom-call(s32[2]{0:T(128)S(1)} %pad_add_fusion.place_ref, s32[16]{0:T(128)S(1)} %slice_reduce_fusion.kind_ref, f32[1,128]{1,0:T(1,128)S(1)} %or_convert_fusion.pick_ref, ...), custom_call_target="tpu_custom_call" | custom-call | tf_op jit(solution)/shard_map/experts/pallas_call | solution.py:187
  58.2 1.4 collective-permute-start.18
  59.7 0.7 collective-permute-start.14
  60.4 1.4 collective-permute-start.7
  61.8 6.2 %collective-permute-done.18 = bf16[128,2048]{1,0:T(8,128)(2,1)S(1)} collective-permute-done((bf16[128,2048]{1,0:T(8,128)(2,1)S(1)}, bf16[128,2048]{1,0:T(8,128)(2,1)S(1)}, u32[]{:S(2)}, u32[]{:S(2)}) %collective-permute-start.18) | collective-permute-done | bytes 524320 | tf_op jit(solution)/shard_map/ppermute | solution.py:26
  68.1 0.4 collective-permute-start.19
  68.5 7.7 %collective-permute-done.14.refs_3_ = bf16[128,2176]{1,0:T(8,128)(2,1)S(1)} collective-permute-done((bf16[128,2176]{1,0:T(8,128)(2,1)S(1)}, bf16[128,2176]{1,0:T(8,128)(2,1)S(1)}, u32[]{:S(2)}, u32[]{:S(2)}) %collective-permute-start.14) | collective-permute-done | bytes 557088 | tf_op jit(solution)/shard_map/ppermute | solution.py:26
  76.2 9.3 %experts.3 = (f32[128,2048]{1,0:T(8,128)S(1)}, bf16[128,2048]{1,0:T(8,128)(2,1)S(1)}, f32[128,2048]{1,0:T(8,128)S(1)}, bf16[128,2048]{1,0:T(8,128)(2,1)S(1)}) custom-call(s32[2]{0:T(128)S(1)} %pad_add_fusion.place_ref, s32[16]{0:T(128)S(1)} %slice_reduce_fusion.kind_ref, f32[1,128]{1,0:T(1,128)S(1)} %or_convert_fusion.pick_ref, ...), custom_call_target="tpu_custom_call" | custom-call | tf_op jit(solution)/shard_map/experts/pallas_call | solution.py:187
  85.5 1.4 collective-permute-start.21
  87.1 1.0 collective-permute-start.8
  88.3 9.3 %collective-permute-done.21 = bf16[128,2048]{1,0:T(8,128)(2,1)S(1)} collective-permute-done((bf16[128,2048]{1,0:T(8,128)(2,1)S(1)}, bf16[128,2048]{1,0:T(8,128)(2,1)S(1)}, u32[]{:S(2)}, u32[]{:S(2)}) %collective-permute-start.21) | collective-permute-done | bytes 524320 | tf_op jit(solution)/shard_map/ppermute | solution.py:26
  97.7 0.4 collective-permute-start.22
  98.1 7.9 %collective-permute-done.15 = bf16[128,2048]{1,0:T(8,128)(2,1)S(1)} collective-permute-done((bf16[128,2048]{1,0:T(8,128)(2,1)S(1)}, bf16[128,2048]{1,0:T(8,128)(2,1)S(1)}, u32[]{:S(2)}, u32[]{:S(2)}) %collective-permute-start.15) | collective-permute-done | bytes 524320 | tf_op jit(solution)/shard_map/ppermute | solution.py:26
  106.2 0.4 collective-permute-start.16
  106.6 3.4 %collective-permute-start.23 = (bf16[64,2048]{1,0:T(8,128)(2,1)S(1)}, bf16[64,2048]{1,0:T(8,128)(2,1)S(1)}, u32[]{:S(2)}, u32[]{:S(2)}) collective-permute-start(bf16[64,2048]{1,0:T(8,128)(2,1)S(1)} %fusion.2), channel_id=1, source_target_pairs={{0,24},{1,25},{2,26},{3,27},{4,28},{5,29},{6,30},{7,31},{8,16},{9,... | collective-permute-start | bytes 786440 | tf_op jit(solution)/shard_map/ppermute | solution.py:26
  110.0 2.6 %collective-permute-done.16 = bf16[64,2048]{1,0:T(8,128)(2,1)S(1)} collective-permute-done((bf16[64,2048]{1,0:T(8,128)(2,1)S(1)}, bf16[64,2048]{1,0:T(8,128)(2,1)S(1)}, u32[]{:S(2)}, u32[]{:S(2)}) %collective-permute-start.16) | collective-permute-done | bytes 262176 | tf_op jit(solution)/shard_map/ppermute | solution.py:26
  112.8 2.1 %collective-permute-done.23 = bf16[64,2048]{1,0:T(8,128)(2,1)S(1)} collective-permute-done((bf16[64,2048]{1,0:T(8,128)(2,1)S(1)}, bf16[64,2048]{1,0:T(8,128)(2,1)S(1)}, u32[]{:S(2)}, u32[]{:S(2)}) %collective-permute-start.23) | collective-permute-done | bytes 262176 | tf_op jit(solution)/shard_map/ppermute | solution.py:26
  114.8 4.2 %collective-permute-done.17 = bf16[64,2048]{1,0:T(8,128)(2,1)S(1)} collective-permute-done((bf16[64,2048]{1,0:T(8,128)(2,1)S(1)}, bf16[64,2048]{1,0:T(8,128)(2,1)S(1)}, u32[]{:S(2)}, u32[]{:S(2)}) %collective-permute-start.17) | collective-permute-done | bytes 262176 | tf_op jit(solution)/shard_map/ppermute | solution.py:26
  119.4 0.5 copy.26
  120.1 1.2 collective-permute-done.24
  121.3 0.2 multiply_reduce_fusion
  121.5 0.5 fusion.11
  122.1 0.2 reduce_sum.29
  122.3 0.2 mul.95
  122.6 0.4 collective-permute-start.25
  123.0 1.9 %collective-permute-start.27 = (bf16[128,512]{1,0:T(8,128)(2,1)S(1)}, bf16[128,512]{1,0:T(8,128)(2,1)S(1)}, u32[]{:S(2)}, u32[]{:S(2)}) collective-permute-start(bf16[128,512]{1,0:T(8,128)(2,1)S(1)} %pad_maximum_fusion.3), channel_id=1, source_target_pairs={{0,16},{1,17},{2,18},{3,19},{4,20},{5,21},{6,22},{7,23},{8,24},{9,... | collective-permute-start | bytes 393224 | tf_op jit(solution)/shard_map/ppermute | solution.py:26
  124.9 2.0 %collective-permute-start.30 = (bf16[128,512]{1,0:T(8,128)(2,1)S(1)}, bf16[128,512]{1,0:T(8,128)(2,1)S(1)}, u32[]{:S(2)}, u32[]{:S(2)}) collective-permute-start(bf16[128,512]{1,0:T(8,128)(2,1)S(1)} %pad_maximum_fusion.3), channel_id=1, source_target_pairs={{0,8},{1,9},{2,10},{3,11},{4,12},{5,13},{6,14},{7,15},{8,0},{9,1},... | collective-permute-start | bytes 393224 | tf_op jit(solution)/shard_map/ppermute | solution.py:26
  126.9 0.5 collective-permute-start.33
  127.4 4.7 %fusion.12 = f32[128,2048]{1,0:T(8,128)S(1)} fusion(bf16[2048,2048]{1,0:T(8,128)(2,1)} %param.18, f32[128,2048]{1,0:T(8,128)S(1)} %get-tuple-element.33, f32[2048]{0:T(1024)S(1)} %copy-done.5, f32[128]{0:T(128)S(1)} %add_rsqrt_fusion.2), kind=kOutput, calls=%fused_computation.55 | convolution fusion | flops 1074528256 | bytes 10494464 | tf_op jit(solution)/shard_map/dot_general | solution.py:357
  132.4 0.3 reduce_sum.28
  133.0 2.1 %collective-permute-start.26 = (bf16[256,512]{1,0:T(8,128)(2,1)S(1)}, bf16[256,512]{1,0:T(8,128)(2,1)S(1)}, u32[]{:S(2)}, u32[]{:S(2)}) collective-permute-start(bf16[256,512]{1,0:T(8,128)(2,1)S(1)} %pad_maximum_fusion.2.refs_0_), channel_id=1, source_target_pairs={{0,4},{1,3},{2,6},{3,1},{4,0},{5,7},{6,2},{7,5},{8,12},{9,11},{10,... | collective-permute-start | bytes 786440 | tf_op jit(solution)/shard_map/ppermute | solution.py:26
  135.0 1.1 collective-permute-start.28
  136.2 1.0 collective-permute-start.31
  137.2 1.1 collective-permute-start.34
  138.4 1.7 %collective-permute-done.28 = bf16[128,512]{1,0:T(8,128)(2,1)S(1)} collective-permute-done((bf16[128,512]{1,0:T(8,128)(2,1)S(1)}, bf16[128,512]{1,0:T(8,128)(2,1)S(1)}, u32[]{:S(2)}, u32[]{:S(2)}) %collective-permute-start.28) | collective-permute-done | bytes 131104 | tf_op jit(solution)/shard_map/ppermute | solution.py:26
  140.1 3.4 %collective-permute-start.29 = (bf16[256,512]{1,0:T(8,128)(2,1)S(1)}, bf16[256,512]{1,0:T(8,128)(2,1)S(1)}, u32[]{:S(2)}, u32[]{:S(2)}) collective-permute-start(bf16[256,512]{1,0:T(8,128)(2,1)S(1)} %constant_dynamic-update-slice_fusion.4.refs_2_), channel_id=1, source_target_pairs={{0,4},{1,3},{2,6},{3,1},{4,0},{5,7},{6,2},{7,5},{8,12},{9,11},{10,... | collective-permute-start | bytes 786440 | tf_op jit(solution)/shard_map/ppermute | solution.py:26
  143.5 2.8 %collective-permute-start.32 = (bf16[256,512]{1,0:T(8,128)(2,1)S(1)}, bf16[256,512]{1,0:T(8,128)(2,1)S(1)}, u32[]{:S(2)}, u32[]{:S(2)}) collective-permute-start(bf16[256,512]{1,0:T(8,128)(2,1)S(1)} %constant_dynamic-update-slice_fusion.6.refs_4_), channel_id=1, source_target_pairs={{0,4},{1,3},{2,6},{3,1},{4,0},{5,7},{6,2},{7,5},{8,12},{9,11},{10,... | collective-permute-start | bytes 786440 | tf_op jit(solution)/shard_map/ppermute | solution.py:26
  146.3 2.8 %collective-permute-start.35 = (bf16[256,512]{1,0:T(8,128)(2,1)S(1)}, bf16[256,512]{1,0:T(8,128)(2,1)S(1)}, u32[]{:S(2)}, u32[]{:S(2)}) collective-permute-start(bf16[256,512]{1,0:T(8,128)(2,1)S(1)} %constant_dynamic-update-slice_fusion.8.refs_6_), channel_id=1, source_target_pairs={{0,4},{1,3},{2,6},{3,1},{4,0},{5,7},{6,2},{7,5},{8,12},{9,11},{10,... | collective-permute-start | bytes 786440 | tf_op jit(solution)/shard_map/ppermute | solution.py:26
  149.1 0.3 mul.86
  149.4 0.5 fusion.1.q_ref
  149.9 0.7 collective-permute-done.32.refs_5_
  150.6 2.8 %collective-permute-done.35.refs_7_ = bf16[256,512]{1,0:T(8,128)(2,1)S(1)} collective-permute-done((bf16[256,512]{1,0:T(8,128)(2,1)S(1)}, bf16[256,512]{1,0:T(8,128)(2,1)S(1)}, u32[]{:S(2)}, u32[]{:S(2)}) %collective-permute-start.35) | collective-permute-done | bytes 262176 | tf_op jit(solution)/shard_map/ppermute | solution.py:26
  153.4 8.6 %attention.1 = bf16[128,2048]{1,0:T(8,128)(2,1)} custom-call(bf16[128,2048]{1,0:T(8,128)(2,1)S(1)} %fusion.1.q_ref, bf16[256,512]{1,0:T(8,128)(2,1)S(1)} %pad_maximum_fusion.2.refs_0_, bf16[256,512]{1,0:T(8,128)(2,1)S(1)} %collective-permute-done.26.refs_1_, bf16[256,512]{1,0:T(8,128)(2,1)S(1)} %constant_dynamic-update-slice_fusion.4.refs_2_, ...), custom_call_target="tpu_custom_call" | custom-call | tf_op jit(solution)/shard_map/attention/pallas_call | solution.py:252
  (80 shorter events, 2.5 us)
Async XLA Ops:
  0.6 119.4 %copy-start = (f32[128]{0:T(128)S(1)}, f32[128]{0:T(128)}, u32[]{:S(2)}) copy-start(f32[128]{0:T(128)} %param.20) | copy-start | bytes 1540
  0.6 6.8 %copy-start.1 = (bf16[2,384,2048]{2,1,0:T(8,128)(2,1)S(1)}, bf16[2,384,2048]{2,1,0:T(8,128)(2,1)}, u32[]{:S(2)}) copy-start(bf16[2,384,2048]{2,1,0:T(8,128)(2,1)} %refs_6_.3) | copy-start | bytes 9437188
  0.7 15.9 %copy-start.6 = (s32[2048]{0:T(1024)S(1)}, s32[2048]{0:T(1024)}, u32[]{:S(2)}) copy-start(s32[2048]{0:T(1024)} %param.12) | copy-start | bytes 24580
  7.0 42.3 %collective-permute-start.5 = (bf16[2,2,2048,384]{3,2,1,0:T(8,128)(2,1)}, bf16[2,2,2048,384]{3,2,1,0:T(8,128)(2,1)}, u32[]{:S(2)}, u32[]{:S(2)}) collective-permute-start(bf16[2,2,2048,384]{3,2,1,0:T(8,128)(2,1)} %bitcast.32.refs_4_), channel_id=1, source_target_pairs={{0,1},{1,0},{2,3},{3,2},{4,5},{5,4},{6,7},{7,6},{8,9},{9,8},{10,11... | collective-permute-start | bytes 18874376 | tf_op jit(solution)/shard_map/ppermute | solution.py:34
  7.5 41.8 %collective-permute-start.6 = (bf16[2,384,2048]{2,1,0:T(8,128)(2,1)S(1)}, bf16[2,384,2048]{2,1,0:T(8,128)(2,1)}, u32[]{:S(2)}, u32[]{:S(2)}) collective-permute-start(bf16[2,384,2048]{2,1,0:T(8,128)(2,1)S(1)} %copy-done.1), channel_id=1, source_target_pairs={{0,1},{1,0},{2,3},{3,2},{4,5},{5,4},{6,7},{7,6},{8,9},{9,8},{10,11... | collective-permute-start | bytes 9437192 | tf_op jit(solution)/shard_map/ppermute | solution.py:34
  9.3 7.8 %collective-permute-start = (bf16[64,2176]{1,0:T(8,128)(2,1)}, bf16[64,2176]{1,0:T(8,128)(2,1)}, u32[]{:S(2)}, u32[]{:S(2)}) collective-permute-start(bf16[64,2176]{1,0:T(8,128)(2,1)} %payload.1), channel_id=1, source_target_pairs={{0,2},{1,5},{2,0},{3,7},{4,6},{5,1},{6,4},{7,3},{8,10},{9,13},{10,... | collective-permute-start | bytes 835592 | tf_op jit(solution)/shard_map/ppermute | solution.py:26
  12.3 15.6 %collective-permute-start.2 = (bf16[64,2176]{1,0:T(8,128)(2,1)}, bf16[64,2176]{1,0:T(8,128)(2,1)}, u32[]{:S(2)}, u32[]{:S(2)}) collective-permute-start(bf16[64,2176]{1,0:T(8,128)(2,1)} %payload.1), channel_id=1, source_target_pairs={{0,16},{1,17},{2,18},{3,19},{4,20},{5,21},{6,22},{7,23},{8,24},{9,... | collective-permute-start | bytes 835592 | tf_op jit(solution)/shard_map/ppermute | solution.py:26
  14.9 15.4 %collective-permute-start.9 = (bf16[64,2176]{1,0:T(8,128)(2,1)}, bf16[64,2176]{1,0:T(8,128)(2,1)S(1)}, u32[]{:S(2)}, u32[]{:S(2)}) collective-permute-start(bf16[64,2176]{1,0:T(8,128)(2,1)} %payload.1), channel_id=1, source_target_pairs={{0,8},{1,9},{2,10},{3,11},{4,12},{5,13},{6,14},{7,15},{8,0},{9,1},... | collective-permute-start | bytes 835592 | tf_op jit(solution)/shard_map/ppermute | solution.py:26
  18.2 17.9 %collective-permute-start.1 = (bf16[128,2176]{1,0:T(8,128)(2,1)S(1)}, bf16[128,2176]{1,0:T(8,128)(2,1)S(1)}, u32[]{:S(2)}, u32[]{:S(2)}) collective-permute-start(bf16[128,2176]{1,0:T(8,128)(2,1)S(1)} %pad_maximum_fusion.refs_0_), channel_id=1, source_target_pairs={{0,4},{1,3},{2,6},{3,1},{4,0},{5,7},{6,2},{7,5},{8,12},{9,11},{10,... | collective-permute-start | bytes 1671176 | tf_op jit(solution)/shard_map/ppermute | solution.py:26
  27.9 6.8 %collective-permute-start.3 = (bf16[64,2176]{1,0:T(8,128)(2,1)}, bf16[64,2176]{1,0:T(8,128)(2,1)S(1)}, u32[]{:S(2)}, u32[]{:S(2)}) collective-permute-start(bf16[64,2176]{1,0:T(8,128)(2,1)} %collective-permute-done.2), channel_id=1, source_target_pairs={{0,2},{1,5},{2,0},{3,7},{4,6},{5,1},{6,4},{7,3},{8,10},{9,13},{10,... | collective-permute-start | bytes 835592 | tf_op jit(solution)/shard_map/ppermute | solution.py:26
  30.3 9.5 %collective-permute-start.12 = (bf16[64,2176]{1,0:T(8,128)(2,1)}, bf16[64,2176]{1,0:T(8,128)(2,1)S(1)}, u32[]{:S(2)}, u32[]{:S(2)}) collective-permute-start(bf16[64,2176]{1,0:T(8,128)(2,1)} %payload.1), channel_id=1, source_target_pairs={{0,24},{1,25},{2,26},{3,27},{4,28},{5,29},{6,30},{7,31},{8,16},{9,... | collective-permute-start | bytes 835592 | tf_op jit(solution)/shard_map/ppermute | solution.py:26
  34.7 9.6 %collective-permute-start.10 = (bf16[64,2176]{1,0:T(8,128)(2,1)S(1)}, bf16[64,2176]{1,0:T(8,128)(2,1)S(1)}, u32[]{:S(2)}, u32[]{:S(2)}) collective-permute-start(bf16[64,2176]{1,0:T(8,128)(2,1)S(1)} %collective-permute-done.9), channel_id=1, source_target_pairs={{0,2},{1,5},{2,0},{3,7},{4,6},{5,1},{6,4},{7,3},{8,10},{9,13},{10,... | collective-permute-start | bytes 835592 | tf_op jit(solution)/shard_map/ppermute | solution.py:26
  36.1 12.6 %collective-permute-start.4 = (bf16[128,2176]{1,0:T(8,128)(2,1)S(1)}, bf16[128,2176]{1,0:T(8,128)(2,1)S(1)}, u32[]{:S(2)}, u32[]{:S(2)}) collective-permute-start(bf16[128,2176]{1,0:T(8,128)(2,1)S(1)} %constant_dynamic-update-slice_fusion.refs_2_), channel_id=1, source_target_pairs={{0,4},{1,3},{2,6},{3,1},{4,0},{5,7},{6,2},{7,5},{8,12},{9,11},{10,... | collective-permute-start | bytes 1671176 | tf_op jit(solution)/shard_map/ppermute | solution.py:26
  44.3 15.4 %collective-permute-start.13 = (bf16[64,2176]{1,0:T(8,128)(2,1)S(1)}, bf16[64,2176]{1,0:T(8,128)(2,1)S(1)}, u32[]{:S(2)}, u32[]{:S(2)}) collective-permute-start(bf16[64,2176]{1,0:T(8,128)(2,1)S(1)} %collective-permute-done.12), channel_id=1, source_target_pairs={{0,2},{1,5},{2,0},{3,7},{4,6},{5,1},{6,4},{7,3},{8,10},{9,13},{10,... | collective-permute-start | bytes 835592 | tf_op jit(solution)/shard_map/ppermute | solution.py:26
  48.7 11.1 %collective-permute-start.11 = (bf16[128,2176]{1,0:T(8,128)(2,1)S(1)}, bf16[128,2176]{1,0:T(8,128)(2,1)S(1)}, u32[]{:S(2)}, u32[]{:S(2)}) collective-permute-start(bf16[128,2176]{1,0:T(8,128)(2,1)S(1)} %constant_dynamic-update-slice_fusion.2.refs_0_), channel_id=1, source_target_pairs={{0,4},{1,3},{2,6},{3,1},{4,0},{5,7},{6,2},{7,5},{8,12},{9,11},{10,... | collective-permute-start | bytes 1671176 | tf_op jit(solution)/shard_map/ppermute | solution.py:26
  58.2 9.8 %collective-permute-start.18 = (bf16[128,2048]{1,0:T(8,128)(2,1)S(1)}, bf16[128,2048]{1,0:T(8,128)(2,1)S(1)}, u32[]{:S(2)}, u32[]{:S(2)}) collective-permute-start(bf16[128,2048]{1,0:T(8,128)(2,1)S(1)} %get-tuple-element.29), channel_id=1, source_target_pairs={{0,4},{1,3},{2,6},{3,1},{4,0},{5,7},{6,2},{7,5},{8,12},{9,11},{10,... | collective-permute-start | bytes 1572872 | tf_op jit(solution)/shard_map/ppermute | solution.py:26
  59.7 16.5 %collective-permute-start.14 = (bf16[128,2176]{1,0:T(8,128)(2,1)S(1)}, bf16[128,2176]{1,0:T(8,128)(2,1)S(1)}, u32[]{:S(2)}, u32[]{:S(2)}) collective-permute-start(bf16[128,2176]{1,0:T(8,128)(2,1)S(1)} %pad_maximum_fusion.1.refs_2_), channel_id=1, source_target_pairs={{0,4},{1,3},{2,6},{3,1},{4,0},{5,7},{6,2},{7,5},{8,12},{9,11},{10,... | collective-permute-start | bytes 1671176 | tf_op jit(solution)/shard_map/ppermute | solution.py:26
  60.4 26.5 %collective-permute-start.7 = (bf16[128,2048]{1,0:T(8,128)(2,1)S(1)}, bf16[128,2048]{1,0:T(8,128)(2,1)S(1)}, u32[]{:S(2)}, u32[]{:S(2)}) collective-permute-start(bf16[128,2048]{1,0:T(8,128)(2,1)S(1)} %get-tuple-element.20), channel_id=1, source_target_pairs={{0,4},{1,3},{2,6},{3,1},{4,0},{5,7},{6,2},{7,5},{8,12},{9,11},{10,... | collective-permute-start | bytes 1572872 | tf_op jit(solution)/shard_map/ppermute | solution.py:26
  68.1 20.0 %collective-permute-start.19 = (bf16[64,2048]{1,0:T(8,128)(2,1)S(1)}, bf16[64,2048]{1,0:T(8,128)(2,1)S(1)}, u32[]{:S(2)}, u32[]{:S(2)}) collective-permute-start(bf16[64,2048]{1,0:T(8,128)(2,1)S(1)} %slice.93), channel_id=1, source_target_pairs={{0,2},{1,5},{2,0},{3,7},{4,6},{5,1},{6,4},{7,3},{8,10},{9,13},{10,... | collective-permute-start | bytes 786440 | tf_op jit(solution)/shard_map/ppermute | solution.py:26
  85.5 12.1 %collective-permute-start.21 = (bf16[128,2048]{1,0:T(8,128)(2,1)S(1)}, bf16[128,2048]{1,0:T(8,128)(2,1)S(1)}, u32[]{:S(2)}, u32[]{:S(2)}) collective-permute-start(bf16[128,2048]{1,0:T(8,128)(2,1)S(1)} %get-tuple-element.31), channel_id=1, source_target_pairs={{0,4},{1,3},{2,6},{3,1},{4,0},{5,7},{6,2},{7,5},{8,12},{9,11},{10,... | collective-permute-start | bytes 1572872 | tf_op jit(solution)/shard_map/ppermute | solution.py:26
  87.1 25.6 %collective-permute-start.8 = (bf16[64,2048]{1,0:T(8,128)(2,1)S(1)}, bf16[64,2048]{1,0:T(8,128)(2,1)S(1)}, u32[]{:S(2)}, u32[]{:S(2)}) collective-permute-start(bf16[64,2048]{1,0:T(8,128)(2,1)S(1)} %slice.95), channel_id=1, source_target_pairs={{0,2},{1,5},{2,0},{3,7},{4,6},{5,1},{6,4},{7,3},{8,10},{9,13},{10,... | collective-permute-start | bytes 786440 | tf_op jit(solution)/shard_map/ppermute | solution.py:26
  88.1 17.8 %collective-permute-start.15 = (bf16[128,2048]{1,0:T(8,128)(2,1)S(1)}, bf16[128,2048]{1,0:T(8,128)(2,1)S(1)}, u32[]{:S(2)}, u32[]{:S(2)}) collective-permute-start(bf16[128,2048]{1,0:T(8,128)(2,1)S(1)} %get-tuple-element.28), channel_id=1, source_target_pairs={{0,4},{1,3},{2,6},{3,1},{4,0},{5,7},{6,2},{7,5},{8,12},{9,11},{10,... | collective-permute-start | bytes 1572872 | tf_op jit(solution)/shard_map/ppermute | solution.py:26
  88.2 24.5 %collective-permute-start.20 = (bf16[64,2048]{1,0:T(8,128)(2,1)S(1)}, bf16[64,2048]{1,0:T(8,128)(2,1)S(1)}, u32[]{:S(2)}, u32[]{:S(2)}) collective-permute-start(bf16[64,2048]{1,0:T(8,128)(2,1)S(1)} %fusion.3), channel_id=1, source_target_pairs={{0,16},{1,17},{2,18},{3,19},{4,20},{5,21},{6,22},{7,23},{8,24},{9,... | collective-permute-start | bytes 786440 | tf_op jit(solution)/shard_map/ppermute | solution.py:26
  97.7 8.8 %collective-permute-start.22 = (bf16[64,2048]{1,0:T(8,128)(2,1)S(1)}, bf16[64,2048]{1,0:T(8,128)(2,1)S(1)}, u32[]{:S(2)}, u32[]{:S(2)}) collective-permute-start(bf16[64,2048]{1,0:T(8,128)(2,1)S(1)} %slice.92), channel_id=1, source_target_pairs={{0,2},{1,5},{2,0},{3,7},{4,6},{5,1},{6,4},{7,3},{8,10},{9,13},{10,... | collective-permute-start | bytes 786440 | tf_op jit(solution)/shard_map/ppermute | solution.py:26
  106.0 13.1 %copy-start.3 = (bf16[64,2176]{1,0:T(8,128)(2,1)S(1)}, bf16[64,2176]{1,0:T(8,128)(2,1)}, u32[]{:S(2)}) copy-start(bf16[64,2176]{1,0:T(8,128)(2,1)} %payload.1) | copy-start | bytes 835588
  106.1 13.2 %copy-start.4 = (bf16[2048,2,256]{2,1,0:T(2,128)(2,1)S(1)}, bf16[2048,2,256]{2,1,0:T(2,128)(2,1)}, u32[]{:S(2)}) copy-start(bf16[2048,2,256]{2,1,0:T(2,128)(2,1)} %param.19) | copy-start | bytes 6291460
  106.2 6.4 %collective-permute-start.16 = (bf16[64,2048]{1,0:T(8,128)(2,1)S(1)}, bf16[64,2048]{1,0:T(8,128)(2,1)S(1)}, u32[]{:S(2)}, u32[]{:S(2)}) collective-permute-start(bf16[64,2048]{1,0:T(8,128)(2,1)S(1)} %slice.94), channel_id=1, source_target_pairs={{0,2},{1,5},{2,0},{3,7},{4,6},{5,1},{6,4},{7,3},{8,10},{9,13},{10,... | collective-permute-start | bytes 786440 | tf_op jit(solution)/shard_map/ppermute | solution.py:26
  106.6 8.2 %collective-permute-start.23 = (bf16[64,2048]{1,0:T(8,128)(2,1)S(1)}, bf16[64,2048]{1,0:T(8,128)(2,1)S(1)}, u32[]{:S(2)}, u32[]{:S(2)}) collective-permute-start(bf16[64,2048]{1,0:T(8,128)(2,1)S(1)} %fusion.2), channel_id=1, source_target_pairs={{0,24},{1,25},{2,26},{3,27},{4,28},{5,29},{6,30},{7,31},{8,16},{9,... | collective-permute-start | bytes 786440 | tf_op jit(solution)/shard_map/ppermute | solution.py:26
  112.7 6.4 %collective-permute-start.17 = (bf16[64,2048]{1,0:T(8,128)(2,1)S(1)}, bf16[64,2048]{1,0:T(8,128)(2,1)S(1)}, u32[]{:S(2)}, u32[]{:S(2)}) collective-permute-start(bf16[64,2048]{1,0:T(8,128)(2,1)S(1)} %fusion.4), channel_id=1, source_target_pairs={{0,8},{1,9},{2,10},{3,11},{4,12},{5,13},{6,14},{7,15},{8,0},{9,1},... | collective-permute-start | bytes 786440 | tf_op jit(solution)/shard_map/ppermute | solution.py:26
  119.3 2.0 %collective-permute-start.24 = (f32[64,2048]{1,0:T(8,128)S(1)}, f32[64,2048]{1,0:T(8,128)S(1)}, u32[]{:S(2)}, u32[]{:S(2)}) collective-permute-start(f32[64,2048]{1,0:T(8,128)S(1)} %fusion.8), channel_id=1, source_target_pairs={{0,1},{1,0},{2,3},{3,2},{4,5},{5,4},{6,7},{7,6},{8,9},{9,8},{10,11... | collective-permute-start | bytes 1572872 | tf_op jit(solution)/shard_map/ppermute | solution.py:34
  119.4 0.7 copy-start.7
  120.0 1.4 copy-start.5
  121.5 5.9 %copy-start.2 = (f32[128,2048]{1,0:T(8,128)}, f32[128,2048]{1,0:T(8,128)S(1)}, u32[]{:S(2)}) copy-start(f32[128,2048]{1,0:T(8,128)S(1)} %get-tuple-element.33) | copy-start | bytes 3145732
  122.6 10.3 %collective-permute-start.25 = (bf16[128,512]{1,0:T(8,128)(2,1)S(1)}, bf16[128,512]{1,0:T(8,128)(2,1)S(1)}, u32[]{:S(2)}, u32[]{:S(2)}) collective-permute-start(bf16[128,512]{1,0:T(8,128)(2,1)S(1)} %pad_maximum_fusion.3), channel_id=1, source_target_pairs={{0,2},{1,5},{2,0},{3,7},{4,6},{5,1},{6,4},{7,3},{8,10},{9,13},{10,... | collective-permute-start | bytes 393224 | tf_op jit(solution)/shard_map/ppermute | solution.py:26
  123.0 12.1 %collective-permute-start.27 = (bf16[128,512]{1,0:T(8,128)(2,1)S(1)}, bf16[128,512]{1,0:T(8,128)(2,1)S(1)}, u32[]{:S(2)}, u32[]{:S(2)}) collective-permute-start(bf16[128,512]{1,0:T(8,128)(2,1)S(1)} %pad_maximum_fusion.3), channel_id=1, source_target_pairs={{0,16},{1,17},{2,18},{3,19},{4,20},{5,21},{6,22},{7,23},{8,24},{9,... | collective-permute-start | bytes 393224 | tf_op jit(solution)/shard_map/ppermute | solution.py:26
  124.9 11.3 %collective-permute-start.30 = (bf16[128,512]{1,0:T(8,128)(2,1)S(1)}, bf16[128,512]{1,0:T(8,128)(2,1)S(1)}, u32[]{:S(2)}, u32[]{:S(2)}) collective-permute-start(bf16[128,512]{1,0:T(8,128)(2,1)S(1)} %pad_maximum_fusion.3), channel_id=1, source_target_pairs={{0,8},{1,9},{2,10},{3,11},{4,12},{5,13},{6,14},{7,15},{8,0},{9,1},... | collective-permute-start | bytes 393224 | tf_op jit(solution)/shard_map/ppermute | solution.py:26
  126.9 10.3 %collective-permute-start.33 = (bf16[128,512]{1,0:T(8,128)(2,1)S(1)}, bf16[128,512]{1,0:T(8,128)(2,1)S(1)}, u32[]{:S(2)}, u32[]{:S(2)}) collective-permute-start(bf16[128,512]{1,0:T(8,128)(2,1)S(1)} %pad_maximum_fusion.3), channel_id=1, source_target_pairs={{0,24},{1,25},{2,26},{3,27},{4,28},{5,29},{6,30},{7,31},{8,16},{9,... | collective-permute-start | bytes 393224 | tf_op jit(solution)/shard_map/ppermute | solution.py:26
  133.0 16.9 %collective-permute-start.26 = (bf16[256,512]{1,0:T(8,128)(2,1)S(1)}, bf16[256,512]{1,0:T(8,128)(2,1)S(1)}, u32[]{:S(2)}, u32[]{:S(2)}) collective-permute-start(bf16[256,512]{1,0:T(8,128)(2,1)S(1)} %pad_maximum_fusion.2.refs_0_), channel_id=1, source_target_pairs={{0,4},{1,3},{2,6},{3,1},{4,0},{5,7},{6,2},{7,5},{8,12},{9,11},{10,... | collective-permute-start | bytes 786440 | tf_op jit(solution)/shard_map/ppermute | solution.py:26
  135.0 5.0 %collective-permute-start.28 = (bf16[128,512]{1,0:T(8,128)(2,1)S(1)}, bf16[128,512]{1,0:T(8,128)(2,1)S(1)}, u32[]{:S(2)}, u32[]{:S(2)}) collective-permute-start(bf16[128,512]{1,0:T(8,128)(2,1)S(1)} %collective-permute-done.27), channel_id=1, source_target_pairs={{0,2},{1,5},{2,0},{3,7},{4,6},{5,1},{6,4},{7,3},{8,10},{9,13},{10,... | collective-permute-start | bytes 393224 | tf_op jit(solution)/shard_map/ppermute | solution.py:26
  136.2 7.3 %collective-permute-start.31 = (bf16[128,512]{1,0:T(8,128)(2,1)S(1)}, bf16[128,512]{1,0:T(8,128)(2,1)S(1)}, u32[]{:S(2)}, u32[]{:S(2)}) collective-permute-start(bf16[128,512]{1,0:T(8,128)(2,1)S(1)} %collective-permute-done.30), channel_id=1, source_target_pairs={{0,2},{1,5},{2,0},{3,7},{4,6},{5,1},{6,4},{7,3},{8,10},{9,13},{10,... | collective-permute-start | bytes 393224 | tf_op jit(solution)/shard_map/ppermute | solution.py:26
  137.2 9.0 %collective-permute-start.34 = (bf16[128,512]{1,0:T(8,128)(2,1)S(1)}, bf16[128,512]{1,0:T(8,128)(2,1)S(1)}, u32[]{:S(2)}, u32[]{:S(2)}) collective-permute-start(bf16[128,512]{1,0:T(8,128)(2,1)S(1)} %collective-permute-done.33), channel_id=1, source_target_pairs={{0,2},{1,5},{2,0},{3,7},{4,6},{5,1},{6,4},{7,3},{8,10},{9,13},{10,... | collective-permute-start | bytes 393224 | tf_op jit(solution)/shard_map/ppermute | solution.py:26
  140.1 9.8 %collective-permute-start.29 = (bf16[256,512]{1,0:T(8,128)(2,1)S(1)}, bf16[256,512]{1,0:T(8,128)(2,1)S(1)}, u32[]{:S(2)}, u32[]{:S(2)}) collective-permute-start(bf16[256,512]{1,0:T(8,128)(2,1)S(1)} %constant_dynamic-update-slice_fusion.4.refs_2_), channel_id=1, source_target_pairs={{0,4},{1,3},{2,6},{3,1},{4,0},{5,7},{6,2},{7,5},{8,12},{9,11},{10,... | collective-permute-start | bytes 786440 | tf_op jit(solution)/shard_map/ppermute | solution.py:26
  143.5 7.1 %collective-permute-start.32 = (bf16[256,512]{1,0:T(8,128)(2,1)S(1)}, bf16[256,512]{1,0:T(8,128)(2,1)S(1)}, u32[]{:S(2)}, u32[]{:S(2)}) collective-permute-start(bf16[256,512]{1,0:T(8,128)(2,1)S(1)} %constant_dynamic-update-slice_fusion.6.refs_4_), channel_id=1, source_target_pairs={{0,4},{1,3},{2,6},{3,1},{4,0},{5,7},{6,2},{7,5},{8,12},{9,11},{10,... | collective-permute-start | bytes 786440 | tf_op jit(solution)/shard_map/ppermute | solution.py:26
  146.3 7.1 %collective-permute-start.35 = (bf16[256,512]{1,0:T(8,128)(2,1)S(1)}, bf16[256,512]{1,0:T(8,128)(2,1)S(1)}, u32[]{:S(2)}, u32[]{:S(2)}) collective-permute-start(bf16[256,512]{1,0:T(8,128)(2,1)S(1)} %constant_dynamic-update-slice_fusion.8.refs_6_), channel_id=1, source_target_pairs={{0,4},{1,3},{2,6},{3,1},{4,0},{5,7},{6,2},{7,5},{8,12},{9,11},{10,... | collective-permute-start | bytes 786440 | tf_op jit(solution)/shard_map/ppermute | solution.py:26

commit v3 on v2

--- a/solution.py
+++ b/solution.py
@@ -10,6 +10,7 @@
 EPSILON = 1e-06
 LANES = 128
 KEYS_AT_ONCE = 2048
+LOG2_E = 1.4426950408889634
 MIB = 1024 * 1024
 
 
@@ -202,61 +203,90 @@
     )(place, kinds, pick, *parts, *weights)
 
 
-def attention_kernel(head_dim, group, q_ref, *refs):
-    kv_refs, out_ref = refs[:-1], refs[-1]
+def attention_kernel(head_dim, group, kv_count, resumes, ends, q_ref, *refs):
+    kv_refs, refs = refs[:kv_count], refs[kv_count:]
+    if resumes:
+        stats_in, mixed_in, refs = refs[0], refs[1], refs[2:]
+    rows = q_ref.shape[0]
     kv_heads = kv_refs[0].shape[1] // (2 * head_dim)
-    scale = head_dim**-0.5
-    rows = q_ref.shape[0]
     step = max(1, KEYS_AT_ONCE // kv_refs[0].shape[0])
+    scale = head_dim**-0.5 * LOG2_E
+
     def columns(ref, head, count=1):
         return ref[:, pl.ds(pl.multiple_of(head * head_dim, head_dim), count * head_dim)]
 
-    def two_heads(pair, carry):
-        g = pair // (group // 2)
-        both = columns(q_ref, 2 * pair, 2)
-        q = jnp.concatenate([both[:, :head_dim], both[:, head_dim:]], axis=0)
-        keys = [columns(ref, g) for ref in kv_refs]
-        vals = [columns(ref, kv_heads + g) for ref in kv_refs]
+    def one_group(g, carry):
+        wide = columns(q_ref, group * g, group)
+        q = jnp.concatenate(
+            [wide[:, i * head_dim : (i + 1) * head_dim] for i in range(group)], axis=0
+        )
         peak, total, mixed = None, 0.0, 0.0
-        for at in range(0, len(keys), step):
+        if resumes:
+            peak, total, mixed = stats_in[g, 0:1], stats_in[g, 1:2], mixed_in[g]
+        for at in range(0, kv_count, step):
             scores = [
-                lax.dot_general(q, k, (((1,), (1,)), ((), ())), preferred_element_type=jnp.float32)
-                for k in keys[at : at + step]
+                lax.dot_general(
+                    columns(ref, g), q, (((1,), (1,)), ((), ())), preferred_element_type=jnp.float32
+                )
+                for ref in kv_refs[at : at + step]
             ]
-            peaks = [jnp.max(s, axis=-1, keepdims=True) for s in scores]
+            peaks = [jnp.max(s, axis=0, keepdims=True) for s in scores]
             if peak is not None:
                 before = peak
                 peak = functools.reduce(jnp.maximum, peaks + [before])
-                shrink = jnp.exp((before - peak) * scale)
+                shrink = jnp.exp2((before - peak) * scale)
                 total, mixed = total * shrink, mixed * shrink
             else:
                 peak = functools.reduce(jnp.maximum, peaks)
-            for s, v in zip(scores, vals[at : at + step]):
-                p = jnp.exp((s - peak) * scale)
-                total = total + jnp.sum(p, axis=-1, keepdims=True)
-                mixed = mixed + jnp.dot(
-                    p.astype(jnp.bfloat16), v, preferred_element_type=jnp.float32
+            for s, ref in zip(scores, kv_refs[at : at + step]):
+                p = jnp.exp2((s - peak) * scale)
+                total = total + jnp.sum(p, axis=0, keepdims=True)
+                mixed = mixed + lax.dot_general(
+                    columns(ref, kv_heads + g),
+                    p.astype(jnp.bfloat16),
+                    (((0,), (0,)), ((), ())),
+                    preferred_element_type=jnp.float32,
                 )
-        mixed = (mixed / total).astype(jnp.bfloat16)
-        at = pl.multiple_of(2 * pair * head_dim, 2 * head_dim)
-        out_ref[:, pl.ds(at, 2 * head_dim)] = jnp.concatenate([mixed[:rows], mixed[rows:]], axis=1)
+        if ends:
+            out = (mixed / total).T.astype(jnp.bfloat16)
+            at = pl.multiple_of(group * g * head_dim, group * head_dim)
+            refs[0][:, pl.ds(at, group * head_dim)] = jnp.concatenate(
+                [out[i * rows : (i + 1) * rows] for i in range(group)], axis=1
+            )
+        else:
+            refs[0][g, 0:1] = peak
+            refs[0][g, 1:2] = total
+            refs[1][g] = mixed
         return carry
 
-    lax.fori_loop(0, kv_heads * group // 2, two_heads, 0, unroll=2 if len(kv_refs) <= 8 and step >= len(kv_refs) else 1)
-
-
-def attention_call(queries, kv_parts, head_dim, group):
+    lax.fori_loop(0, kv_heads, one_group, 0, unroll=kv_heads if kv_count <= step else 1)
+
+
+def attention_call(queries, kv_parts, head_dim, group, state, ends):
     vmem = pl.BlockSpec(memory_space=pltpu.VMEM)
     rows, width = queries.shape
     keys = sum(part.shape[0] for part in kv_parts)
+    kv_heads = width // (head_dim * group)
+    shapes = (jax.ShapeDtypeStruct((rows, width), jnp.bfloat16),)
+    if not ends:
+        shapes = (
+            jax.ShapeDtypeStruct((kv_heads, 8, group * rows), jnp.float32),
+            jax.ShapeDtypeStruct((kv_heads, head_dim, group * rows), jnp.float32),
+        )
+    state = state or ()
     return pl.pallas_call(
-        functools.partial(attention_kernel, head_dim, group),
-        out_shape=jax.ShapeDtypeStruct((rows, width), jnp.bfloat16),
-        in_specs=[vmem] * (1 + len(kv_parts)),
-        out_specs=vmem,
+        functools.partial(attention_kernel, head_dim, group, len(kv_parts), bool(state), ends),
+        out_shape=shapes,
+        in_specs=[vmem] * (1 + len(kv_parts) + len(state)),
+        out_specs=(vmem,) * len(shapes),
         compiler_params=pltpu.CompilerParams(vmem_limit_bytes=48 * MIB),
+        cost_estimate=pl.CostEstimate(
+            flops=4 * rows * keys * width,
+            bytes_accessed=4 * rows * width,
+            transcendentals=rows * keys * width // head_dim,
+        ),
         name="attention",
-    )(queries, *kv_parts)
+    )(queries, *kv_parts, *state)
 
 
 def body(
@@ -366,7 +396,8 @@
     for s in slot_order:
         pair = jnp.concatenate([arrived[s], swap(arrived[s], 1, 2)], axis=0)
         kv_parts += [pair, swap(pair, 2, 1)]
-    attended = attention_call(queries, kv_parts, head_dim, heads // kv_heads)
+    state = attention_call(queries, kv_parts[:-4], head_dim, heads // kv_heads, None, False)
+    (attended,) = attention_call(queries, kv_parts[-4:], head_dim, heads // kv_heads, state, True)
     return hidden_out, attended
 
 

time: 164 us -> 161 us (0.982); the launches traced: 162 us -> 162 us
  starting transfers between devices: 48.6 us -> 41.9 us
  waiting for transfers between devices: 65.7 us -> 70.9 us
    ppermute x33, starting transfers between devices: 48 us -> 41.3 us  [swap(): return lax.ppermute(value, ('expert', 'half'), pairs)]
    ppermute x33, waiting for transfers between devices: 64.5 us -> 69.7 us  [swap(): return lax.ppermute(value, ('expert', 'half'), pairs)]
    pallas_call x2, Pallas kernels: 18.2 us -> 20.5 us  [expert_call(): pl.pallas_call(functools.partial(expert_kernel, slots, units), out_shape=...]
    pallas_call x1 -> x2, Pallas kernels: 8.61 us -> 7.43 us  [attention_call(): pl.pallas_call(functools.partial(attention_kernel, head_dim, group, len(k...]
  transfers between devices with their start and end apart: 36 -> 36, of which waited for: 17 -> 19; matrix products, arithmetic and copies ran while one was open for 6% -> 6% of each run, Pallas kernels for 12% -> 16%
where the time goes in v3:
time: 161 us; the launch traced here: 162 us
  waiting for transfers between devices  70.9 us (44%)
  starting transfers between devices  41.9 us (26%)
  Pallas kernels  29.7 us (18%)
  local copies, waits for them, and re-layouts  9.4 us (6%)
  matrix products  5.2 us (3%)
  other arithmetic  3.47 us (2%)
    ppermute x33, waiting for transfers between devices, swap(): return lax.ppermute(value, ('expert', 'half'), pairs)  69.7 us
    ppermute x33, starting transfers between devices, swap(): return lax.ppermute(value, ('expert', 'half'), pairs)  41.3 us
    pallas_call x2, Pallas kernels, expert_call(): pl.pallas_call(functools.partial(expert_kernel, slots, units), out_shape=...  20.5 us
    unnamed x24, local copies, waits for them, and re-layouts  8.31 us
    pallas_call x2, Pallas kernels, attention_call(): pl.pallas_call(functools.partial(attention_kernel, head_dim, group, len(k...  7.43 us
    dot_general x1, matrix products, body(): queries = jnp.dot(normed, w_query, preferred_element_type=jnp.float32)  4.72 us
  transfers between devices with their start and end apart: 36, of which 19 were waited for; matrix products, arithmetic and copies ran while one was open for 6% of the time, Pallas kernels for 16%

profile of v3, /device:TPU:0, one launch (start us, length us, event | category | flops | bytes accessed | tf_op | source)
XLA Modules:
  0.0 161.7 jit_solution(2170653343220707424)
XLA Ops:
  0.7 6.4 %copy.32 = bf16[2,2048,2,384]{3,1,2,0:T(8,128)(2,1)} copy(bf16[2,2048,2,384]{3,2,1,0:T(2,128)(2,1)} %param.15) | data formatting | bytes 12582912 | tf_op args[4]
  7.0 0.5 collective-permute-start.5
  7.6 1.8 %payload.1 = bf16[64,2176]{1,0:T(8,128)(2,1)} custom-call(s32[1]{0:T(128)} %bitcast.core_ref, bf16[128,2048]{1,0:T(8,128)(2,1)} %hidden_ref.1, s32[8,128]{1,0:T(8,128)} %bitcast.39, f32[8,128]{1,0:T(8,128)} %bitcast.40), custom_call_target="tpu_custom_call" | custom-call | tf_op jit(solution)/shard_map/payload/pallas_call | solution.py:58
  9.4 2.9 %collective-permute-start = (bf16[64,2176]{1,0:T(8,128)(2,1)}, bf16[64,2176]{1,0:T(8,128)(2,1)}, u32[]{:S(2)}, u32[]{:S(2)}) collective-permute-start(bf16[64,2176]{1,0:T(8,128)(2,1)} %payload.1), channel_id=1, source_target_pairs={{0,2},{1,5},{2,0},{3,7},{4,6},{5,1},{6,4},{7,3},{8,10},{9,13},{10,... | collective-permute-start | bytes 835592 | tf_op jit(solution)/shard_map/ppermute | solution.py:27
  12.3 2.6 %collective-permute-start.2 = (bf16[64,2176]{1,0:T(8,128)(2,1)}, bf16[64,2176]{1,0:T(8,128)(2,1)}, u32[]{:S(2)}, u32[]{:S(2)}) collective-permute-start(bf16[64,2176]{1,0:T(8,128)(2,1)} %payload.1), channel_id=1, source_target_pairs={{0,16},{1,17},{2,18},{3,19},{4,20},{5,21},{6,22},{7,23},{8,24},{9,... | collective-permute-start | bytes 835592 | tf_op jit(solution)/shard_map/ppermute | solution.py:27
  14.9 1.6 collective-permute-start.9
  16.6 0.5 collective-permute-done
  17.1 1.1 pad_maximum_fusion.refs_0_
  18.2 2.1 %collective-permute-start.1 = (bf16[128,2176]{1,0:T(8,128)(2,1)S(1)}, bf16[128,2176]{1,0:T(8,128)(2,1)S(1)}, u32[]{:S(2)}, u32[]{:S(2)}) collective-permute-start(bf16[128,2176]{1,0:T(8,128)(2,1)S(1)} %pad_maximum_fusion.refs_0_), channel_id=1, source_target_pairs={{0,4},{1,3},{2,6},{3,1},{4,0},{5,7},{6,2},{7,5},{8,12},{9,11},{10,... | collective-permute-start | bytes 1671176 | tf_op jit(solution)/shard_map/ppermute | solution.py:27
  20.3 7.6 %collective-permute-done.2 = bf16[64,2176]{1,0:T(8,128)(2,1)} collective-permute-done((bf16[64,2176]{1,0:T(8,128)(2,1)}, bf16[64,2176]{1,0:T(8,128)(2,1)}, u32[]{:S(2)}, u32[]{:S(2)}) %collective-permute-start.2) | collective-permute-done | bytes 278560 | tf_op jit(solution)/shard_map/ppermute | solution.py:27
  27.9 1.4 collective-permute-start.3
  29.3 1.0 constant_dynamic-update-slice_fusion.1
  30.3 3.6 %collective-permute-start.12 = (bf16[64,2176]{1,0:T(8,128)(2,1)}, bf16[64,2176]{1,0:T(8,128)(2,1)S(1)}, u32[]{:S(2)}, u32[]{:S(2)}) collective-permute-start(bf16[64,2176]{1,0:T(8,128)(2,1)} %payload.1), channel_id=1, source_target_pairs={{0,24},{1,25},{2,26},{3,27},{4,28},{5,29},{6,30},{7,31},{8,16},{9,... | collective-permute-start | bytes 835592 | tf_op jit(solution)/shard_map/ppermute | solution.py:27
  33.9 0.8 collective-permute-done.3
  34.7 1.4 collective-permute-start.10
  36.1 0.7 collective-permute-start.4
  36.8 2.9 %collective-permute-done.12 = bf16[64,2176]{1,0:T(8,128)(2,1)S(1)} collective-permute-done((bf16[64,2176]{1,0:T(8,128)(2,1)}, bf16[64,2176]{1,0:T(8,128)(2,1)S(1)}, u32[]{:S(2)}, u32[]{:S(2)}) %collective-permute-start.12) | collective-permute-done | bytes 278560 | tf_op jit(solution)/shard_map/ppermute | solution.py:27
  39.8 4.5 %collective-permute-done.10 = bf16[64,2176]{1,0:T(8,128)(2,1)S(1)} collective-permute-done((bf16[64,2176]{1,0:T(8,128)(2,1)S(1)}, bf16[64,2176]{1,0:T(8,128)(2,1)S(1)}, u32[]{:S(2)}, u32[]{:S(2)}) %collective-permute-start.10) | collective-permute-done | bytes 278560 | tf_op jit(solution)/shard_map/ppermute | solution.py:27
  44.3 1.4 collective-permute-start.13
  45.7 3.0 %collective-permute-done.4.refs_3_ = bf16[128,2176]{1,0:T(8,128)(2,1)S(1)} collective-permute-done((bf16[128,2176]{1,0:T(8,128)(2,1)S(1)}, bf16[128,2176]{1,0:T(8,128)(2,1)S(1)}, u32[]{:S(2)}, u32[]{:S(2)}) %collective-permute-start.4) | collective-permute-done | bytes 557088 | tf_op jit(solution)/shard_map/ppermute | solution.py:27
  48.7 0.6 collective-permute-start.11
  49.3 9.6 %experts.2 = (f32[128,2048]{1,0:T(8,128)S(1)}, bf16[128,2048]{1,0:T(8,128)(2,1)S(1)}, f32[128,2048]{1,0:T(8,128)S(1)}, bf16[128,2048]{1,0:T(8,128)(2,1)S(1)}) custom-call(s32[2]{0:T(128)S(1)} %pad_add_fusion.place_ref, s32[16]{0:T(128)S(1)} %slice_reduce_fusion.kind_ref, f32[1,128]{1,0:T(1,128)S(1)} %or_convert_fusion.pick_ref, ...), custom_call_target="tpu_custom_call" | custom-call | tf_op jit(solution)/shard_map/experts/pallas_call | solution.py:188
  58.9 1.4 collective-permute-start.18
  60.4 0.7 collective-permute-start.14
  61.1 1.4 collective-permute-start.7
  62.5 6.2 %collective-permute-done.18 = bf16[128,2048]{1,0:T(8,128)(2,1)S(1)} collective-permute-done((bf16[128,2048]{1,0:T(8,128)(2,1)S(1)}, bf16[128,2048]{1,0:T(8,128)(2,1)S(1)}, u32[]{:S(2)}, u32[]{:S(2)}) %collective-permute-start.18) | collective-permute-done | bytes 524320 | tf_op jit(solution)/shard_map/ppermute | solution.py:27
  68.8 0.4 collective-permute-start.19
  69.2 7.7 %collective-permute-done.14.refs_3_ = bf16[128,2176]{1,0:T(8,128)(2,1)S(1)} collective-permute-done((bf16[128,2176]{1,0:T(8,128)(2,1)S(1)}, bf16[128,2176]{1,0:T(8,128)(2,1)S(1)}, u32[]{:S(2)}, u32[]{:S(2)}) %collective-permute-start.14) | collective-permute-done | bytes 557088 | tf_op jit(solution)/shard_map/ppermute | solution.py:27
  76.9 10.9 %experts.3 = (f32[128,2048]{1,0:T(8,128)S(1)}, bf16[128,2048]{1,0:T(8,128)(2,1)S(1)}, f32[128,2048]{1,0:T(8,128)S(1)}, bf16[128,2048]{1,0:T(8,128)(2,1)S(1)}) custom-call(s32[2]{0:T(128)S(1)} %pad_add_fusion.place_ref, s32[16]{0:T(128)S(1)} %slice_reduce_fusion.kind_ref, f32[1,128]{1,0:T(1,128)S(1)} %or_convert_fusion.pick_ref, ...), custom_call_target="tpu_custom_call" | custom-call | tf_op jit(solution)/shard_map/experts/pallas_call | solution.py:188
  87.8 1.4 collective-permute-start.21
  89.5 1.0 collective-permute-start.8
  90.6 9.3 %collective-permute-done.21 = bf16[128,2048]{1,0:T(8,128)(2,1)S(1)} collective-permute-done((bf16[128,2048]{1,0:T(8,128)(2,1)S(1)}, bf16[128,2048]{1,0:T(8,128)(2,1)S(1)}, u32[]{:S(2)}, u32[]{:S(2)}) %collective-permute-start.21) | collective-permute-done | bytes 524320 | tf_op jit(solution)/shard_map/ppermute | solution.py:27
  100.1 0.4 collective-permute-start.22
  100.4 7.9 %collective-permute-done.15 = bf16[128,2048]{1,0:T(8,128)(2,1)S(1)} collective-permute-done((bf16[128,2048]{1,0:T(8,128)(2,1)S(1)}, bf16[128,2048]{1,0:T(8,128)(2,1)S(1)}, u32[]{:S(2)}, u32[]{:S(2)}) %collective-permute-start.15) | collective-permute-done | bytes 524320 | tf_op jit(solution)/shard_map/ppermute | solution.py:27
  108.5 0.4 collective-permute-start.16
  108.9 3.4 %collective-permute-start.23 = (bf16[64,2048]{1,0:T(8,128)(2,1)S(1)}, bf16[64,2048]{1,0:T(8,128)(2,1)S(1)}, u32[]{:S(2)}, u32[]{:S(2)}) collective-permute-start(bf16[64,2048]{1,0:T(8,128)(2,1)S(1)} %fusion.2), channel_id=1, source_target_pairs={{0,24},{1,25},{2,26},{3,27},{4,28},{5,29},{6,30},{7,31},{8,16},{9,... | collective-permute-start | bytes 786440 | tf_op jit(solution)/shard_map/ppermute | solution.py:27
  112.4 2.5 %collective-permute-done.16 = bf16[64,2048]{1,0:T(8,128)(2,1)S(1)} collective-permute-done((bf16[64,2048]{1,0:T(8,128)(2,1)S(1)}, bf16[64,2048]{1,0:T(8,128)(2,1)S(1)}, u32[]{:S(2)}, u32[]{:S(2)}) %collective-permute-start.16) | collective-permute-done | bytes 262176 | tf_op jit(solution)/shard_map/ppermute | solution.py:27
  115.1 2.1 %collective-permute-done.23 = bf16[64,2048]{1,0:T(8,128)(2,1)S(1)} collective-permute-done((bf16[64,2048]{1,0:T(8,128)(2,1)S(1)}, bf16[64,2048]{1,0:T(8,128)(2,1)S(1)}, u32[]{:S(2)}, u32[]{:S(2)}) %collective-permute-start.23) | collective-permute-done | bytes 262176 | tf_op jit(solution)/shard_map/ppermute | solution.py:27
  117.2 4.2 %collective-permute-done.17 = bf16[64,2048]{1,0:T(8,128)(2,1)S(1)} collective-permute-done((bf16[64,2048]{1,0:T(8,128)(2,1)S(1)}, bf16[64,2048]{1,0:T(8,128)(2,1)S(1)}, u32[]{:S(2)}, u32[]{:S(2)}) %collective-permute-start.17) | collective-permute-done | bytes 262176 | tf_op jit(solution)/shard_map/ppermute | solution.py:27
  121.7 0.5 copy.26
  122.4 1.2 collective-permute-done.24
  123.8 0.5 fusion.11
  124.4 0.2 reduce_sum.29
  125.1 3.3 %collective-permute-start.28 = (bf16[128,512]{1,0:T(8,128)(2,1)S(1)}, bf16[128,512]{1,0:T(8,128)(2,1)S(1)}, u32[]{:S(2)}, u32[]{:S(2)}) collective-permute-start(bf16[128,512]{1,0:T(8,128)(2,1)S(1)} %pad_maximum_fusion.3), channel_id=1, source_target_pairs={{0,24},{1,25},{2,26},{3,27},{4,28},{5,29},{6,30},{7,31},{8,16},{9,... | collective-permute-start | bytes 393224 | tf_op jit(solution)/shard_map/ppermute | solution.py:27
  128.4 0.3 collective-permute-start.31
  128.8 0.5 collective-permute-start.33
  129.2 4.7 %fusion.12 = f32[128,2048]{1,0:T(8,128)S(1)} fusion(bf16[2048,2048]{1,0:T(8,128)(2,1)} %param.18, f32[128,2048]{1,0:T(8,128)S(1)} %get-tuple-element.37, f32[2048]{0:T(1024)S(1)} %copy-done.5, f32[128]{0:T(128)S(1)} %add_rsqrt_fusion.2), kind=kOutput, calls=%fused_computation.55 | convolution fusion | flops 1074528256 | bytes 10494464 | tf_op jit(solution)/shard_map/dot_general | solution.py:387
  134.3 0.3 reduce_sum.28
  134.8 2.1 %collective-permute-start.32 = (bf16[256,512]{1,0:T(8,128)(2,1)S(1)}, bf16[256,512]{1,0:T(8,128)(2,1)S(1)}, u32[]{:S(2)}, u32[]{:S(2)}) collective-permute-start(bf16[256,512]{1,0:T(8,128)(2,1)S(1)} %pad_maximum_fusion.2.refs_0_), channel_id=1, source_target_pairs={{0,4},{1,3},{2,6},{3,1},{4,0},{5,7},{6,2},{7,5},{8,12},{9,11},{10,... | collective-permute-start | bytes 786440 | tf_op jit(solution)/shard_map/ppermute | solution.py:27
  136.9 1.3 collective-permute-start.26
  138.2 0.9 collective-permute-start.29
  139.1 1.8 %collective-permute-done.33 = bf16[128,512]{1,0:T(8,128)(2,1)S(1)} collective-permute-done((bf16[128,512]{1,0:T(8,128)(2,1)S(1)}, bf16[128,512]{1,0:T(8,128)(2,1)S(1)}, u32[]{:S(2)}, u32[]{:S(2)}) %collective-permute-start.33) | collective-permute-done | bytes 131104 | tf_op jit(solution)/shard_map/ppermute | solution.py:27
  140.9 0.4 collective-permute-start.34
  141.3 0.9 collective-permute-done.26
  142.2 1.1 collective-permute-start.27
  143.3 0.2 collective-permute-done.29
  143.6 0.8 collective-permute-start.30
  144.4 2.9 %collective-permute-done.34 = bf16[128,512]{1,0:T(8,128)(2,1)S(1)} collective-permute-done((bf16[128,512]{1,0:T(8,128)(2,1)S(1)}, bf16[128,512]{1,0:T(8,128)(2,1)S(1)}, u32[]{:S(2)}, u32[]{:S(2)}) %collective-permute-start.34) | collective-permute-done | bytes 131104 | tf_op jit(solution)/shard_map/ppermute | solution.py:27
  147.3 1.5 collective-permute-start.35
  148.9 0.3 mul.86
  149.2 0.5 fusion.1.q_ref
  149.7 4.6 %collective-permute-done.35.refs_3_ = bf16[256,512]{1,0:T(8,128)(2,1)S(1)} collective-permute-done((bf16[256,512]{1,0:T(8,128)(2,1)S(1)}, bf16[256,512]{1,0:T(8,128)(2,1)S(1)}, u32[]{:S(2)}, u32[]{:S(2)}) %collective-permute-start.35) | collective-permute-done | bytes 262176 | tf_op jit(solution)/shard_map/ppermute | solution.py:27
  154.3 3.4 %attention.2 = (f32[2,8,1024]{2,1,0:T(8,128)S(1)}, f32[2,128,1024]{2,1,0:T(8,128)S(1)}) custom-call(bf16[128,2048]{1,0:T(8,128)(2,1)S(1)} %fusion.1.q_ref, bf16[256,512]{1,0:T(8,128)(2,1)S(1)} %pad_maximum_fusion.2.refs_0_, bf16[256,512]{1,0:T(8,128)(2,1)S(1)} %collective-permute-done.32.refs_1_, ...), custom_call_target="tpu_custom_call" | custom-call | flops 1073741824 | bytes 1048576 | tf_op jit(solution)/shard_map/attention/pallas_call | solution.py:277
  157.7 4.0 %attention.3 = bf16[128,2048]{1,0:T(8,128)(2,1)} custom-call(bf16[128,2048]{1,0:T(8,128)(2,1)S(1)} %fusion.1.q_ref, bf16[256,512]{1,0:T(8,128)(2,1)S(1)} %constant_dynamic-update-slice_fusion.4.refs_0_, bf16[256,512]{1,0:T(8,128)(2,1)S(1)} %collective-permute-done.27.refs_1_, bf16[256,512]{1,0:T(8,128)(2,1)S(1)} %constant_dynamic-update-slice_fusion.6.refs_2_, ...), custom_call_target="tpu_custom_call" | custom-call | flops 1073741824 | bytes 1048576 | tf_op jit(solution)/shard_map/attention/pallas_call | solution.py:277
  (81 shorter events, 3.1 us)
Async XLA Ops:
  0.6 121.8 %copy-start = (f32[128]{0:T(128)S(1)}, f32[128]{0:T(128)}, u32[]{:S(2)}) copy-start(f32[128]{0:T(128)} %param.20) | copy-start | bytes 1540
  0.6 6.9 %copy-start.1 = (bf16[2,384,2048]{2,1,0:T(8,128)(2,1)S(1)}, bf16[2,384,2048]{2,1,0:T(8,128)(2,1)}, u32[]{:S(2)}) copy-start(bf16[2,384,2048]{2,1,0:T(8,128)(2,1)} %refs_6_.3) | copy-start | bytes 9437188
  0.7 15.9 %copy-start.6 = (s32[2048]{0:T(1024)S(1)}, s32[2048]{0:T(1024)}, u32[]{:S(2)}) copy-start(s32[2048]{0:T(1024)} %param.12) | copy-start | bytes 24580
  7.0 42.3 %collective-permute-start.5 = (bf16[2,2,2048,384]{3,2,1,0:T(8,128)(2,1)}, bf16[2,2,2048,384]{3,2,1,0:T(8,128)(2,1)}, u32[]{:S(2)}, u32[]{:S(2)}) collective-permute-start(bf16[2,2,2048,384]{3,2,1,0:T(8,128)(2,1)} %bitcast.32.refs_4_), channel_id=1, source_target_pairs={{0,1},{1,0},{2,3},{3,2},{4,5},{5,4},{6,7},{7,6},{8,9},{9,8},{10,11... | collective-permute-start | bytes 18874376 | tf_op jit(solution)/shard_map/ppermute | solution.py:35
  7.5 41.8 %collective-permute-start.6 = (bf16[2,384,2048]{2,1,0:T(8,128)(2,1)S(1)}, bf16[2,384,2048]{2,1,0:T(8,128)(2,1)}, u32[]{:S(2)}, u32[]{:S(2)}) collective-permute-start(bf16[2,384,2048]{2,1,0:T(8,128)(2,1)S(1)} %copy-done.1), channel_id=1, source_target_pairs={{0,1},{1,0},{2,3},{3,2},{4,5},{5,4},{6,7},{7,6},{8,9},{9,8},{10,11... | collective-permute-start | bytes 9437192 | tf_op jit(solution)/shard_map/ppermute | solution.py:35
  9.4 7.8 %collective-permute-start = (bf16[64,2176]{1,0:T(8,128)(2,1)}, bf16[64,2176]{1,0:T(8,128)(2,1)}, u32[]{:S(2)}, u32[]{:S(2)}) collective-permute-start(bf16[64,2176]{1,0:T(8,128)(2,1)} %payload.1), channel_id=1, source_target_pairs={{0,2},{1,5},{2,0},{3,7},{4,6},{5,1},{6,4},{7,3},{8,10},{9,13},{10,... | collective-permute-start | bytes 835592 | tf_op jit(solution)/shard_map/ppermute | solution.py:27
  12.3 15.6 %collective-permute-start.2 = (bf16[64,2176]{1,0:T(8,128)(2,1)}, bf16[64,2176]{1,0:T(8,128)(2,1)}, u32[]{:S(2)}, u32[]{:S(2)}) collective-permute-start(bf16[64,2176]{1,0:T(8,128)(2,1)} %payload.1), channel_id=1, source_target_pairs={{0,16},{1,17},{2,18},{3,19},{4,20},{5,21},{6,22},{7,23},{8,24},{9,... | collective-permute-start | bytes 835592 | tf_op jit(solution)/shard_map/ppermute | solution.py:27
  14.9 15.4 %collective-permute-start.9 = (bf16[64,2176]{1,0:T(8,128)(2,1)}, bf16[64,2176]{1,0:T(8,128)(2,1)S(1)}, u32[]{:S(2)}, u32[]{:S(2)}) collective-permute-start(bf16[64,2176]{1,0:T(8,128)(2,1)} %payload.1), channel_id=1, source_target_pairs={{0,8},{1,9},{2,10},{3,11},{4,12},{5,13},{6,14},{7,15},{8,0},{9,1},... | collective-permute-start | bytes 835592 | tf_op jit(solution)/shard_map/ppermute | solution.py:27
  18.2 17.9 %collective-permute-start.1 = (bf16[128,2176]{1,0:T(8,128)(2,1)S(1)}, bf16[128,2176]{1,0:T(8,128)(2,1)S(1)}, u32[]{:S(2)}, u32[]{:S(2)}) collective-permute-start(bf16[128,2176]{1,0:T(8,128)(2,1)S(1)} %pad_maximum_fusion.refs_0_), channel_id=1, source_target_pairs={{0,4},{1,3},{2,6},{3,1},{4,0},{5,7},{6,2},{7,5},{8,12},{9,11},{10,... | collective-permute-start | bytes 1671176 | tf_op jit(solution)/shard_map/ppermute | solution.py:27
  27.9 6.8 %collective-permute-start.3 = (bf16[64,2176]{1,0:T(8,128)(2,1)}, bf16[64,2176]{1,0:T(8,128)(2,1)S(1)}, u32[]{:S(2)}, u32[]{:S(2)}) collective-permute-start(bf16[64,2176]{1,0:T(8,128)(2,1)} %collective-permute-done.2), channel_id=1, source_target_pairs={{0,2},{1,5},{2,0},{3,7},{4,6},{5,1},{6,4},{7,3},{8,10},{9,13},{10,... | collective-permute-start | bytes 835592 | tf_op jit(solution)/shard_map/ppermute | solution.py:27
  30.3 9.5 %collective-permute-start.12 = (bf16[64,2176]{1,0:T(8,128)(2,1)}, bf16[64,2176]{1,0:T(8,128)(2,1)S(1)}, u32[]{:S(2)}, u32[]{:S(2)}) collective-permute-start(bf16[64,2176]{1,0:T(8,128)(2,1)} %payload.1), channel_id=1, source_target_pairs={{0,24},{1,25},{2,26},{3,27},{4,28},{5,29},{6,30},{7,31},{8,16},{9,... | collective-permute-start | bytes 835592 | tf_op jit(solution)/shard_map/ppermute | solution.py:27
  34.7 9.6 %collective-permute-start.10 = (bf16[64,2176]{1,0:T(8,128)(2,1)S(1)}, bf16[64,2176]{1,0:T(8,128)(2,1)S(1)}, u32[]{:S(2)}, u32[]{:S(2)}) collective-permute-start(bf16[64,2176]{1,0:T(8,128)(2,1)S(1)} %collective-permute-done.9), channel_id=1, source_target_pairs={{0,2},{1,5},{2,0},{3,7},{4,6},{5,1},{6,4},{7,3},{8,10},{9,13},{10,... | collective-permute-start | bytes 835592 | tf_op jit(solution)/shard_map/ppermute | solution.py:27
  36.1 12.6 %collective-permute-start.4 = (bf16[128,2176]{1,0:T(8,128)(2,1)S(1)}, bf16[128,2176]{1,0:T(8,128)(2,1)S(1)}, u32[]{:S(2)}, u32[]{:S(2)}) collective-permute-start(bf16[128,2176]{1,0:T(8,128)(2,1)S(1)} %constant_dynamic-update-slice_fusion.refs_2_), channel_id=1, source_target_pairs={{0,4},{1,3},{2,6},{3,1},{4,0},{5,7},{6,2},{7,5},{8,12},{9,11},{10,... | collective-permute-start | bytes 1671176 | tf_op jit(solution)/shard_map/ppermute | solution.py:27
  44.3 16.1 %collective-permute-start.13 = (bf16[64,2176]{1,0:T(8,128)(2,1)S(1)}, bf16[64,2176]{1,0:T(8,128)(2,1)S(1)}, u32[]{:S(2)}, u32[]{:S(2)}) collective-permute-start(bf16[64,2176]{1,0:T(8,128)(2,1)S(1)} %collective-permute-done.12), channel_id=1, source_target_pairs={{0,2},{1,5},{2,0},{3,7},{4,6},{5,1},{6,4},{7,3},{8,10},{9,13},{10,... | collective-permute-start | bytes 835592 | tf_op jit(solution)/shard_map/ppermute | solution.py:27
  48.7 11.7 %collective-permute-start.11 = (bf16[128,2176]{1,0:T(8,128)(2,1)S(1)}, bf16[128,2176]{1,0:T(8,128)(2,1)S(1)}, u32[]{:S(2)}, u32[]{:S(2)}) collective-permute-start(bf16[128,2176]{1,0:T(8,128)(2,1)S(1)} %constant_dynamic-update-slice_fusion.2.refs_0_), channel_id=1, source_target_pairs={{0,4},{1,3},{2,6},{3,1},{4,0},{5,7},{6,2},{7,5},{8,12},{9,11},{10,... | collective-permute-start | bytes 1671176 | tf_op jit(solution)/shard_map/ppermute | solution.py:27
  58.9 9.8 %collective-permute-start.18 = (bf16[128,2048]{1,0:T(8,128)(2,1)S(1)}, bf16[128,2048]{1,0:T(8,128)(2,1)S(1)}, u32[]{:S(2)}, u32[]{:S(2)}) collective-permute-start(bf16[128,2048]{1,0:T(8,128)(2,1)S(1)} %get-tuple-element.31), channel_id=1, source_target_pairs={{0,4},{1,3},{2,6},{3,1},{4,0},{5,7},{6,2},{7,5},{8,12},{9,11},{10,... | collective-permute-start | bytes 1572872 | tf_op jit(solution)/shard_map/ppermute | solution.py:27
  60.4 16.5 %collective-permute-start.14 = (bf16[128,2176]{1,0:T(8,128)(2,1)S(1)}, bf16[128,2176]{1,0:T(8,128)(2,1)S(1)}, u32[]{:S(2)}, u32[]{:S(2)}) collective-permute-start(bf16[128,2176]{1,0:T(8,128)(2,1)S(1)} %pad_maximum_fusion.1.refs_2_), channel_id=1, source_target_pairs={{0,4},{1,3},{2,6},{3,1},{4,0},{5,7},{6,2},{7,5},{8,12},{9,11},{10,... | collective-permute-start | bytes 1671176 | tf_op jit(solution)/shard_map/ppermute | solution.py:27
  61.1 28.2 %collective-permute-start.7 = (bf16[128,2048]{1,0:T(8,128)(2,1)S(1)}, bf16[128,2048]{1,0:T(8,128)(2,1)S(1)}, u32[]{:S(2)}, u32[]{:S(2)}) collective-permute-start(bf16[128,2048]{1,0:T(8,128)(2,1)S(1)} %get-tuple-element.22), channel_id=1, source_target_pairs={{0,4},{1,3},{2,6},{3,1},{4,0},{5,7},{6,2},{7,5},{8,12},{9,11},{10,... | collective-permute-start | bytes 1572872 | tf_op jit(solution)/shard_map/ppermute | solution.py:27
  68.8 21.7 %collective-permute-start.19 = (bf16[64,2048]{1,0:T(8,128)(2,1)S(1)}, bf16[64,2048]{1,0:T(8,128)(2,1)S(1)}, u32[]{:S(2)}, u32[]{:S(2)}) collective-permute-start(bf16[64,2048]{1,0:T(8,128)(2,1)S(1)} %slice.93), channel_id=1, source_target_pairs={{0,2},{1,5},{2,0},{3,7},{4,6},{5,1},{6,4},{7,3},{8,10},{9,13},{10,... | collective-permute-start | bytes 786440 | tf_op jit(solution)/shard_map/ppermute | solution.py:27
  87.8 12.1 %collective-permute-start.21 = (bf16[128,2048]{1,0:T(8,128)(2,1)S(1)}, bf16[128,2048]{1,0:T(8,128)(2,1)S(1)}, u32[]{:S(2)}, u32[]{:S(2)}) collective-permute-start(bf16[128,2048]{1,0:T(8,128)(2,1)S(1)} %get-tuple-element.33), channel_id=1, source_target_pairs={{0,4},{1,3},{2,6},{3,1},{4,0},{5,7},{6,2},{7,5},{8,12},{9,11},{10,... | collective-permute-start | bytes 1572872 | tf_op jit(solution)/shard_map/ppermute | solution.py:27
  89.5 25.6 %collective-permute-start.8 = (bf16[64,2048]{1,0:T(8,128)(2,1)S(1)}, bf16[64,2048]{1,0:T(8,128)(2,1)S(1)}, u32[]{:S(2)}, u32[]{:S(2)}) collective-permute-start(bf16[64,2048]{1,0:T(8,128)(2,1)S(1)} %slice.95), channel_id=1, source_target_pairs={{0,2},{1,5},{2,0},{3,7},{4,6},{5,1},{6,4},{7,3},{8,10},{9,13},{10,... | collective-permute-start | bytes 786440 | tf_op jit(solution)/shard_map/ppermute | solution.py:27
  90.5 17.8 %collective-permute-start.15 = (bf16[128,2048]{1,0:T(8,128)(2,1)S(1)}, bf16[128,2048]{1,0:T(8,128)(2,1)S(1)}, u32[]{:S(2)}, u32[]{:S(2)}) collective-permute-start(bf16[128,2048]{1,0:T(8,128)(2,1)S(1)} %get-tuple-element.30), channel_id=1, source_target_pairs={{0,4},{1,3},{2,6},{3,1},{4,0},{5,7},{6,2},{7,5},{8,12},{9,11},{10,... | collective-permute-start | bytes 1572872 | tf_op jit(solution)/shard_map/ppermute | solution.py:27
  90.6 24.5 %collective-permute-start.20 = (bf16[64,2048]{1,0:T(8,128)(2,1)S(1)}, bf16[64,2048]{1,0:T(8,128)(2,1)S(1)}, u32[]{:S(2)}, u32[]{:S(2)}) collective-permute-start(bf16[64,2048]{1,0:T(8,128)(2,1)S(1)} %fusion.3), channel_id=1, source_target_pairs={{0,16},{1,17},{2,18},{3,19},{4,20},{5,21},{6,22},{7,23},{8,24},{9,... | collective-permute-start | bytes 786440 | tf_op jit(solution)/shard_map/ppermute | solution.py:27
  100.1 8.8 %collective-permute-start.22 = (bf16[64,2048]{1,0:T(8,128)(2,1)S(1)}, bf16[64,2048]{1,0:T(8,128)(2,1)S(1)}, u32[]{:S(2)}, u32[]{:S(2)}) collective-permute-start(bf16[64,2048]{1,0:T(8,128)(2,1)S(1)} %slice.92), channel_id=1, source_target_pairs={{0,2},{1,5},{2,0},{3,7},{4,6},{5,1},{6,4},{7,3},{8,10},{9,13},{10,... | collective-permute-start | bytes 786440 | tf_op jit(solution)/shard_map/ppermute | solution.py:27
  108.3 13.1 %copy-start.3 = (bf16[64,2176]{1,0:T(8,128)(2,1)S(1)}, bf16[64,2176]{1,0:T(8,128)(2,1)}, u32[]{:S(2)}) copy-start(bf16[64,2176]{1,0:T(8,128)(2,1)} %payload.1) | copy-start | bytes 835588
  108.5 13.2 %copy-start.4 = (bf16[2048,2,256]{2,1,0:T(2,128)(2,1)S(1)}, bf16[2048,2,256]{2,1,0:T(2,128)(2,1)}, u32[]{:S(2)}) copy-start(bf16[2048,2,256]{2,1,0:T(2,128)(2,1)} %param.19) | copy-start | bytes 6291460
  108.5 6.4 %collective-permute-start.16 = (bf16[64,2048]{1,0:T(8,128)(2,1)S(1)}, bf16[64,2048]{1,0:T(8,128)(2,1)S(1)}, u32[]{:S(2)}, u32[]{:S(2)}) collective-permute-start(bf16[64,2048]{1,0:T(8,128)(2,1)S(1)} %slice.94), channel_id=1, source_target_pairs={{0,2},{1,5},{2,0},{3,7},{4,6},{5,1},{6,4},{7,3},{8,10},{9,13},{10,... | collective-permute-start | bytes 786440 | tf_op jit(solution)/shard_map/ppermute | solution.py:27
  108.9 8.2 %collective-permute-start.23 = (bf16[64,2048]{1,0:T(8,128)(2,1)S(1)}, bf16[64,2048]{1,0:T(8,128)(2,1)S(1)}, u32[]{:S(2)}, u32[]{:S(2)}) collective-permute-start(bf16[64,2048]{1,0:T(8,128)(2,1)S(1)} %fusion.2), channel_id=1, source_target_pairs={{0,24},{1,25},{2,26},{3,27},{4,28},{5,29},{6,30},{7,31},{8,16},{9,... | collective-permute-start | bytes 786440 | tf_op jit(solution)/shard_map/ppermute | solution.py:27
  115.0 6.4 %collective-permute-start.17 = (bf16[64,2048]{1,0:T(8,128)(2,1)S(1)}, bf16[64,2048]{1,0:T(8,128)(2,1)S(1)}, u32[]{:S(2)}, u32[]{:S(2)}) collective-permute-start(bf16[64,2048]{1,0:T(8,128)(2,1)S(1)} %fusion.4), channel_id=1, source_target_pairs={{0,8},{1,9},{2,10},{3,11},{4,12},{5,13},{6,14},{7,15},{8,0},{9,1},... | collective-permute-start | bytes 786440 | tf_op jit(solution)/shard_map/ppermute | solution.py:27
  121.6 2.0 %collective-permute-start.24 = (f32[64,2048]{1,0:T(8,128)S(1)}, f32[64,2048]{1,0:T(8,128)S(1)}, u32[]{:S(2)}, u32[]{:S(2)}) collective-permute-start(f32[64,2048]{1,0:T(8,128)S(1)} %fusion.8), channel_id=1, source_target_pairs={{0,1},{1,0},{2,3},{3,2},{4,5},{5,4},{6,7},{7,6},{8,9},{9,8},{10,11... | collective-permute-start | bytes 1572872 | tf_op jit(solution)/shard_map/ppermute | solution.py:35
  121.7 0.7 copy-start.7
  122.4 1.4 copy-start.5
  123.8 5.5 %copy-start.2 = (f32[128,2048]{1,0:T(8,128)}, f32[128,2048]{1,0:T(8,128)S(1)}, u32[]{:S(2)}) copy-start(f32[128,2048]{1,0:T(8,128)S(1)} %get-tuple-element.37) | copy-start | bytes 3145732
  124.9 12.0 %collective-permute-start.25 = (bf16[128,512]{1,0:T(8,128)(2,1)S(1)}, bf16[128,512]{1,0:T(8,128)(2,1)S(1)}, u32[]{:S(2)}, u32[]{:S(2)}) collective-permute-start(bf16[128,512]{1,0:T(8,128)(2,1)S(1)} %pad_maximum_fusion.3), channel_id=1, source_target_pairs={{0,8},{1,9},{2,10},{3,11},{4,12},{5,13},{6,14},{7,15},{8,0},{9,1},... | collective-permute-start | bytes 393224 | tf_op jit(solution)/shard_map/ppermute | solution.py:27
  125.1 13.1 %collective-permute-start.28 = (bf16[128,512]{1,0:T(8,128)(2,1)S(1)}, bf16[128,512]{1,0:T(8,128)(2,1)S(1)}, u32[]{:S(2)}, u32[]{:S(2)}) collective-permute-start(bf16[128,512]{1,0:T(8,128)(2,1)S(1)} %pad_maximum_fusion.3), channel_id=1, source_target_pairs={{0,24},{1,25},{2,26},{3,27},{4,28},{5,29},{6,30},{7,31},{8,16},{9,... | collective-permute-start | bytes 393224 | tf_op jit(solution)/shard_map/ppermute | solution.py:27
  128.4 6.4 %collective-permute-start.31 = (bf16[128,512]{1,0:T(8,128)(2,1)S(1)}, bf16[128,512]{1,0:T(8,128)(2,1)S(1)}, u32[]{:S(2)}, u32[]{:S(2)}) collective-permute-start(bf16[128,512]{1,0:T(8,128)(2,1)S(1)} %pad_maximum_fusion.3), channel_id=1, source_target_pairs={{0,2},{1,5},{2,0},{3,7},{4,6},{5,1},{6,4},{7,3},{8,10},{9,13},{10,... | collective-permute-start | bytes 393224 | tf_op jit(solution)/shard_map/ppermute | solution.py:27
  128.8 12.1 %collective-permute-start.33 = (bf16[128,512]{1,0:T(8,128)(2,1)S(1)}, bf16[128,512]{1,0:T(8,128)(2,1)S(1)}, u32[]{:S(2)}, u32[]{:S(2)}) collective-permute-start(bf16[128,512]{1,0:T(8,128)(2,1)S(1)} %pad_maximum_fusion.3), channel_id=1, source_target_pairs={{0,16},{1,17},{2,18},{3,19},{4,20},{5,21},{6,22},{7,23},{8,24},{9,... | collective-permute-start | bytes 393224 | tf_op jit(solution)/shard_map/ppermute | solution.py:27
  134.8 14.9 %collective-permute-start.32 = (bf16[256,512]{1,0:T(8,128)(2,1)S(1)}, bf16[256,512]{1,0:T(8,128)(2,1)S(1)}, u32[]{:S(2)}, u32[]{:S(2)}) collective-permute-start(bf16[256,512]{1,0:T(8,128)(2,1)S(1)} %pad_maximum_fusion.2.refs_0_), channel_id=1, source_target_pairs={{0,4},{1,3},{2,6},{3,1},{4,0},{5,7},{6,2},{7,5},{8,12},{9,11},{10,... | collective-permute-start | bytes 786440 | tf_op jit(solution)/shard_map/ppermute | solution.py:27
  136.9 5.3 %collective-permute-start.26 = (bf16[128,512]{1,0:T(8,128)(2,1)S(1)}, bf16[128,512]{1,0:T(8,128)(2,1)S(1)}, u32[]{:S(2)}, u32[]{:S(2)}) collective-permute-start(bf16[128,512]{1,0:T(8,128)(2,1)S(1)} %collective-permute-done.25), channel_id=1, source_target_pairs={{0,2},{1,5},{2,0},{3,7},{4,6},{5,1},{6,4},{7,3},{8,10},{9,13},{10,... | collective-permute-start | bytes 393224 | tf_op jit(solution)/shard_map/ppermute | solution.py:27
  138.2 5.4 %collective-permute-start.29 = (bf16[128,512]{1,0:T(8,128)(2,1)S(1)}, bf16[128,512]{1,0:T(8,128)(2,1)S(1)}, u32[]{:S(2)}, u32[]{:S(2)}) collective-permute-start(bf16[128,512]{1,0:T(8,128)(2,1)S(1)} %collective-permute-done.28), channel_id=1, source_target_pairs={{0,2},{1,5},{2,0},{3,7},{4,6},{5,1},{6,4},{7,3},{8,10},{9,13},{10,... | collective-permute-start | bytes 393224 | tf_op jit(solution)/shard_map/ppermute | solution.py:27
  140.9 6.4 %collective-permute-start.34 = (bf16[128,512]{1,0:T(8,128)(2,1)S(1)}, bf16[128,512]{1,0:T(8,128)(2,1)S(1)}, u32[]{:S(2)}, u32[]{:S(2)}) collective-permute-start(bf16[128,512]{1,0:T(8,128)(2,1)S(1)} %collective-permute-done.33), channel_id=1, source_target_pairs={{0,2},{1,5},{2,0},{3,7},{4,6},{5,1},{6,4},{7,3},{8,10},{9,13},{10,... | collective-permute-start | bytes 393224 | tf_op jit(solution)/shard_map/ppermute | solution.py:27
  142.2 15.5 %collective-permute-start.27 = (bf16[256,512]{1,0:T(8,128)(2,1)S(1)}, bf16[256,512]{1,0:T(8,128)(2,1)S(1)}, u32[]{:S(2)}, u32[]{:S(2)}) collective-permute-start(bf16[256,512]{1,0:T(8,128)(2,1)S(1)} %constant_dynamic-update-slice_fusion.4.refs_0_), channel_id=1, source_target_pairs={{0,4},{1,3},{2,6},{3,1},{4,0},{5,7},{6,2},{7,5},{8,12},{9,11},{10,... | collective-permute-start | bytes 786440 | tf_op jit(solution)/shard_map/ppermute | solution.py:27
  143.6 14.1 %collective-permute-start.30 = (bf16[256,512]{1,0:T(8,128)(2,1)S(1)}, bf16[256,512]{1,0:T(8,128)(2,1)S(1)}, u32[]{:S(2)}, u32[]{:S(2)}) collective-permute-start(bf16[256,512]{1,0:T(8,128)(2,1)S(1)} %constant_dynamic-update-slice_fusion.6.refs_2_), channel_id=1, source_target_pairs={{0,4},{1,3},{2,6},{3,1},{4,0},{5,7},{6,2},{7,5},{8,12},{9,11},{10,... | collective-permute-start | bytes 786440 | tf_op jit(solution)/shard_map/ppermute | solution.py:27
  147.3 6.9 %collective-permute-start.35 = (bf16[256,512]{1,0:T(8,128)(2,1)S(1)}, bf16[256,512]{1,0:T(8,128)(2,1)S(1)}, u32[]{:S(2)}, u32[]{:S(2)}) collective-permute-start(bf16[256,512]{1,0:T(8,128)(2,1)S(1)} %constant_dynamic-update-slice_fusion.8.refs_2_), channel_id=1, source_target_pairs={{0,4},{1,3},{2,6},{3,1},{4,0},{5,7},{6,2},{7,5},{8,12},{9,11},{10,... | collective-permute-start | bytes 786440 | tf_op jit(solution)/shard_map/ppermute | solution.py:27

commit v4 on v3

--- a/solution.py
+++ b/solution.py
@@ -389,9 +389,11 @@
     queries = rms_scale(queries.reshape(tok_rows, heads, head_dim), q_gain)
     queries = queries.reshape(tok_rows, heads * head_dim).astype(jnp.bfloat16)
 
-    arrived = {0: own_kv}
-    for s in range(1, slots):
-        arrived[s] = swap(own_kv, 4 * s, 4 * s)
+    arrived, bit = {0: own_kv}, slots // 2
+    while bit:
+        for s in sorted(arrived):
+            arrived[s + bit] = swap(arrived[s], 4 * bit, 4 * bit)
+        bit //= 2
     kv_parts = []
     for s in slot_order:
         pair = jnp.concatenate([arrived[s], swap(arrived[s], 1, 2)], axis=0)

time: 161 us -> 162 us (level)
    ppermute x33, waiting for transfers between devices: 69.7 us -> 68.1 us  [swap(): return lax.ppermute(value, ('expert', 'half'), pairs)]
  transfers between devices with their start and end apart: 36 -> 36, of which waited for: 19 -> 19; matrix products, arithmetic and copies ran while one was open for 6% -> 6% of each run, Pallas kernels for 16% -> 17%
where the time goes in v4:
time: 162 us; the launch traced here: 161 us
  waiting for transfers between devices  69.3 us (43%)
  starting transfers between devices  42 us (26%)
  Pallas kernels  30.9 us (19%)
  local copies, waits for them, and re-layouts  9.4 us (6%)
  matrix products  5.21 us (3%)
  other arithmetic  3.47 us (2%)
    ppermute x33, waiting for transfers between devices, swap(): return lax.ppermute(value, ('expert', 'half'), pairs)  68.1 us
    ppermute x33, starting transfers between devices, swap(): return lax.ppermute(value, ('expert', 'half'), pairs)  41.4 us
    pallas_call x2, Pallas kernels, expert_call(): pl.pallas_call(functools.partial(expert_kernel, slots, units), out_shape=...  21.6 us
    unnamed x24, local copies, waits for them, and re-layouts  8.31 us
    pallas_call x2, Pallas kernels, attention_call(): pl.pallas_call(functools.partial(attention_kernel, head_dim, group, len(k...  7.42 us
    dot_general x1, matrix products, body(): queries = jnp.dot(normed, w_query, preferred_element_type=jnp.float32)  4.72 us
  transfers between devices with their start and end apart: 36, of which 19 were waited for; matrix products, arithmetic and copies ran while one was open for 6% of the time, Pallas kernels for 17%

profile of v4, /device:TPU:0, one launch (start us, length us, event | category | flops | bytes accessed | tf_op | source)
XLA Modules:
  0.0 161.3 jit_solution(15626507056733598961)
XLA Ops:
  0.7 6.4 %copy.32 = bf16[2,2048,2,384]{3,1,2,0:T(8,128)(2,1)} copy(bf16[2,2048,2,384]{3,2,1,0:T(2,128)(2,1)} %param.15) | data formatting | bytes 12582912 | tf_op args[4]
  7.0 0.5 collective-permute-start.5
  7.6 1.8 %payload.1 = bf16[64,2176]{1,0:T(8,128)(2,1)} custom-call(s32[1]{0:T(128)} %bitcast.core_ref, bf16[128,2048]{1,0:T(8,128)(2,1)} %hidden_ref.1, s32[8,128]{1,0:T(8,128)} %bitcast.39, f32[8,128]{1,0:T(8,128)} %bitcast.40), custom_call_target="tpu_custom_call" | custom-call | tf_op jit(solution)/shard_map/payload/pallas_call | solution.py:58
  9.4 2.9 %collective-permute-start = (bf16[64,2176]{1,0:T(8,128)(2,1)}, bf16[64,2176]{1,0:T(8,128)(2,1)}, u32[]{:S(2)}, u32[]{:S(2)}) collective-permute-start(bf16[64,2176]{1,0:T(8,128)(2,1)} %payload.1), channel_id=1, source_target_pairs={{0,2},{1,5},{2,0},{3,7},{4,6},{5,1},{6,4},{7,3},{8,10},{9,13},{10,... | collective-permute-start | bytes 835592 | tf_op jit(solution)/shard_map/ppermute | solution.py:27
  12.3 2.6 %collective-permute-start.2 = (bf16[64,2176]{1,0:T(8,128)(2,1)}, bf16[64,2176]{1,0:T(8,128)(2,1)}, u32[]{:S(2)}, u32[]{:S(2)}) collective-permute-start(bf16[64,2176]{1,0:T(8,128)(2,1)} %payload.1), channel_id=1, source_target_pairs={{0,16},{1,17},{2,18},{3,19},{4,20},{5,21},{6,22},{7,23},{8,24},{9,... | collective-permute-start | bytes 835592 | tf_op jit(solution)/shard_map/ppermute | solution.py:27
  14.9 1.6 collective-permute-start.9
  16.6 0.5 collective-permute-done
  17.1 1.1 pad_maximum_fusion.refs_0_
  18.2 2.1 %collective-permute-start.1 = (bf16[128,2176]{1,0:T(8,128)(2,1)S(1)}, bf16[128,2176]{1,0:T(8,128)(2,1)S(1)}, u32[]{:S(2)}, u32[]{:S(2)}) collective-permute-start(bf16[128,2176]{1,0:T(8,128)(2,1)S(1)} %pad_maximum_fusion.refs_0_), channel_id=1, source_target_pairs={{0,4},{1,3},{2,6},{3,1},{4,0},{5,7},{6,2},{7,5},{8,12},{9,11},{10,... | collective-permute-start | bytes 1671176 | tf_op jit(solution)/shard_map/ppermute | solution.py:27
  20.3 7.6 %collective-permute-done.2 = bf16[64,2176]{1,0:T(8,128)(2,1)} collective-permute-done((bf16[64,2176]{1,0:T(8,128)(2,1)}, bf16[64,2176]{1,0:T(8,128)(2,1)}, u32[]{:S(2)}, u32[]{:S(2)}) %collective-permute-start.2) | collective-permute-done | bytes 278560 | tf_op jit(solution)/shard_map/ppermute | solution.py:27
  27.9 1.4 collective-permute-start.3
  29.3 1.0 constant_dynamic-update-slice_fusion.1
  30.3 3.6 %collective-permute-start.12 = (bf16[64,2176]{1,0:T(8,128)(2,1)}, bf16[64,2176]{1,0:T(8,128)(2,1)S(1)}, u32[]{:S(2)}, u32[]{:S(2)}) collective-permute-start(bf16[64,2176]{1,0:T(8,128)(2,1)} %payload.1), channel_id=1, source_target_pairs={{0,24},{1,25},{2,26},{3,27},{4,28},{5,29},{6,30},{7,31},{8,16},{9,... | collective-permute-start | bytes 835592 | tf_op jit(solution)/shard_map/ppermute | solution.py:27
  33.9 0.8 collective-permute-done.3
  34.7 1.4 collective-permute-start.10
  36.1 0.7 collective-permute-start.4
  36.8 2.9 %collective-permute-done.12 = bf16[64,2176]{1,0:T(8,128)(2,1)S(1)} collective-permute-done((bf16[64,2176]{1,0:T(8,128)(2,1)}, bf16[64,2176]{1,0:T(8,128)(2,1)S(1)}, u32[]{:S(2)}, u32[]{:S(2)}) %collective-permute-start.12) | collective-permute-done | bytes 278560 | tf_op jit(solution)/shard_map/ppermute | solution.py:27
  39.8 4.5 %collective-permute-done.10 = bf16[64,2176]{1,0:T(8,128)(2,1)S(1)} collective-permute-done((bf16[64,2176]{1,0:T(8,128)(2,1)S(1)}, bf16[64,2176]{1,0:T(8,128)(2,1)S(1)}, u32[]{:S(2)}, u32[]{:S(2)}) %collective-permute-start.10) | collective-permute-done | bytes 278560 | tf_op jit(solution)/shard_map/ppermute | solution.py:27
  44.3 1.4 collective-permute-start.13
  45.7 3.0 %collective-permute-done.4.refs_3_ = bf16[128,2176]{1,0:T(8,128)(2,1)S(1)} collective-permute-done((bf16[128,2176]{1,0:T(8,128)(2,1)S(1)}, bf16[128,2176]{1,0:T(8,128)(2,1)S(1)}, u32[]{:S(2)}, u32[]{:S(2)}) %collective-permute-start.4) | collective-permute-done | bytes 557088 | tf_op jit(solution)/shard_map/ppermute | solution.py:27
  48.7 0.6 collective-permute-start.11
  49.3 10.7 %experts.2 = (f32[128,2048]{1,0:T(8,128)S(1)}, bf16[128,2048]{1,0:T(8,128)(2,1)S(1)}, f32[128,2048]{1,0:T(8,128)S(1)}, bf16[128,2048]{1,0:T(8,128)(2,1)S(1)}) custom-call(s32[2]{0:T(128)S(1)} %pad_add_fusion.place_ref, s32[16]{0:T(128)S(1)} %slice_reduce_fusion.kind_ref, f32[1,128]{1,0:T(1,128)S(1)} %or_convert_fusion.pick_ref, ...), custom_call_target="tpu_custom_call" | custom-call | tf_op jit(solution)/shard_map/experts/pallas_call | solution.py:188
  60.1 1.4 collective-permute-start.18
  61.6 0.7 collective-permute-start.14
  62.3 1.4 collective-permute-start.7
  63.7 6.2 %collective-permute-done.18 = bf16[128,2048]{1,0:T(8,128)(2,1)S(1)} collective-permute-done((bf16[128,2048]{1,0:T(8,128)(2,1)S(1)}, bf16[128,2048]{1,0:T(8,128)(2,1)S(1)}, u32[]{:S(2)}, u32[]{:S(2)}) %collective-permute-start.18) | collective-permute-done | bytes 524320 | tf_op jit(solution)/shard_map/ppermute | solution.py:27
  70.0 0.4 collective-permute-start.19
  70.3 7.7 %collective-permute-done.14.refs_3_ = bf16[128,2176]{1,0:T(8,128)(2,1)S(1)} collective-permute-done((bf16[128,2176]{1,0:T(8,128)(2,1)S(1)}, bf16[128,2176]{1,0:T(8,128)(2,1)S(1)}, u32[]{:S(2)}, u32[]{:S(2)}) %collective-permute-start.14) | collective-permute-done | bytes 557088 | tf_op jit(solution)/shard_map/ppermute | solution.py:27
  78.1 10.9 %experts.3 = (f32[128,2048]{1,0:T(8,128)S(1)}, bf16[128,2048]{1,0:T(8,128)(2,1)S(1)}, f32[128,2048]{1,0:T(8,128)S(1)}, bf16[128,2048]{1,0:T(8,128)(2,1)S(1)}) custom-call(s32[2]{0:T(128)S(1)} %pad_add_fusion.place_ref, s32[16]{0:T(128)S(1)} %slice_reduce_fusion.kind_ref, f32[1,128]{1,0:T(1,128)S(1)} %or_convert_fusion.pick_ref, ...), custom_call_target="tpu_custom_call" | custom-call | tf_op jit(solution)/shard_map/experts/pallas_call | solution.py:188
  89.0 1.4 collective-permute-start.21
  90.6 1.0 collective-permute-start.8
  91.8 9.2 %collective-permute-done.21 = bf16[128,2048]{1,0:T(8,128)(2,1)S(1)} collective-permute-done((bf16[128,2048]{1,0:T(8,128)(2,1)S(1)}, bf16[128,2048]{1,0:T(8,128)(2,1)S(1)}, u32[]{:S(2)}, u32[]{:S(2)}) %collective-permute-start.21) | collective-permute-done | bytes 524320 | tf_op jit(solution)/shard_map/ppermute | solution.py:27
  101.2 0.4 collective-permute-start.22
  101.6 7.9 %collective-permute-done.15 = bf16[128,2048]{1,0:T(8,128)(2,1)S(1)} collective-permute-done((bf16[128,2048]{1,0:T(8,128)(2,1)S(1)}, bf16[128,2048]{1,0:T(8,128)(2,1)S(1)}, u32[]{:S(2)}, u32[]{:S(2)}) %collective-permute-start.15) | collective-permute-done | bytes 524320 | tf_op jit(solution)/shard_map/ppermute | solution.py:27
  109.6 0.4 collective-permute-start.16
  110.1 3.4 %collective-permute-start.23 = (bf16[64,2048]{1,0:T(8,128)(2,1)S(1)}, bf16[64,2048]{1,0:T(8,128)(2,1)S(1)}, u32[]{:S(2)}, u32[]{:S(2)}) collective-permute-start(bf16[64,2048]{1,0:T(8,128)(2,1)S(1)} %fusion.2), channel_id=1, source_target_pairs={{0,24},{1,25},{2,26},{3,27},{4,28},{5,29},{6,30},{7,31},{8,16},{9,... | collective-permute-start | bytes 786440 | tf_op jit(solution)/shard_map/ppermute | solution.py:27
  113.5 2.5 %collective-permute-done.16 = bf16[64,2048]{1,0:T(8,128)(2,1)S(1)} collective-permute-done((bf16[64,2048]{1,0:T(8,128)(2,1)S(1)}, bf16[64,2048]{1,0:T(8,128)(2,1)S(1)}, u32[]{:S(2)}, u32[]{:S(2)}) %collective-permute-start.16) | collective-permute-done | bytes 262176 | tf_op jit(solution)/shard_map/ppermute | solution.py:27
  116.2 2.1 %collective-permute-done.23 = bf16[64,2048]{1,0:T(8,128)(2,1)S(1)} collective-permute-done((bf16[64,2048]{1,0:T(8,128)(2,1)S(1)}, bf16[64,2048]{1,0:T(8,128)(2,1)S(1)}, u32[]{:S(2)}, u32[]{:S(2)}) %collective-permute-start.23) | collective-permute-done | bytes 262176 | tf_op jit(solution)/shard_map/ppermute | solution.py:27
  118.4 4.2 %collective-permute-done.17 = bf16[64,2048]{1,0:T(8,128)(2,1)S(1)} collective-permute-done((bf16[64,2048]{1,0:T(8,128)(2,1)S(1)}, bf16[64,2048]{1,0:T(8,128)(2,1)S(1)}, u32[]{:S(2)}, u32[]{:S(2)}) %collective-permute-start.17) | collective-permute-done | bytes 262176 | tf_op jit(solution)/shard_map/ppermute | solution.py:27
  122.9 0.5 copy.26
  123.6 1.2 collective-permute-done.24
  124.8 0.2 multiply_reduce_fusion
  125.0 0.5 fusion.11
  125.6 0.2 reduce_sum.29
  126.1 0.2 collective-permute-start.25
  126.3 3.8 %collective-permute-start.28 = (bf16[128,512]{1,0:T(8,128)(2,1)S(1)}, bf16[128,512]{1,0:T(8,128)(2,1)S(1)}, u32[]{:S(2)}, u32[]{:S(2)}) collective-permute-start(bf16[128,512]{1,0:T(8,128)(2,1)S(1)} %pad_maximum_fusion.3), channel_id=1, source_target_pairs={{0,16},{1,17},{2,18},{3,19},{4,20},{5,21},{6,22},{7,23},{8,24},{9,... | collective-permute-start | bytes 393224 | tf_op jit(solution)/shard_map/ppermute | solution.py:27
  130.1 0.3 collective-permute-start.32
  130.4 4.7 %fusion.12 = f32[128,2048]{1,0:T(8,128)S(1)} fusion(bf16[2048,2048]{1,0:T(8,128)(2,1)} %param.18, f32[128,2048]{1,0:T(8,128)S(1)} %get-tuple-element.37, f32[2048]{0:T(1024)S(1)} %copy-done.5, f32[128]{0:T(128)S(1)} %add_rsqrt_fusion.2), kind=kOutput, calls=%fused_computation.55 | convolution fusion | flops 1074528256 | bytes 10494464 | tf_op jit(solution)/shard_map/dot_general | solution.py:387
  135.4 0.3 reduce_sum.28
  136.0 2.1 %collective-permute-start.33 = (bf16[256,512]{1,0:T(8,128)(2,1)S(1)}, bf16[256,512]{1,0:T(8,128)(2,1)S(1)}, u32[]{:S(2)}, u32[]{:S(2)}) collective-permute-start(bf16[256,512]{1,0:T(8,128)(2,1)S(1)} %pad_maximum_fusion.2.refs_0_), channel_id=1, source_target_pairs={{0,4},{1,3},{2,6},{3,1},{4,0},{5,7},{6,2},{7,5},{8,12},{9,11},{10,... | collective-permute-start | bytes 786440 | tf_op jit(solution)/shard_map/ppermute | solution.py:27
  138.1 1.2 collective-permute-start.26
  139.5 0.8 collective-permute-start.34
  140.3 3.1 %collective-permute-done.26 = bf16[128,512]{1,0:T(8,128)(2,1)S(1)} collective-permute-done((bf16[128,512]{1,0:T(8,128)(2,1)S(1)}, bf16[128,512]{1,0:T(8,128)(2,1)S(1)}, u32[]{:S(2)}, u32[]{:S(2)}) %collective-permute-start.26) | collective-permute-done | bytes 131104 | tf_op jit(solution)/shard_map/ppermute | solution.py:27
  143.4 0.6 collective-permute-start.27
  144.0 0.4 collective-permute-done.29
  144.4 0.8 collective-permute-start.30
  145.2 1.3 collective-permute-start.35
  146.5 4.3 %collective-permute-done.30 = bf16[128,512]{1,0:T(8,128)(2,1)S(1)} collective-permute-done((bf16[128,512]{1,0:T(8,128)(2,1)S(1)}, bf16[128,512]{1,0:T(8,128)(2,1)S(1)}, u32[]{:S(2)}, u32[]{:S(2)}) %collective-permute-start.30) | collective-permute-done | bytes 131104 | tf_op jit(solution)/shard_map/ppermute | solution.py:27
  150.8 1.2 collective-permute-start.31
  152.0 0.3 mul.86
  152.3 0.5 fusion.1.q_ref
  152.9 3.4 %attention.2 = (f32[2,8,1024]{2,1,0:T(8,128)S(1)}, f32[2,128,1024]{2,1,0:T(8,128)S(1)}) custom-call(bf16[128,2048]{1,0:T(8,128)(2,1)S(1)} %fusion.1.q_ref, bf16[256,512]{1,0:T(8,128)(2,1)S(1)} %pad_maximum_fusion.2.refs_0_, bf16[256,512]{1,0:T(8,128)(2,1)S(1)} %collective-permute-done.33.refs_1_, ...), custom_call_target="tpu_custom_call" | custom-call | flops 1073741824 | bytes 1048576 | tf_op jit(solution)/shard_map/attention/pallas_call | solution.py:277
  156.3 0.9 collective-permute-done.31.refs_3_
  157.2 4.0 %attention.3 = bf16[128,2048]{1,0:T(8,128)(2,1)} custom-call(bf16[128,2048]{1,0:T(8,128)(2,1)S(1)} %fusion.1.q_ref, bf16[256,512]{1,0:T(8,128)(2,1)S(1)} %constant_dynamic-update-slice_fusion.4.refs_0_, bf16[256,512]{1,0:T(8,128)(2,1)S(1)} %collective-permute-done.27.refs_1_, bf16[256,512]{1,0:T(8,128)(2,1)S(1)} %constant_dynamic-update-slice_fusion.6.refs_2_, ...), custom_call_target="tpu_custom_call" | custom-call | flops 1073741824 | bytes 1048576 | tf_op jit(solution)/shard_map/attention/pallas_call | solution.py:277
  (81 shorter events, 2.9 us)
Async XLA Ops:
  0.6 122.9 %copy-start = (f32[128]{0:T(128)S(1)}, f32[128]{0:T(128)}, u32[]{:S(2)}) copy-start(f32[128]{0:T(128)} %param.20) | copy-start | bytes 1540
  0.6 6.9 %copy-start.1 = (bf16[2,384,2048]{2,1,0:T(8,128)(2,1)S(1)}, bf16[2,384,2048]{2,1,0:T(8,128)(2,1)}, u32[]{:S(2)}) copy-start(bf16[2,384,2048]{2,1,0:T(8,128)(2,1)} %refs_6_.3) | copy-start | bytes 9437188
  0.7 15.9 %copy-start.6 = (s32[2048]{0:T(1024)S(1)}, s32[2048]{0:T(1024)}, u32[]{:S(2)}) copy-start(s32[2048]{0:T(1024)} %param.12) | copy-start | bytes 24580
  7.0 42.3 %collective-permute-start.5 = (bf16[2,2,2048,384]{3,2,1,0:T(8,128)(2,1)}, bf16[2,2,2048,384]{3,2,1,0:T(8,128)(2,1)}, u32[]{:S(2)}, u32[]{:S(2)}) collective-permute-start(bf16[2,2,2048,384]{3,2,1,0:T(8,128)(2,1)} %bitcast.32.refs_4_), channel_id=1, source_target_pairs={{0,1},{1,0},{2,3},{3,2},{4,5},{5,4},{6,7},{7,6},{8,9},{9,8},{10,11... | collective-permute-start | bytes 18874376 | tf_op jit(solution)/shard_map/ppermute | solution.py:35
  7.5 41.8 %collective-permute-start.6 = (bf16[2,384,2048]{2,1,0:T(8,128)(2,1)S(1)}, bf16[2,384,2048]{2,1,0:T(8,128)(2,1)}, u32[]{:S(2)}, u32[]{:S(2)}) collective-permute-start(bf16[2,384,2048]{2,1,0:T(8,128)(2,1)S(1)} %copy-done.1), channel_id=1, source_target_pairs={{0,1},{1,0},{2,3},{3,2},{4,5},{5,4},{6,7},{7,6},{8,9},{9,8},{10,11... | collective-permute-start | bytes 9437192 | tf_op jit(solution)/shard_map/ppermute | solution.py:35
  9.4 7.8 %collective-permute-start = (bf16[64,2176]{1,0:T(8,128)(2,1)}, bf16[64,2176]{1,0:T(8,128)(2,1)}, u32[]{:S(2)}, u32[]{:S(2)}) collective-permute-start(bf16[64,2176]{1,0:T(8,128)(2,1)} %payload.1), channel_id=1, source_target_pairs={{0,2},{1,5},{2,0},{3,7},{4,6},{5,1},{6,4},{7,3},{8,10},{9,13},{10,... | collective-permute-start | bytes 835592 | tf_op jit(solution)/shard_map/ppermute | solution.py:27
  12.3 15.6 %collective-permute-start.2 = (bf16[64,2176]{1,0:T(8,128)(2,1)}, bf16[64,2176]{1,0:T(8,128)(2,1)}, u32[]{:S(2)}, u32[]{:S(2)}) collective-permute-start(bf16[64,2176]{1,0:T(8,128)(2,1)} %payload.1), channel_id=1, source_target_pairs={{0,16},{1,17},{2,18},{3,19},{4,20},{5,21},{6,22},{7,23},{8,24},{9,... | collective-permute-start | bytes 835592 | tf_op jit(solution)/shard_map/ppermute | solution.py:27
  14.9 15.4 %collective-permute-start.9 = (bf16[64,2176]{1,0:T(8,128)(2,1)}, bf16[64,2176]{1,0:T(8,128)(2,1)S(1)}, u32[]{:S(2)}, u32[]{:S(2)}) collective-permute-start(bf16[64,2176]{1,0:T(8,128)(2,1)} %payload.1), channel_id=1, source_target_pairs={{0,8},{1,9},{2,10},{3,11},{4,12},{5,13},{6,14},{7,15},{8,0},{9,1},... | collective-permute-start | bytes 835592 | tf_op jit(solution)/shard_map/ppermute | solution.py:27
  18.2 17.9 %collective-permute-start.1 = (bf16[128,2176]{1,0:T(8,128)(2,1)S(1)}, bf16[128,2176]{1,0:T(8,128)(2,1)S(1)}, u32[]{:S(2)}, u32[]{:S(2)}) collective-permute-start(bf16[128,2176]{1,0:T(8,128)(2,1)S(1)} %pad_maximum_fusion.refs_0_), channel_id=1, source_target_pairs={{0,4},{1,3},{2,6},{3,1},{4,0},{5,7},{6,2},{7,5},{8,12},{9,11},{10,... | collective-permute-start | bytes 1671176 | tf_op jit(solution)/shard_map/ppermute | solution.py:27
  27.9 6.8 %collective-permute-start.3 = (bf16[64,2176]{1,0:T(8,128)(2,1)}, bf16[64,2176]{1,0:T(8,128)(2,1)S(1)}, u32[]{:S(2)}, u32[]{:S(2)}) collective-permute-start(bf16[64,2176]{1,0:T(8,128)(2,1)} %collective-permute-done.2), channel_id=1, source_target_pairs={{0,2},{1,5},{2,0},{3,7},{4,6},{5,1},{6,4},{7,3},{8,10},{9,13},{10,... | collective-permute-start | bytes 835592 | tf_op jit(solution)/shard_map/ppermute | solution.py:27
  30.3 9.5 %collective-permute-start.12 = (bf16[64,2176]{1,0:T(8,128)(2,1)}, bf16[64,2176]{1,0:T(8,128)(2,1)S(1)}, u32[]{:S(2)}, u32[]{:S(2)}) collective-permute-start(bf16[64,2176]{1,0:T(8,128)(2,1)} %payload.1), channel_id=1, source_target_pairs={{0,24},{1,25},{2,26},{3,27},{4,28},{5,29},{6,30},{7,31},{8,16},{9,... | collective-permute-start | bytes 835592 | tf_op jit(solution)/shard_map/ppermute | solution.py:27
  34.7 9.6 %collective-permute-start.10 = (bf16[64,2176]{1,0:T(8,128)(2,1)S(1)}, bf16[64,2176]{1,0:T(8,128)(2,1)S(1)}, u32[]{:S(2)}, u32[]{:S(2)}) collective-permute-start(bf16[64,2176]{1,0:T(8,128)(2,1)S(1)} %collective-permute-done.9), channel_id=1, source_target_pairs={{0,2},{1,5},{2,0},{3,7},{4,6},{5,1},{6,4},{7,3},{8,10},{9,13},{10,... | collective-permute-start | bytes 835592 | tf_op jit(solution)/shard_map/ppermute | solution.py:27
  36.1 12.6 %collective-permute-start.4 = (bf16[128,2176]{1,0:T(8,128)(2,1)S(1)}, bf16[128,2176]{1,0:T(8,128)(2,1)S(1)}, u32[]{:S(2)}, u32[]{:S(2)}) collective-permute-start(bf16[128,2176]{1,0:T(8,128)(2,1)S(1)} %constant_dynamic-update-slice_fusion.refs_2_), channel_id=1, source_target_pairs={{0,4},{1,3},{2,6},{3,1},{4,0},{5,7},{6,2},{7,5},{8,12},{9,11},{10,... | collective-permute-start | bytes 1671176 | tf_op jit(solution)/shard_map/ppermute | solution.py:27
  44.3 17.2 %collective-permute-start.13 = (bf16[64,2176]{1,0:T(8,128)(2,1)S(1)}, bf16[64,2176]{1,0:T(8,128)(2,1)S(1)}, u32[]{:S(2)}, u32[]{:S(2)}) collective-permute-start(bf16[64,2176]{1,0:T(8,128)(2,1)S(1)} %collective-permute-done.12), channel_id=1, source_target_pairs={{0,2},{1,5},{2,0},{3,7},{4,6},{5,1},{6,4},{7,3},{8,10},{9,13},{10,... | collective-permute-start | bytes 835592 | tf_op jit(solution)/shard_map/ppermute | solution.py:27
  48.7 12.9 %collective-permute-start.11 = (bf16[128,2176]{1,0:T(8,128)(2,1)S(1)}, bf16[128,2176]{1,0:T(8,128)(2,1)S(1)}, u32[]{:S(2)}, u32[]{:S(2)}) collective-permute-start(bf16[128,2176]{1,0:T(8,128)(2,1)S(1)} %constant_dynamic-update-slice_fusion.2.refs_0_), channel_id=1, source_target_pairs={{0,4},{1,3},{2,6},{3,1},{4,0},{5,7},{6,2},{7,5},{8,12},{9,11},{10,... | collective-permute-start | bytes 1671176 | tf_op jit(solution)/shard_map/ppermute | solution.py:27
  60.1 9.8 %collective-permute-start.18 = (bf16[128,2048]{1,0:T(8,128)(2,1)S(1)}, bf16[128,2048]{1,0:T(8,128)(2,1)S(1)}, u32[]{:S(2)}, u32[]{:S(2)}) collective-permute-start(bf16[128,2048]{1,0:T(8,128)(2,1)S(1)} %get-tuple-element.31), channel_id=1, source_target_pairs={{0,4},{1,3},{2,6},{3,1},{4,0},{5,7},{6,2},{7,5},{8,12},{9,11},{10,... | collective-permute-start | bytes 1572872 | tf_op jit(solution)/shard_map/ppermute | solution.py:27
  61.6 16.5 %collective-permute-start.14 = (bf16[128,2176]{1,0:T(8,128)(2,1)S(1)}, bf16[128,2176]{1,0:T(8,128)(2,1)S(1)}, u32[]{:S(2)}, u32[]{:S(2)}) collective-permute-start(bf16[128,2176]{1,0:T(8,128)(2,1)S(1)} %pad_maximum_fusion.1.refs_2_), channel_id=1, source_target_pairs={{0,4},{1,3},{2,6},{3,1},{4,0},{5,7},{6,2},{7,5},{8,12},{9,11},{10,... | collective-permute-start | bytes 1671176 | tf_op jit(solution)/shard_map/ppermute | solution.py:27
  62.3 28.2 %collective-permute-start.7 = (bf16[128,2048]{1,0:T(8,128)(2,1)S(1)}, bf16[128,2048]{1,0:T(8,128)(2,1)S(1)}, u32[]{:S(2)}, u32[]{:S(2)}) collective-permute-start(bf16[128,2048]{1,0:T(8,128)(2,1)S(1)} %get-tuple-element.22), channel_id=1, source_target_pairs={{0,4},{1,3},{2,6},{3,1},{4,0},{5,7},{6,2},{7,5},{8,12},{9,11},{10,... | collective-permute-start | bytes 1572872 | tf_op jit(solution)/shard_map/ppermute | solution.py:27
  70.0 21.7 %collective-permute-start.19 = (bf16[64,2048]{1,0:T(8,128)(2,1)S(1)}, bf16[64,2048]{1,0:T(8,128)(2,1)S(1)}, u32[]{:S(2)}, u32[]{:S(2)}) collective-permute-start(bf16[64,2048]{1,0:T(8,128)(2,1)S(1)} %slice.93), channel_id=1, source_target_pairs={{0,2},{1,5},{2,0},{3,7},{4,6},{5,1},{6,4},{7,3},{8,10},{9,13},{10,... | collective-permute-start | bytes 786440 | tf_op jit(solution)/shard_map/ppermute | solution.py:27
  89.0 12.1 %collective-permute-start.21 = (bf16[128,2048]{1,0:T(8,128)(2,1)S(1)}, bf16[128,2048]{1,0:T(8,128)(2,1)S(1)}, u32[]{:S(2)}, u32[]{:S(2)}) collective-permute-start(bf16[128,2048]{1,0:T(8,128)(2,1)S(1)} %get-tuple-element.33), channel_id=1, source_target_pairs={{0,4},{1,3},{2,6},{3,1},{4,0},{5,7},{6,2},{7,5},{8,12},{9,11},{10,... | collective-permute-start | bytes 1572872 | tf_op jit(solution)/shard_map/ppermute | solution.py:27
  90.6 25.6 %collective-permute-start.8 = (bf16[64,2048]{1,0:T(8,128)(2,1)S(1)}, bf16[64,2048]{1,0:T(8,128)(2,1)S(1)}, u32[]{:S(2)}, u32[]{:S(2)}) collective-permute-start(bf16[64,2048]{1,0:T(8,128)(2,1)S(1)} %slice.95), channel_id=1, source_target_pairs={{0,2},{1,5},{2,0},{3,7},{4,6},{5,1},{6,4},{7,3},{8,10},{9,13},{10,... | collective-permute-start | bytes 786440 | tf_op jit(solution)/shard_map/ppermute | solution.py:27
  91.7 17.8 %collective-permute-start.15 = (bf16[128,2048]{1,0:T(8,128)(2,1)S(1)}, bf16[128,2048]{1,0:T(8,128)(2,1)S(1)}, u32[]{:S(2)}, u32[]{:S(2)}) collective-permute-start(bf16[128,2048]{1,0:T(8,128)(2,1)S(1)} %get-tuple-element.30), channel_id=1, source_target_pairs={{0,4},{1,3},{2,6},{3,1},{4,0},{5,7},{6,2},{7,5},{8,12},{9,11},{10,... | collective-permute-start | bytes 1572872 | tf_op jit(solution)/shard_map/ppermute | solution.py:27
  91.7 24.5 %collective-permute-start.20 = (bf16[64,2048]{1,0:T(8,128)(2,1)S(1)}, bf16[64,2048]{1,0:T(8,128)(2,1)S(1)}, u32[]{:S(2)}, u32[]{:S(2)}) collective-permute-start(bf16[64,2048]{1,0:T(8,128)(2,1)S(1)} %fusion.3), channel_id=1, source_target_pairs={{0,16},{1,17},{2,18},{3,19},{4,20},{5,21},{6,22},{7,23},{8,24},{9,... | collective-permute-start | bytes 786440 | tf_op jit(solution)/shard_map/ppermute | solution.py:27
  101.2 8.8 %collective-permute-start.22 = (bf16[64,2048]{1,0:T(8,128)(2,1)S(1)}, bf16[64,2048]{1,0:T(8,128)(2,1)S(1)}, u32[]{:S(2)}, u32[]{:S(2)}) collective-permute-start(bf16[64,2048]{1,0:T(8,128)(2,1)S(1)} %slice.92), channel_id=1, source_target_pairs={{0,2},{1,5},{2,0},{3,7},{4,6},{5,1},{6,4},{7,3},{8,10},{9,13},{10,... | collective-permute-start | bytes 786440 | tf_op jit(solution)/shard_map/ppermute | solution.py:27
  109.5 13.1 %copy-start.3 = (bf16[64,2176]{1,0:T(8,128)(2,1)S(1)}, bf16[64,2176]{1,0:T(8,128)(2,1)}, u32[]{:S(2)}) copy-start(bf16[64,2176]{1,0:T(8,128)(2,1)} %payload.1) | copy-start | bytes 835588
  109.6 13.2 %copy-start.4 = (bf16[2048,2,256]{2,1,0:T(2,128)(2,1)S(1)}, bf16[2048,2,256]{2,1,0:T(2,128)(2,1)}, u32[]{:S(2)}) copy-start(bf16[2048,2,256]{2,1,0:T(2,128)(2,1)} %param.19) | copy-start | bytes 6291460
  109.6 6.4 %collective-permute-start.16 = (bf16[64,2048]{1,0:T(8,128)(2,1)S(1)}, bf16[64,2048]{1,0:T(8,128)(2,1)S(1)}, u32[]{:S(2)}, u32[]{:S(2)}) collective-permute-start(bf16[64,2048]{1,0:T(8,128)(2,1)S(1)} %slice.94), channel_id=1, source_target_pairs={{0,2},{1,5},{2,0},{3,7},{4,6},{5,1},{6,4},{7,3},{8,10},{9,13},{10,... | collective-permute-start | bytes 786440 | tf_op jit(solution)/shard_map/ppermute | solution.py:27
  110.1 8.2 %collective-permute-start.23 = (bf16[64,2048]{1,0:T(8,128)(2,1)S(1)}, bf16[64,2048]{1,0:T(8,128)(2,1)S(1)}, u32[]{:S(2)}, u32[]{:S(2)}) collective-permute-start(bf16[64,2048]{1,0:T(8,128)(2,1)S(1)} %fusion.2), channel_id=1, source_target_pairs={{0,24},{1,25},{2,26},{3,27},{4,28},{5,29},{6,30},{7,31},{8,16},{9,... | collective-permute-start | bytes 786440 | tf_op jit(solution)/shard_map/ppermute | solution.py:27
  116.1 6.4 %collective-permute-start.17 = (bf16[64,2048]{1,0:T(8,128)(2,1)S(1)}, bf16[64,2048]{1,0:T(8,128)(2,1)S(1)}, u32[]{:S(2)}, u32[]{:S(2)}) collective-permute-start(bf16[64,2048]{1,0:T(8,128)(2,1)S(1)} %fusion.4), channel_id=1, source_target_pairs={{0,8},{1,9},{2,10},{3,11},{4,12},{5,13},{6,14},{7,15},{8,0},{9,1},... | collective-permute-start | bytes 786440 | tf_op jit(solution)/shard_map/ppermute | solution.py:27
  122.8 2.0 %collective-permute-start.24 = (f32[64,2048]{1,0:T(8,128)S(1)}, f32[64,2048]{1,0:T(8,128)S(1)}, u32[]{:S(2)}, u32[]{:S(2)}) collective-permute-start(f32[64,2048]{1,0:T(8,128)S(1)} %fusion.8), channel_id=1, source_target_pairs={{0,1},{1,0},{2,3},{3,2},{4,5},{5,4},{6,7},{7,6},{8,9},{9,8},{10,11... | collective-permute-start | bytes 1572872 | tf_op jit(solution)/shard_map/ppermute | solution.py:35
  122.9 0.7 copy-start.7
  123.5 1.4 copy-start.5
  125.0 5.5 %copy-start.2 = (f32[128,2048]{1,0:T(8,128)}, f32[128,2048]{1,0:T(8,128)S(1)}, u32[]{:S(2)}) copy-start(f32[128,2048]{1,0:T(8,128)S(1)} %get-tuple-element.37) | copy-start | bytes 3145732
  126.1 12.0 %collective-permute-start.25 = (bf16[128,512]{1,0:T(8,128)(2,1)S(1)}, bf16[128,512]{1,0:T(8,128)(2,1)S(1)}, u32[]{:S(2)}, u32[]{:S(2)}) collective-permute-start(bf16[128,512]{1,0:T(8,128)(2,1)S(1)} %pad_maximum_fusion.3), channel_id=1, source_target_pairs={{0,8},{1,9},{2,10},{3,11},{4,12},{5,13},{6,14},{7,15},{8,0},{9,1},... | collective-permute-start | bytes 393224 | tf_op jit(solution)/shard_map/ppermute | solution.py:27
  126.3 13.0 %collective-permute-start.28 = (bf16[128,512]{1,0:T(8,128)(2,1)S(1)}, bf16[128,512]{1,0:T(8,128)(2,1)S(1)}, u32[]{:S(2)}, u32[]{:S(2)}) collective-permute-start(bf16[128,512]{1,0:T(8,128)(2,1)S(1)} %pad_maximum_fusion.3), channel_id=1, source_target_pairs={{0,16},{1,17},{2,18},{3,19},{4,20},{5,21},{6,22},{7,23},{8,24},{9,... | collective-permute-start | bytes 393224 | tf_op jit(solution)/shard_map/ppermute | solution.py:27
  130.1 5.9 %collective-permute-start.32 = (bf16[128,512]{1,0:T(8,128)(2,1)S(1)}, bf16[128,512]{1,0:T(8,128)(2,1)S(1)}, u32[]{:S(2)}, u32[]{:S(2)}) collective-permute-start(bf16[128,512]{1,0:T(8,128)(2,1)S(1)} %pad_maximum_fusion.3), channel_id=1, source_target_pairs={{0,2},{1,5},{2,0},{3,7},{4,6},{5,1},{6,4},{7,3},{8,10},{9,13},{10,... | collective-permute-start | bytes 393224 | tf_op jit(solution)/shard_map/ppermute | solution.py:27
  136.0 16.8 %collective-permute-start.33 = (bf16[256,512]{1,0:T(8,128)(2,1)S(1)}, bf16[256,512]{1,0:T(8,128)(2,1)S(1)}, u32[]{:S(2)}, u32[]{:S(2)}) collective-permute-start(bf16[256,512]{1,0:T(8,128)(2,1)S(1)} %pad_maximum_fusion.2.refs_0_), channel_id=1, source_target_pairs={{0,4},{1,3},{2,6},{3,1},{4,0},{5,7},{6,2},{7,5},{8,12},{9,11},{10,... | collective-permute-start | bytes 786440 | tf_op jit(solution)/shard_map/ppermute | solution.py:27
  138.1 5.3 %collective-permute-start.26 = (bf16[128,512]{1,0:T(8,128)(2,1)S(1)}, bf16[128,512]{1,0:T(8,128)(2,1)S(1)}, u32[]{:S(2)}, u32[]{:S(2)}) collective-permute-start(bf16[128,512]{1,0:T(8,128)(2,1)S(1)} %collective-permute-done.25), channel_id=1, source_target_pairs={{0,2},{1,5},{2,0},{3,7},{4,6},{5,1},{6,4},{7,3},{8,10},{9,13},{10,... | collective-permute-start | bytes 393224 | tf_op jit(solution)/shard_map/ppermute | solution.py:27
  139.3 5.0 %collective-permute-start.29 = (bf16[128,512]{1,0:T(8,128)(2,1)S(1)}, bf16[128,512]{1,0:T(8,128)(2,1)S(1)}, u32[]{:S(2)}, u32[]{:S(2)}) collective-permute-start(bf16[128,512]{1,0:T(8,128)(2,1)S(1)} %collective-permute-done.28), channel_id=1, source_target_pairs={{0,8},{1,9},{2,10},{3,11},{4,12},{5,13},{6,14},{7,15},{8,0},{9,1},... | collective-permute-start | bytes 393224 | tf_op jit(solution)/shard_map/ppermute | solution.py:27
  139.5 5.7 %collective-permute-start.34 = (bf16[128,512]{1,0:T(8,128)(2,1)S(1)}, bf16[128,512]{1,0:T(8,128)(2,1)S(1)}, u32[]{:S(2)}, u32[]{:S(2)}) collective-permute-start(bf16[128,512]{1,0:T(8,128)(2,1)S(1)} %collective-permute-done.28), channel_id=1, source_target_pairs={{0,2},{1,5},{2,0},{3,7},{4,6},{5,1},{6,4},{7,3},{8,10},{9,13},{10,... | collective-permute-start | bytes 393224 | tf_op jit(solution)/shard_map/ppermute | solution.py:27
  143.4 12.9 %collective-permute-start.27 = (bf16[256,512]{1,0:T(8,128)(2,1)S(1)}, bf16[256,512]{1,0:T(8,128)(2,1)S(1)}, u32[]{:S(2)}, u32[]{:S(2)}) collective-permute-start(bf16[256,512]{1,0:T(8,128)(2,1)S(1)} %constant_dynamic-update-slice_fusion.4.refs_0_), channel_id=1, source_target_pairs={{0,4},{1,3},{2,6},{3,1},{4,0},{5,7},{6,2},{7,5},{8,12},{9,11},{10,... | collective-permute-start | bytes 786440 | tf_op jit(solution)/shard_map/ppermute | solution.py:27
  144.4 6.4 %collective-permute-start.30 = (bf16[128,512]{1,0:T(8,128)(2,1)S(1)}, bf16[128,512]{1,0:T(8,128)(2,1)S(1)}, u32[]{:S(2)}, u32[]{:S(2)}) collective-permute-start(bf16[128,512]{1,0:T(8,128)(2,1)S(1)} %collective-permute-done.29), channel_id=1, source_target_pairs={{0,2},{1,5},{2,0},{3,7},{4,6},{5,1},{6,4},{7,3},{8,10},{9,13},{10,... | collective-permute-start | bytes 393224 | tf_op jit(solution)/shard_map/ppermute | solution.py:27
  145.2 7.7 %collective-permute-start.35 = (bf16[256,512]{1,0:T(8,128)(2,1)S(1)}, bf16[256,512]{1,0:T(8,128)(2,1)S(1)}, u32[]{:S(2)}, u32[]{:S(2)}) collective-permute-start(bf16[256,512]{1,0:T(8,128)(2,1)S(1)} %constant_dynamic-update-slice_fusion.8.refs_2_), channel_id=1, source_target_pairs={{0,4},{1,3},{2,6},{3,1},{4,0},{5,7},{6,2},{7,5},{8,12},{9,11},{10,... | collective-permute-start | bytes 786440 | tf_op jit(solution)/shard_map/ppermute | solution.py:27
  150.8 6.4 %collective-permute-start.31 = (bf16[256,512]{1,0:T(8,128)(2,1)S(1)}, bf16[256,512]{1,0:T(8,128)(2,1)S(1)}, u32[]{:S(2)}, u32[]{:S(2)}) collective-permute-start(bf16[256,512]{1,0:T(8,128)(2,1)S(1)} %constant_dynamic-update-slice_fusion.6.refs_2_), channel_id=1, source_target_pairs={{0,4},{1,3},{2,6},{3,1},{4,0},{5,7},{6,2},{7,5},{8,12},{9,11},{10,... | collective-permute-start | bytes 786440 | tf_op jit(solution)/shard_map/ppermute | solution.py:27
